TPU v7x, 32 devices: a whole 2x2x4 slice. The times are simulated.
32 devices in a mesh: leaf: 16 (over z, y, x), grp: 2 (over core).
Axes of the slice: x: 2, y: 2, z: 4, core: 2. Of those that a mesh axis runs over, the one named last changes fastest.
Arguments:
- points: bfloat16 [256, 32768], P(None, ('leaf', 'grp')), may hold values from -6 to 6
- charges: bfloat16 [64, 32768], P(None, ('leaf', 'grp')), may hold values from -6 to 6
- order: int32 [32768], P(('leaf', 'grp')), may hold values from 0 to 1023, as said below
- near_mask: int32 [32, 5], P(('leaf', 'grp')), may hold values from 0 to 1, as said below
- skeletons: int32 [32, 5, 128], P(('leaf', 'grp')), may hold values from 0 to 1023, as said below
- leaf_interp: bfloat16 [128, 32768], P(None, ('leaf', 'grp')), may hold values from -0.5 to 0.5
- transfer: bfloat16 [32, 4, 128, 128], P(('leaf', 'grp')), as said below
Outputs:
- potentials: float32 [64, 32768], P(None, ('leaf', 'grp'))
Inputs may be any that keep to these rules, and one draw needn't show every extreme that they name: `order`: within each block of 1024 consecutive entries, a permutation of 0 to 1023. `near_mask`: entry 2 of every row is 1; an entry is 0 where it points outside the leaf coordinates; the pattern is symmetric: block b marks the block k leaf coordinates away exactly when that block marks b. Level 0 holds 128 different rows of the block; level j >= 1 holds 128 different positions of 0 to 255 in the two children's skeletons; the set of a node is the same on every block of that node. `transfer`: the matrix of a node is the same on every block of that node.
All inputs are finite; a program needn't handle non-finite values.
Results may differ from a plain program's by a relative error of at most 0.0019.
Values may be sent and summed in bfloat16 or wider, within the bound.
No kernel may reach another device: no remote copies, remote signals or barrier semaphores. Data moves between devices by JAX's collectives and lax.ppermute only.
A program may use at most 64 MiB of HBM per device.

v0:
```python
import functools

import jax
import jax.numpy as jnp
from jax import lax
from jax.experimental import pallas as pl
from jax.experimental.pallas import tpu as pltpu
from jax.sharding import PartitionSpec as P

REACH = 2
BF16 = jnp.bfloat16
F32 = jnp.float32
LOG2E = 1.4426950408889634
HIGHEST = lax.Precision.HIGHEST
PAD = 16
JOIN_FLOPS = 500
VMEM_LIMIT = 40 * 1024 * 1024
START_VMEM = 56 * 1024 * 1024

NN = ((1,), (0,))
NT = ((1,), (1,))
TN = ((0,), (0,))


def dot(left, right, contract=NN, precision=None):
    return lax.dot_general(
        left, right, (contract, ((), ())), preferred_element_type=F32, precision=precision
    )


def halves(value):
    high = value.astype(BF16)
    return high, (value - high.astype(F32)).astype(BF16)


def dot_split(left, right, contract=NN):
    rows = left.shape[0]
    both = dot(jnp.concatenate(halves(left), axis=0), right, contract)
    return both[:rows] + both[rows:]


def row_norms(points):
    wide = points.astype(F32)
    return jnp.sum(wide * wide, axis=0, keepdims=True)


def column_norms(points):
    wide = points.astype(F32)
    high, low = halves(wide * wide)
    ones = jnp.ones((points.shape[0], 128), BF16)
    return dot(high, ones, TN) + dot(low, ones, TN)


def one_hot(index, rows, first):
    place = lax.broadcasted_iota(jnp.int32, (rows, index.shape[1]), 0) + first
    return jnp.where(place == index, 1.0, 0.0).astype(BF16)


def small_kernel(source, target):
    scale = 2.0 * LOG2E / source.shape[0]
    inner = dot(source, target, TN)
    squares = column_norms(source)[:, : target.shape[1]] + row_norms(target)
    return jnp.exp2(scale * (2.0 * inner - squares))


def pick(first, second, index, bit):
    count = first.shape[1]
    table = jnp.concatenate(
        [one_hot(index, count, count * bit), one_hot(index, count, count * (1 - bit))], axis=0
    )
    return dot(jnp.concatenate([first, second], axis=1), table).astype(BF16)


def write_message(weights, coords, matrix, message_ref, passed_ref):
    dimension, sides = coords.shape[0], weights.shape[0]
    passed = dot_split(weights, matrix, NT)
    message_ref[:dimension] = coords
    message_ref[dimension : dimension + sides] = weights.astype(BF16)
    message_ref[dimension + sides : dimension + 2 * sides] = passed.astype(BF16)
    passed_ref[...] = passed


def start_kernel(*refs):
    inputs, outs, held = refs[:7], refs[7:12], refs[12:19]
    made, sems, out_sems = refs[19:24], refs[24], refs[25]
    copies = [
        pltpu.make_async_copy(source, target, sems.at[number])
        for number, (source, target) in enumerate(zip(inputs, held))
    ]
    for copy in copies:
        copy.start()
    stores = [
        pltpu.make_async_copy(source, target, out_sems.at[number])
        for number, (source, target) in enumerate(zip(made, outs))
    ]
    order, skeletons, mask, charges, points, interp, transfer = held
    ordered_ref, coords_ref, marks_ref, message_ref, passed_ref = made
    dimension, rows = points.shape
    sides, count = passed_ref.shape
    for copy in copies[:4]:
        copy.wait()
    width = rows // 4
    for column in range(0, rows, width):
        table = one_hot(order[:, column : column + width], rows, 0)
        ordered_ref[:, column : column + width] = dot(charges[...], table).astype(BF16)
    stores[0].start()
    copies[4].wait()
    coords = dot(points[...], one_hot(skeletons[0], rows, 0)).astype(BF16)
    coords_ref[...] = coords
    stores[1].start()
    lane = lax.broadcasted_iota(jnp.int32, (1, count), 1)
    pattern = jnp.zeros((1, count), jnp.int32)
    for offset in range(mask.shape[1]):
        pattern = jnp.where(lane == offset, mask[:, offset : offset + 1], pattern)
    marks = jnp.broadcast_to(pattern.astype(F32), (PAD, count)).astype(BF16)
    marks_ref[...] = marks
    message_ref[dimension + 2 * sides :] = marks
    stores[2].start()
    copies[5].wait()
    weights = dot(ordered_ref[...], interp[...], NT)
    copies[6].wait()
    write_message(weights, coords, transfer[0], message_ref, passed_ref)
    stores[3].start()
    stores[4].start()
    for store in stores:
        store.wait()


def marked(marks, offset):
    rows = marks.astype(F32)
    lane = lax.broadcasted_iota(jnp.int32, rows.shape, 1)
    return jnp.max(jnp.where(lane == REACH + offset, rows, 0.0)) > 0.5


def round_kernel(level, last, skeletons, transfer, coords, passed, message, *outs):
    dimension = coords.shape[0]
    sides = passed.shape[0]
    bit = (lax.axis_index("leaf") >> level) & 1
    joined = pick(coords[...], message[:dimension], skeletons[level + 1], bit)
    span = slice(dimension + sides, dimension + 2 * sides)
    weights = passed[...] + message[span].astype(F32)
    if last:
        outs[0][:dimension] = joined
        outs[0][dimension:] = weights.astype(BF16)
        return
    outs[0][...] = joined
    write_message(weights, joined, transfer[level + 1], outs[1], outs[2])


def sibling_term(coords, message, sides):
    dimension = coords.shape[0]
    weights = message[dimension : dimension + sides].astype(F32)
    return dot(weights, small_kernel(message[:dimension], coords[...]), NN, HIGHEST)


def term_kernel(sides, levels, transfer, coords, message, term_ref, *product_ref):
    term_ref[...] = sibling_term(coords, message, sides)
    if product_ref:
        product = transfer[levels - 1].astype(F32)
        for level in range(levels - 2, -1, -1):
            product = dot(product, transfer[level].astype(F32), NN, HIGHEST)
        product_ref[0][...] = product


def last_terms_kernel(sides, levels, transfer, *refs):
    pairs, terms, potential_ref = refs[:4], refs[4:-1], refs[-1]
    late = [sibling_term(pairs[0], pairs[1], sides), sibling_term(pairs[2], pairs[3], sides)]
    terms = [ref[...] for ref in terms] + late
    potential = terms[-1]
    for level in range(levels - 2, -1, -1):
        potential = dot_split(potential, transfer[level]) + terms[level]
    potential_ref[...] = potential


def lane_norms(tall):
    square = jnp.square(tall.astype(F32))
    norms = jnp.sum(square, axis=1, keepdims=True) * (2.0 * LOG2E / tall.shape[1])
    return jnp.broadcast_to(norms, (tall.shape[0], 128))


def turn_kernel(points, ordered, tall_ref, norms_ref):
    dimension, rows = points.shape
    sides = ordered.shape[0]
    tall_ref[:rows] = jnp.transpose(points[...])
    norms_ref[...] = lane_norms(tall_ref[:rows])
    for number in range(rows // dimension):
        first = rows + number * sides
        tall_ref[first : first + sides] = ordered[:, number * dimension : (number + 1) * dimension]


def bands(tall, norms, wide):
    dimension, rows = wide.shape
    scale = 2.0 * LOG2E / dimension
    target_norms = row_norms(wide[...]) * scale
    for row in range(0, rows, dimension):
        band = slice(row, row + dimension)
        source = tall[band]
        inner = dot(source, wide[...])
        own = lane_norms(source) if norms is None else norms[band]
        squares = jnp.tile(own, (1, rows // 128)) + target_norms
        yield band, jnp.exp2((2.0 * scale) * inner - squares).astype(BF16)


def self_kernel(tall, norms, wide, ordered, near_ref):
    for band, tile in bands(tall, norms, wide):
        near_ref[:, band] = dot(ordered[...], tile, NT)


def back_kernel(tall, norms, ordered, back_wide, back_ordered, marks, near, near_ref, held_ref):
    near_ref[...] = near[...]
    used = marked(marks[...], -2)

    @pl.when(used)
    def _():
        for band, tile in bands(tall, norms, back_wide):
            near_ref[:, band] += dot(back_ordered[...], tile, NT)
            part = dot(ordered[:, band], tile)
            if band.start:
                held_ref[...] += part
            else:
                held_ref[...] = part

    @pl.when(jnp.logical_not(used))
    def _():
        held_ref[...] = jnp.zeros_like(held_ref)


def pair_kernel(wide, ordered, side_tall, back_wide, back_ordered, marks, message, near, held,
                near_ref, back_ref, side_ref, sum_ref):
    dimension, rows = wide.shape
    sides = ordered.shape[0]
    odd = lax.rem(lax.axis_index("leaf"), 2)
    go_odd = jnp.logical_and(odd == 1, marked(message[message.shape[0] - PAD :], -1))
    go_even = jnp.logical_and(odd == 0, marked(marks[...], 1))

    def pair(other_wide, other_ordered):
        for band, tile in bands(side_tall, None, other_wide):
            side_ref[:, band] = dot(other_ordered[...], tile, NT).astype(BF16)
            first = rows + band.start // dimension * sides
            part = dot(side_tall[first : first + sides], tile)
            if band.start:
                sum_ref[...] += part
            else:
                sum_ref[...] = part

    @pl.when(go_odd)
    def _():
        pair(back_wide, back_ordered)
        back_ref[...] = (held[...] + sum_ref[...]).astype(BF16)
        near_ref[...] = near[...]

    @pl.when(go_even)
    def _():
        pair(wide, ordered)
        back_ref[...] = held[...].astype(BF16)
        near_ref[...] = near[...] + sum_ref[...]

    @pl.when(jnp.logical_not(jnp.logical_or(go_odd, go_even)))
    def _():
        back_ref[...] = held[...].astype(BF16)
        near_ref[...] = near[...]
        side_ref[...] = jnp.zeros_like(side_ref)


def far_kernel(others, own_top, potential, product, interp, near, *refs):
    tops, out_ref = refs[:others], refs[-1]
    sides = out_ref.shape[0]
    dimension = own_top.shape[0] - sides
    total = potential[...]
    above = None
    for top in tops:
        part = dot(
            top[dimension:].astype(F32),
            small_kernel(top[:dimension], own_top[:dimension]),
            NN,
            HIGHEST,
        )
        above = part if above is None else above + part
    if above is not None:
        total = total + dot(above, product[...], NN, HIGHEST)
    out_ref[...] = near[...] + dot_split(total, interp[...])


def total_kernel(here, back, side, out_ref):
    out_ref[...] = here[...] + (back[...].astype(F32) + side[...].astype(F32))


def call(kernel, outs, args, scratch=(), anywhere=False, flops=0, exps=0, name=None):
    vmem = pl.BlockSpec(memory_space=pltpu.VMEM)
    rest = pl.BlockSpec(memory_space=pl.ANY) if anywhere else vmem
    moved = 0 if anywhere or flops == 0 else sum(a.size * a.dtype.itemsize for a in list(args) + list(outs))
    return pl.pallas_call(
        kernel,
        out_shape=outs,
        in_specs=[rest] * len(args),
        out_specs=[rest if anywhere else vmem] * len(outs),
        scratch_shapes=list(scratch),
        compiler_params=pltpu.CompilerParams(
            vmem_limit_bytes=START_VMEM if anywhere else VMEM_LIMIT
        ),
        cost_estimate=pl.CostEstimate(flops=flops, bytes_accessed=moved, transcendentals=exps),
        name=name,
    )(*args)


def swapped(value, axis, flip):
    count = lax.axis_size(axis)
    return lax.ppermute(value, axis, [(place, place ^ flip) for place in range(count)])


def rotated(value, axis, turn):
    count = lax.axis_size(axis)
    return lax.ppermute(value, axis, [(place, (place + turn) % count) for place in range(count)])


def shifted(value, axis, step):
    places = range(lax.axis_size(axis))
    return lax.ppermute(
        value, axis, [(place, place + step) for place in places if place + step in places]
    )


def shape(dims, dtype):
    return jax.ShapeDtypeStruct(dims, dtype)


def local(points, charges, order, near_mask, skeletons, leaf_interp, transfer):
    dimension, rows = points.shape
    sides, count = charges.shape[0], leaf_interp.shape[0]
    leaves, groups = lax.axis_size("leaf"), lax.axis_size("grp")
    levels = leaves.bit_length() - 1
    skeletons = jnp.transpose(skeletons, (1, 0, 2))
    transfer = transfer[0]
    block_sums = shape((sides, rows), F32)
    block_values = shape((sides, rows), BF16)
    node_points = shape((dimension, count), BF16)
    node_sums = shape((sides, count), F32)
    tile_flops = 2 * rows * rows * (dimension + 2 * sides)

    back_points = rotated(points, "leaf", 2)

    inputs = [order.reshape(1, rows), skeletons, near_mask, charges, points, leaf_interp, transfer]
    made = [
        block_values,
        node_points,
        shape((PAD, count), BF16),
        shape((dimension + 2 * sides + PAD, count), BF16),
        node_sums,
    ]
    ordered, coords, marks, message, passed = call(
        start_kernel,
        made,
        inputs,
        scratch=[pltpu.VMEM(value.shape, value.dtype) for value in inputs + made]
        + [pltpu.SemaphoreType.DMA((len(inputs),)), pltpu.SemaphoreType.DMA((len(made),))],
        anywhere=True,
        name="start",
    )
    tall, norms = call(
        turn_kernel,
        [shape((rows + sides * rows // dimension, dimension), BF16), shape((rows, 128), F32)],
        [points, ordered],
        name="turn",
    )
    (near,) = call(
        self_kernel,
        [block_sums],
        [tall, norms, points, ordered],
        name="self_tile",
    )

    history, terms = [], []
    for level in range(levels):
        received = swapped(message, "leaf", 1 << level)
        if level == 0:
            received, near = lax.optimization_barrier((received, near))
            first_received = received
            side_tall = swapped(tall, "leaf", 1)
        if level == 1:
            received, back_points = lax.optimization_barrier((received, back_points))
        last = level == levels - 1
        if level and not last:
            made = call(
                functools.partial(term_kernel, sides, levels),
                [node_sums] + [shape((count, count), F32)] * (level == 1),
                [transfer] + history[-2:],
                flops=8 * dimension * count * count,
                name="sibling_term",
            )
            terms.append(made[0])
            if level == 1:
                product = made[1]
            passed = lax.optimization_barrier((passed, made[0]))[0]
        history += [coords, received]
        if level == levels - 2:
            near, held = call(
                back_kernel,
                [block_sums, block_sums],
                [tall, norms, ordered, back_points, back_ordered, marks]
                + [lax.optimization_barrier((near, passed))[0]],
                flops=tile_flops,
                exps=rows * rows,
                name="back_tile",
            )
            passed, held = lax.optimization_barrier((passed, held))
        if last:
            near, back, side = call(
                pair_kernel,
                [block_sums, block_values, block_values],
                [points, ordered, side_tall, back_points, back_ordered, marks, first_received]
                + [lax.optimization_barrier((near, passed))[0], held],
                scratch=[pltpu.VMEM((sides, rows), F32)],
                flops=tile_flops,
                exps=rows * rows,
                name="pair_tile",
            )
            passed, near = lax.optimization_barrier((passed, near))
            back = shifted(back, "leaf", -2)
            side = swapped(side, "leaf", 1)
        if last:
            outs = [shape((dimension + sides, count), BF16)]
        else:
            outs = [node_points, shape((dimension + 2 * sides, count), BF16), node_sums]
        results = call(
            functools.partial(round_kernel, level, last),
            outs,
            [skeletons, transfer, coords, passed, received],
            flops=(JOIN_FLOPS if level < 2 else 8) * dimension * count * count,
            name="join_level",
        )
        if not last:
            coords, message, passed = results
        if level == 0:
            sent = lax.optimization_barrier((ordered, results[-1]))[0]
            back_ordered = shifted(sent, "leaf", 2)
    own_top = results[0]
    tops = [rotated(own_top, "grp", turn) for turn in range(1, groups)]
    (potential,) = call(
        functools.partial(last_terms_kernel, sides, levels),
        [node_sums],
        [transfer] + history[-4:] + terms,
        flops=8 * dimension * count * count,
        exps=count * count,
        name="last_terms",
    )
    (here,) = call(
        functools.partial(far_kernel, len(tops)),
        [block_sums],
        [own_top, potential, product, leaf_interp, near] + tops,
        flops=4 * sides * rows * count,
        name="far_field",
    )
    (out,) = call(total_kernel, [block_sums], [here, back, side], flops=2 * sides * rows, name="total")
    return out


def solution(mesh):
    in_specs = (
        P(None, ("leaf", "grp")),
        P(None, ("leaf", "grp")),
        P(("leaf", "grp")),
        P(("leaf", "grp"), None),
        P(("leaf", "grp"), None, None),
        P(None, ("leaf", "grp")),
        P(("leaf", "grp"), None, None, None),
    )
    out_specs = P(None, ("leaf", "grp"))
    return jax.shard_map(local, mesh=mesh, in_specs=in_specs, out_specs=out_specs, check_vma=False)
```

profile of v0, /device:TPU:0, one launch (start us, length us, event | category | flops | bytes accessed | tf_op | source)
XLA Modules:
  0.0 38.0 jit_solution(1666886729810602236)
XLA Ops:
  0.0 3.0 %collective-permute-start.2 = (bf16[256,1024]{1,0:T(8,128)(2,1)}, bf16[256,1024]{1,0:T(8,128)(2,1)S(1)}, u32[]{:S(2)}, u32[]{:S(2)}) collective-permute-start(bf16[256,1024]{1,0:T(8,128)(2,1)} %wide.3), channel_id=1, source_target_pairs={{0,4},{2,6},{4,8},{6,10},{8,12},{10,14},{12,16},{14,18},{16,20},{1... | collective-permute-start | bytes 1572872 | tf_op jit(solution)/shard_map/ppermute | solution.py:313
  3.0 0.0 copy-start.1
  3.0 3.0 %start.1 = (bf16[64,1024]{1,0:T(8,128)(2,1)}, bf16[256,128]{1,0:T(8,128)(2,1)}, bf16[16,128]{1,0:T(8,128)(2,1)}, bf16[400,128]{1,0:T(8,128)(2,1)}, f32[64,128]{1,0:T(8,128)}) custom-call(s32[1,1024]{1,0:T(1,128)} %bitcast.16, s32[5,1,128]{2,1,0:T(1,128)} %bitcast.11, s32[1,5]{1,0:T(1,128)} %refs_2_.1, bf16[64,1024]{1,0:T(8,128)(2,1)} %refs_3_.1, ...), custom_call_target="tpu_custom_call" | custom-call | tf_op jit(solution)/shard_map/start/pallas_call | solution.py:292
  6.0 1.6 %collective-permute-start = (bf16[400,128]{1,0:T(8,128)(2,1)}, bf16[400,128]{1,0:T(8,128)(2,1)S(1)}, u32[]{:S(2)}, u32[]{:S(2)}) collective-permute-start(bf16[400,128]{1,0:T(8,128)(2,1)} %get-tuple-element.43), channel_id=1, source_target_pairs={{0,2},{2,0},{4,6},{6,4},{8,10},{10,8},{12,14},{14,12},{16,18},{18,... | collective-permute-start | bytes 307208 | tf_op jit(solution)/shard_map/ppermute | solution.py:308
  7.5 0.0 copy-done.1
  7.6 0.0 copy-start.3
  7.6 0.9 %copy-done.3 = bf16[64,1024]{1,0:T(8,128)(2,1)S(1)} copy-done((bf16[64,1024]{1,0:T(8,128)(2,1)S(1)}, bf16[64,1024]{1,0:T(8,128)(2,1)}, u32[]{:S(2)}) %copy-start.3) | copy-done | bytes 131096
  8.5 0.3 turn.1
  8.8 0.6 %collective-permute-start.5 = (bf16[1280,256]{1,0:T(8,128)(2,1)S(1)}, bf16[1280,256]{1,0:T(8,128)(2,1)S(1)}, u32[]{:S(2)}, u32[]{:S(2)}) collective-permute-start(bf16[1280,256]{1,0:T(8,128)(2,1)S(1)} %get-tuple-element.45.tall), channel_id=1, source_target_pairs={{0,2},{2,0},{4,6},{6,4},{8,10},{10,8},{12,14},{14,12},{16,18},{18,... | collective-permute-start | bytes 1966088 | tf_op jit(solution)/shard_map/ppermute | solution.py:308
  9.4 0.0 copy-start
  9.4 0.0 copy-start.5
  9.4 0.0 copy-start.7
  9.4 1.4 %self_tile.1.near = f32[64,1024]{1,0:T(8,128)S(1)} custom-call(bf16[1280,256]{1,0:T(8,128)(2,1)S(1)} %get-tuple-element.45.tall, f32[1024,128]{1,0:T(8,128)S(1)} %get-tuple-element.46.norms, bf16[256,1024]{1,0:T(8,128)(2,1)S(1)} %copy-done.1, bf16[64,1024]{1,0:T(8,128)(2,1)S(1)} %copy-done.3), custom_call_target="tpu_custom_call" | custom-call | tf_op jit(solution)/shard_map/self_tile/pallas_call | solution.py:292
  10.9 0.0 copy-start.6
  10.9 0.3 collective-permute-done.message
  11.1 0.0 copy-done
  11.1 0.0 copy-done.5
  11.1 0.0 copy-done.7
  11.1 0.4 %copy-done.6 = s32[1,5,128]{2,0,1:T(1,128)S(1)} copy-done((s32[1,5,128]{2,0,1:T(1,128)S(1)}, s32[1,5,128]{2,0,1:T(1,128)}, u32[]{:S(2)}) %copy-start.6) | copy-done | bytes 2584
  11.5 0.2 join_level.4
  11.8 1.6 %collective-permute-start.1 = (bf16[384,128]{1,0:T(8,128)(2,1)S(1)}, bf16[384,128]{1,0:T(8,128)(2,1)S(1)}, u32[]{:S(2)}, u32[]{:S(2)}) collective-permute-start(bf16[384,128]{1,0:T(8,128)(2,1)S(1)} %get-tuple-element.52), channel_id=1, source_target_pairs={{0,4},{2,6},{4,0},{6,2},{8,12},{10,14},{12,8},{14,10},{16,20},{18,... | collective-permute-start | bytes 294920 | tf_op jit(solution)/shard_map/ppermute | solution.py:308
  13.3 0.0 copy-start.4
  13.3 0.8 %sibling_term.2 = (f32[64,128]{1,0:T(8,128)S(1)}, f32[128,128]{1,0:T(8,128)S(1)}) custom-call(bf16[4,128,128]{2,1,0:T(8,128)(2,1)S(1)} %bitcast.5, bf16[256,128]{1,0:T(8,128)(2,1)S(1)} %copy-done.5, bf16[400,128]{1,0:T(8,128)(2,1)S(1)} %collective-permute-done.message), custom_call_target="tpu_custom_call" | custom-call | flops 33554432 | bytes 397312 | tf_op jit(solution)/shard_map/sibling_term/pallas_call | solution.py:292
  14.1 0.1 copy-done.4
  14.3 2.4 %collective-permute-start.3 = (bf16[64,1024]{1,0:T(8,128)(2,1)S(1)}, bf16[64,1024]{1,0:T(8,128)(2,1)S(1)}, u32[]{:S(2)}, u32[]{:S(2)}) collective-permute-start(bf16[64,1024]{1,0:T(8,128)(2,1)S(1)} %copy-done.4), channel_id=1, source_target_pairs={{0,4},{2,6},{4,8},{6,10},{8,12},{10,14},{12,16},{14,18},{16,20},{1... | collective-permute-start | bytes 393224 | tf_op jit(solution)/shard_map/ppermute | solution.py:318
  16.7 3.6 %collective-permute-done.1.message = bf16[384,128]{1,0:T(8,128)(2,1)S(1)} collective-permute-done((bf16[384,128]{1,0:T(8,128)(2,1)S(1)}, bf16[384,128]{1,0:T(8,128)(2,1)S(1)}, u32[]{:S(2)}, u32[]{:S(2)}) %collective-permute-start.1) | collective-permute-done | bytes 98336 | tf_op jit(solution)/shard_map/ppermute | solution.py:308
  20.2 0.0 collective-permute-done.2.back_wide
  20.2 0.2 join_level.5
  20.5 0.0 copy-start.8
  20.5 0.1 collective-permute-start.4
  20.6 0.5 %sibling_term.3.refs_5_ = f32[64,128]{1,0:T(8,128)S(1)} custom-call(bf16[4,128,128]{2,1,0:T(8,128)(2,1)S(1)} %bitcast.7, bf16[256,128]{1,0:T(8,128)(2,1)S(1)} %get-tuple-element.48.coords, bf16[384,128]{1,0:T(8,128)(2,1)S(1)} %collective-permute-done.1.message), custom_call_target="tpu_custom_call" | custom-call | flops 33554432 | bytes 327680 | tf_op jit(solution)/shard_map/sibling_term/pallas_call | solution.py:292
  21.0 0.0 collective-permute-done.3.back_ordered
  21.0 0.1 copy-done.8
  21.1 0.2 back_tile.1
  21.3 4.0 %collective-permute-done.4.message.refs_1_ = bf16[384,128]{1,0:T(8,128)(2,1)S(1)} collective-permute-done((bf16[384,128]{1,0:T(8,128)(2,1)S(1)}, bf16[384,128]{1,0:T(8,128)(2,1)S(1)}, u32[]{:S(2)}, u32[]{:S(2)}) %collective-permute-start.4) | collective-permute-done | bytes 98336 | tf_op jit(solution)/shard_map/ppermute | solution.py:308
  25.3 0.2 join_level.6
  25.5 3.4 %collective-permute-start.6 = (bf16[384,128]{1,0:T(8,128)(2,1)S(1)}, bf16[384,128]{1,0:T(8,128)(2,1)S(1)}, u32[]{:S(2)}, u32[]{:S(2)}) collective-permute-start(bf16[384,128]{1,0:T(8,128)(2,1)S(1)} %get-tuple-element.72), channel_id=1, source_target_pairs={{0,16},{2,18},{4,20},{6,22},{8,24},{10,26},{12,28},{14,30},{16,0},... | collective-permute-start | bytes 294920 | tf_op jit(solution)/shard_map/ppermute | solution.py:308
  28.9 0.0 collective-permute-done.5.side_tall
  28.9 0.2 pair_tile.1
  29.1 1.3 %collective-permute-start.8 = (bf16[64,1024]{1,0:T(8,128)(2,1)S(1)}, bf16[64,1024]{1,0:T(8,128)(2,1)S(1)}, u32[]{:S(2)}, u32[]{:S(2)}) collective-permute-start(bf16[64,1024]{1,0:T(8,128)(2,1)S(1)} %get-tuple-element.75), channel_id=1, source_target_pairs={{4,0},{6,2},{8,4},{10,6},{12,8},{14,10},{16,12},{18,14},{20,16},{2... | collective-permute-start | bytes 393224 | tf_op jit(solution)/shard_map/ppermute | solution.py:318
  30.4 0.2 collective-permute-start.9
  30.5 3.7 %collective-permute-done.6.message.refs_3_ = bf16[384,128]{1,0:T(8,128)(2,1)S(1)} collective-permute-done((bf16[384,128]{1,0:T(8,128)(2,1)S(1)}, bf16[384,128]{1,0:T(8,128)(2,1)S(1)}, u32[]{:S(2)}, u32[]{:S(2)}) %collective-permute-start.6) | collective-permute-done | bytes 98336 | tf_op jit(solution)/shard_map/ppermute | solution.py:308
  34.2 0.2 join_level.7.own_top
  34.4 0.0 copy-start.2
  34.4 0.1 collective-permute-start.7
  34.5 0.9 %last_terms.1.potential = f32[64,128]{1,0:T(8,128)S(1)} custom-call(bf16[4,128,128]{2,1,0:T(8,128)(2,1)S(1)} %bitcast.10, bf16[256,128]{1,0:T(8,128)(2,1)S(1)} %get-tuple-element.54.coords.refs_0_, bf16[384,128]{1,0:T(8,128)(2,1)S(1)} %collective-permute-done.4.message.refs_1_, bf16[256,128]{1,0:T(8,128)(2,1)S(1)} %get-tuple-element.65.coords.refs_2_, ...), custom_call_target="tpu_custom_call" | custom-call | flops 33554432 | bytes 557056 | tf_op jit(solution)/shard_map/last_terms/pallas_call | solution.py:292
  35.4 0.3 collective-permute-done.7.refs_0_
  35.8 0.0 copy-done.2
  35.8 0.9 %far_field.1.here = f32[64,1024]{1,0:T(8,128)S(1)} custom-call(bf16[320,128]{1,0:T(8,128)(2,1)S(1)} %join_level.7.own_top, f32[64,128]{1,0:T(8,128)S(1)} %last_terms.1.potential, f32[128,128]{1,0:T(8,128)S(1)} %get-tuple-element.73.product, bf16[128,1024]{1,0:T(8,128)(2,1)S(1)} %copy-done.2, f32[64,1024]{1,0:T(8,128)S(1)} %get-tuple-element.74.near, ...), custom_call_target="tpu_custom_call" | custom-call | flops 33554432 | bytes 1048576 | tf_op jit(solution)/shard_map/far_field/pallas_call | solution.py:292
  36.6 0.6 %collective-permute-done.8.back = bf16[64,1024]{1,0:T(8,128)(2,1)S(1)} collective-permute-done((bf16[64,1024]{1,0:T(8,128)(2,1)S(1)}, bf16[64,1024]{1,0:T(8,128)(2,1)S(1)}, u32[]{:S(2)}, u32[]{:S(2)}) %collective-permute-start.8) | collective-permute-done | bytes 131104 | tf_op jit(solution)/shard_map/ppermute | solution.py:318
  37.2 0.0 collective-permute-done.9.side
  37.3 0.7 %total.1 = f32[64,1024]{1,0:T(8,128)} custom-call(f32[64,1024]{1,0:T(8,128)S(1)} %far_field.1.here, bf16[64,1024]{1,0:T(8,128)(2,1)S(1)} %collective-permute-done.8.back, bf16[64,1024]{1,0:T(8,128)(2,1)S(1)} %collective-permute-done.9.side), custom_call_target="tpu_custom_call" | custom-call | flops 131072 | bytes 786432 | tf_op jit(solution)/shard_map/total/pallas_call | solution.py:292
Async XLA Ops:
  0.0 20.2 %collective-permute-start.2 = (bf16[256,1024]{1,0:T(8,128)(2,1)}, bf16[256,1024]{1,0:T(8,128)(2,1)S(1)}, u32[]{:S(2)}, u32[]{:S(2)}) collective-permute-start(bf16[256,1024]{1,0:T(8,128)(2,1)} %wide.3), channel_id=1, source_target_pairs={{0,4},{2,6},{4,8},{6,10},{8,12},{10,14},{12,16},{14,18},{16,20},{1... | collective-permute-start | bytes 1572872 | tf_op jit(solution)/shard_map/ppermute | solution.py:313
  3.0 4.6 %copy-start.1 = (bf16[256,1024]{1,0:T(8,128)(2,1)S(1)}, bf16[256,1024]{1,0:T(8,128)(2,1)}, u32[]{:S(2)}) copy-start(bf16[256,1024]{1,0:T(8,128)(2,1)} %wide.3) | copy-start | bytes 1572868
  6.0 5.1 %collective-permute-start = (bf16[400,128]{1,0:T(8,128)(2,1)}, bf16[400,128]{1,0:T(8,128)(2,1)S(1)}, u32[]{:S(2)}, u32[]{:S(2)}) collective-permute-start(bf16[400,128]{1,0:T(8,128)(2,1)} %get-tuple-element.43), channel_id=1, source_target_pairs={{0,2},{2,0},{4,6},{6,4},{8,10},{10,8},{12,14},{14,12},{16,18},{18,... | collective-permute-start | bytes 307208 | tf_op jit(solution)/shard_map/ppermute | solution.py:308
  7.6 0.9 %copy-start.3 = (bf16[64,1024]{1,0:T(8,128)(2,1)S(1)}, bf16[64,1024]{1,0:T(8,128)(2,1)}, u32[]{:S(2)}) copy-start(bf16[64,1024]{1,0:T(8,128)(2,1)} %get-tuple-element.58.ordered) | copy-start | bytes 393220
  8.8 20.1 %collective-permute-start.5 = (bf16[1280,256]{1,0:T(8,128)(2,1)S(1)}, bf16[1280,256]{1,0:T(8,128)(2,1)S(1)}, u32[]{:S(2)}, u32[]{:S(2)}) collective-permute-start(bf16[1280,256]{1,0:T(8,128)(2,1)S(1)} %get-tuple-element.45.tall), channel_id=1, source_target_pairs={{0,2},{2,0},{4,6},{6,4},{8,10},{10,8},{12,14},{14,12},{16,18},{18,... | collective-permute-start | bytes 1966088 | tf_op jit(solution)/shard_map/ppermute | solution.py:308
  9.4 1.7 %copy-start = (bf16[1,4,128,128]{3,2,1,0:T(8,128)(2,1)S(1)}, bf16[1,4,128,128]{3,2,1,0:T(8,128)(2,1)}, u32[]{:S(2)}) copy-start(bf16[1,4,128,128]{3,2,1,0:T(8,128)(2,1)} %param.13) | copy-start | bytes 393220
  9.4 1.7 %copy-start.5 = (bf16[256,128]{1,0:T(8,128)(2,1)S(1)}, bf16[256,128]{1,0:T(8,128)(2,1)}, u32[]{:S(2)}) copy-start(bf16[256,128]{1,0:T(8,128)(2,1)} %get-tuple-element.41.coords) | copy-start | bytes 196612
  9.4 1.7 %copy-start.7 = (f32[64,128]{1,0:T(8,128)S(1)}, f32[64,128]{1,0:T(8,128)}, u32[]{:S(2)}) copy-start(f32[64,128]{1,0:T(8,128)} %get-tuple-element.42.passed) | copy-start | bytes 98308
  10.9 0.7 %copy-start.6 = (s32[1,5,128]{2,0,1:T(1,128)S(1)}, s32[1,5,128]{2,0,1:T(1,128)}, u32[]{:S(2)}) copy-start(s32[1,5,128]{2,0,1:T(1,128)} %param.11) | copy-start | bytes 7684
  11.8 8.5 %collective-permute-start.1 = (bf16[384,128]{1,0:T(8,128)(2,1)S(1)}, bf16[384,128]{1,0:T(8,128)(2,1)S(1)}, u32[]{:S(2)}, u32[]{:S(2)}) collective-permute-start(bf16[384,128]{1,0:T(8,128)(2,1)S(1)} %get-tuple-element.52), channel_id=1, source_target_pairs={{0,4},{2,6},{4,0},{6,2},{8,12},{10,14},{12,8},{14,10},{16,20},{18,... | collective-permute-start | bytes 294920 | tf_op jit(solution)/shard_map/ppermute | solution.py:308
  13.3 0.9 %copy-start.4 = (bf16[64,1024]{1,0:T(8,128)(2,1)S(1)}, bf16[64,1024]{1,0:T(8,128)(2,1)}, u32[]{:S(2)}) copy-start(bf16[64,1024]{1,0:T(8,128)(2,1)} %get-tuple-element.58.ordered) | copy-start | bytes 393220
  14.3 6.8 %collective-permute-start.3 = (bf16[64,1024]{1,0:T(8,128)(2,1)S(1)}, bf16[64,1024]{1,0:T(8,128)(2,1)S(1)}, u32[]{:S(2)}, u32[]{:S(2)}) collective-permute-start(bf16[64,1024]{1,0:T(8,128)(2,1)S(1)} %copy-done.4), channel_id=1, source_target_pairs={{0,4},{2,6},{4,8},{6,10},{8,12},{10,14},{12,16},{14,18},{16,20},{1... | collective-permute-start | bytes 393224 | tf_op jit(solution)/shard_map/ppermute | solution.py:318
  20.5 0.7 %copy-start.8 = (bf16[16,128]{1,0:T(8,128)(2,1)S(1)}, bf16[16,128]{1,0:T(8,128)(2,1)}, u32[]{:S(2)}) copy-start(bf16[16,128]{1,0:T(8,128)(2,1)} %get-tuple-element.59.marks) | copy-start | bytes 12292
  20.5 4.8 %collective-permute-start.4 = (bf16[384,128]{1,0:T(8,128)(2,1)S(1)}, bf16[384,128]{1,0:T(8,128)(2,1)S(1)}, u32[]{:S(2)}, u32[]{:S(2)}) collective-permute-start(bf16[384,128]{1,0:T(8,128)(2,1)S(1)} %get-tuple-element.64), channel_id=1, source_target_pairs={{0,8},{2,10},{4,12},{6,14},{8,0},{10,2},{12,4},{14,6},{16,24},{18,... | collective-permute-start | bytes 294920 | tf_op jit(solution)/shard_map/ppermute | solution.py:308
  25.5 8.7 %collective-permute-start.6 = (bf16[384,128]{1,0:T(8,128)(2,1)S(1)}, bf16[384,128]{1,0:T(8,128)(2,1)S(1)}, u32[]{:S(2)}, u32[]{:S(2)}) collective-permute-start(bf16[384,128]{1,0:T(8,128)(2,1)S(1)} %get-tuple-element.72), channel_id=1, source_target_pairs={{0,16},{2,18},{4,20},{6,22},{8,24},{10,26},{12,28},{14,30},{16,0},... | collective-permute-start | bytes 294920 | tf_op jit(solution)/shard_map/ppermute | solution.py:308
  29.1 8.2 %collective-permute-start.8 = (bf16[64,1024]{1,0:T(8,128)(2,1)S(1)}, bf16[64,1024]{1,0:T(8,128)(2,1)S(1)}, u32[]{:S(2)}, u32[]{:S(2)}) collective-permute-start(bf16[64,1024]{1,0:T(8,128)(2,1)S(1)} %get-tuple-element.75), channel_id=1, source_target_pairs={{4,0},{6,2},{8,4},{10,6},{12,8},{14,10},{16,12},{18,14},{20,16},{2... | collective-permute-start | bytes 393224 | tf_op jit(solution)/shard_map/ppermute | solution.py:318
  30.4 6.9 %collective-permute-start.9 = (bf16[64,1024]{1,0:T(8,128)(2,1)S(1)}, bf16[64,1024]{1,0:T(8,128)(2,1)S(1)}, u32[]{:S(2)}, u32[]{:S(2)}) collective-permute-start(bf16[64,1024]{1,0:T(8,128)(2,1)S(1)} %get-tuple-element.76), channel_id=1, source_target_pairs={{0,2},{2,0},{4,6},{6,4},{8,10},{10,8},{12,14},{14,12},{16,18},{18,... | collective-permute-start | bytes 393224 | tf_op jit(solution)/shard_map/ppermute | solution.py:308
  34.4 1.4 %copy-start.2 = (bf16[128,1024]{1,0:T(8,128)(2,1)S(1)}, bf16[128,1024]{1,0:T(8,128)(2,1)}, u32[]{:S(2)}) copy-start(bf16[128,1024]{1,0:T(8,128)(2,1)} %interp.1) | copy-start | bytes 786436
  34.4 1.3 %collective-permute-start.7 = (bf16[320,128]{1,0:T(8,128)(2,1)S(1)}, bf16[320,128]{1,0:T(8,128)(2,1)S(1)}, u32[]{:S(2)}, u32[]{:S(2)}) collective-permute-start(bf16[320,128]{1,0:T(8,128)(2,1)S(1)} %join_level.7.own_top), channel_id=1, source_target_pairs={{0,1},{1,0},{2,3},{3,2},{4,5},{5,4},{6,7},{7,6},{8,9},{9,8},{10,11... | collective-permute-start | bytes 245768 | tf_op jit(solution)/shard_map/ppermute | solution.py:313
where the time goes:
time: 37.6 us; the launch traced here: 38 us
  starting transfers between devices  14.1 us (38%)
  waiting for transfers between devices  12.5 us (33%)
  Pallas kernels  9.75 us (26%)
  local copies, waits for them, and re-layouts  1.52 us (4%)
    ppermute x6, waiting for transfers between devices, swapped(): lax.ppermute(value, axis, [(place, place ^ flip) for place in range(count)])  11.5 us
    pallas_call x14, Pallas kernels, call(): pl.pallas_call(kernel, out_shape=outs, in_specs=[rest] * len(args), out_s...  9.75 us
    ppermute x6, starting transfers between devices, swapped(): lax.ppermute(value, axis, [(place, place ^ flip) for place in range(count)])  7.35 us
    ppermute x2, starting transfers between devices, shifted(): lax.ppermute(value, axis, [(place, place + step) for place in places if p...  3.7 us
    ppermute x2, starting transfers between devices, rotated(): lax.ppermute(value, axis, [(place, (place + turn) % count) for place in r...  3.04 us
    unnamed x18, local copies, waits for them, and re-layouts  1.52 us
  transfers between devices with their start and end apart: 10, of which 6 were waited for; matrix products, arithmetic and copies ran while one was open for 0% of the time, Pallas kernels for 24%

commit v1 on v0

--- a/solution.py
+++ b/solution.py
@@ -415,7 +415,7 @@
                 name="pair_tile",
             )
             passed, near = lax.optimization_barrier((passed, near))
-            back = shifted(back, "leaf", -2)
+            back = rotated(back, "leaf", -2)
             side = swapped(side, "leaf", 1)
         if last:
             outs = [shape((dimension + sides, count), BF16)]

time: 37.6 us -> 38.5 us (1.024)
  the two profiles are of different devices: /device:TPU:0 before, /device:TPU:25 now
where the time goes in v1:
time: 38.5 us; the launch traced here: 38.2 us
  waiting for transfers between devices  16 us (42%)
  Pallas kernels  11.5 us (30%)
  starting transfers between devices  8.75 us (23%)
  local copies, waits for them, and re-layouts  1.76 us (5%)
    ppermute x6, waiting for transfers between devices, swapped(): lax.ppermute(value, axis, [(place, place ^ flip) for place in range(count)])  16 us
    pallas_call x14, Pallas kernels, call(): pl.pallas_call(kernel, out_shape=outs, in_specs=[rest] * len(args), out_s...  11.5 us
    ppermute x6, starting transfers between devices, swapped(): lax.ppermute(value, axis, [(place, place ^ flip) for place in range(count)])  3.5 us
    ppermute x1, starting transfers between devices, shifted(): lax.ppermute(value, axis, [(place, place + step) for place in places if p...  3.35 us
    ppermute x3, starting transfers between devices, rotated(): lax.ppermute(value, axis, [(place, (place + turn) % count) for place in r...  1.9 us
    unnamed x18, local copies, waits for them, and re-layouts  1.76 us
  transfers between devices with their start and end apart: 10, of which 3 were waited for; matrix products, arithmetic and copies ran while one was open for 0% of the time, Pallas kernels for 28%

profile of v1, /device:TPU:25, one launch (start us, length us, event | category | flops | bytes accessed | tf_op | source)
XLA Modules:
  0.0 38.2 jit_solution(17516392650824187112)
XLA Ops:
  0.0 1.2 %collective-permute-start.2 = (bf16[256,1024]{1,0:T(8,128)(2,1)}, bf16[256,1024]{1,0:T(8,128)(2,1)S(1)}, u32[]{:S(2)}, u32[]{:S(2)}) collective-permute-start(bf16[256,1024]{1,0:T(8,128)(2,1)} %wide.3), channel_id=1, source_target_pairs={{0,4},{2,6},{4,8},{6,10},{8,12},{10,14},{12,16},{14,18},{16,20},{1... | collective-permute-start | bytes 1572872 | tf_op jit(solution)/shard_map/ppermute | solution.py:313
  1.2 0.0 copy-start.1
  1.2 3.0 %start.1 = (bf16[64,1024]{1,0:T(8,128)(2,1)}, bf16[256,128]{1,0:T(8,128)(2,1)}, bf16[16,128]{1,0:T(8,128)(2,1)}, bf16[400,128]{1,0:T(8,128)(2,1)}, f32[64,128]{1,0:T(8,128)}) custom-call(s32[1,1024]{1,0:T(1,128)} %bitcast.16, s32[5,1,128]{2,1,0:T(1,128)} %bitcast.11, s32[1,5]{1,0:T(1,128)} %refs_2_.1, bf16[64,1024]{1,0:T(8,128)(2,1)} %refs_3_.1, ...), custom_call_target="tpu_custom_call" | custom-call | tf_op jit(solution)/shard_map/start/pallas_call | solution.py:292
  4.3 1.3 %collective-permute-start = (bf16[400,128]{1,0:T(8,128)(2,1)}, bf16[400,128]{1,0:T(8,128)(2,1)S(1)}, u32[]{:S(2)}, u32[]{:S(2)}) collective-permute-start(bf16[400,128]{1,0:T(8,128)(2,1)} %get-tuple-element.43), channel_id=1, source_target_pairs={{0,2},{2,0},{4,6},{6,4},{8,10},{10,8},{12,14},{14,12},{16,18},{18,... | collective-permute-start | bytes 307208 | tf_op jit(solution)/shard_map/ppermute | solution.py:308
  5.5 0.0 copy-done.1
  5.6 0.0 copy-start.3
  5.6 0.9 %copy-done.3 = bf16[64,1024]{1,0:T(8,128)(2,1)S(1)} copy-done((bf16[64,1024]{1,0:T(8,128)(2,1)S(1)}, bf16[64,1024]{1,0:T(8,128)(2,1)}, u32[]{:S(2)}) %copy-start.3) | copy-done | bytes 131096
  6.5 0.3 turn.1
  6.8 0.3 collective-permute-start.5
  7.1 0.0 copy-start
  7.1 0.0 copy-start.5
  7.1 0.0 copy-start.7
  7.1 1.4 %self_tile.1.near = f32[64,1024]{1,0:T(8,128)S(1)} custom-call(bf16[1280,256]{1,0:T(8,128)(2,1)S(1)} %get-tuple-element.45.tall, f32[1024,128]{1,0:T(8,128)S(1)} %get-tuple-element.46.norms, bf16[256,1024]{1,0:T(8,128)(2,1)S(1)} %copy-done.1, bf16[64,1024]{1,0:T(8,128)(2,1)S(1)} %copy-done.3), custom_call_target="tpu_custom_call" | custom-call | tf_op jit(solution)/shard_map/self_tile/pallas_call | solution.py:292
  8.6 0.0 copy-start.6
  8.6 0.0 collective-permute-done.message
  8.6 0.0 copy-done
  8.6 0.0 copy-done.5
  8.6 0.0 copy-done.7
  8.6 0.6 %copy-done.6 = s32[1,5,128]{2,0,1:T(1,128)S(1)} copy-done((s32[1,5,128]{2,0,1:T(1,128)S(1)}, s32[1,5,128]{2,0,1:T(1,128)}, u32[]{:S(2)}) %copy-start.6) | copy-done | bytes 2584
  9.2 0.2 join_level.4
  9.5 0.1 collective-permute-start.1
  9.6 0.0 copy-start.4
  9.6 0.8 %sibling_term.2 = (f32[64,128]{1,0:T(8,128)S(1)}, f32[128,128]{1,0:T(8,128)S(1)}) custom-call(bf16[4,128,128]{2,1,0:T(8,128)(2,1)S(1)} %bitcast.5, bf16[256,128]{1,0:T(8,128)(2,1)S(1)} %copy-done.5, bf16[400,128]{1,0:T(8,128)(2,1)S(1)} %collective-permute-done.message), custom_call_target="tpu_custom_call" | custom-call | flops 33554432 | bytes 397312 | tf_op jit(solution)/shard_map/sibling_term/pallas_call | solution.py:292
  10.4 0.1 copy-done.4
  10.5 3.3 %collective-permute-start.3 = (bf16[64,1024]{1,0:T(8,128)(2,1)S(1)}, bf16[64,1024]{1,0:T(8,128)(2,1)S(1)}, u32[]{:S(2)}, u32[]{:S(2)}) collective-permute-start(bf16[64,1024]{1,0:T(8,128)(2,1)S(1)} %copy-done.4), channel_id=1, source_target_pairs={{0,4},{2,6},{4,8},{6,10},{8,12},{10,14},{12,16},{14,18},{16,20},{1... | collective-permute-start | bytes 393224 | tf_op jit(solution)/shard_map/ppermute | solution.py:318
  13.8 6.1 %collective-permute-done.1.message = bf16[384,128]{1,0:T(8,128)(2,1)S(1)} collective-permute-done((bf16[384,128]{1,0:T(8,128)(2,1)S(1)}, bf16[384,128]{1,0:T(8,128)(2,1)S(1)}, u32[]{:S(2)}, u32[]{:S(2)}) %collective-permute-start.1) | collective-permute-done | bytes 98336 | tf_op jit(solution)/shard_map/ppermute | solution.py:308
  19.9 0.0 collective-permute-done.2.back_wide
  19.9 0.2 join_level.5
  20.1 0.0 copy-start.8
  20.1 0.1 collective-permute-start.4
  20.2 0.5 %sibling_term.3.refs_5_ = f32[64,128]{1,0:T(8,128)S(1)} custom-call(bf16[4,128,128]{2,1,0:T(8,128)(2,1)S(1)} %bitcast.7, bf16[256,128]{1,0:T(8,128)(2,1)S(1)} %get-tuple-element.48.coords, bf16[384,128]{1,0:T(8,128)(2,1)S(1)} %collective-permute-done.1.message), custom_call_target="tpu_custom_call" | custom-call | flops 33554432 | bytes 327680 | tf_op jit(solution)/shard_map/sibling_term/pallas_call | solution.py:292
  20.7 0.0 collective-permute-done.3.back_ordered
  20.7 0.1 copy-done.8
  20.8 1.9 %back_tile.1 = (f32[64,1024]{1,0:T(8,128)S(1)}, f32[64,1024]{1,0:T(8,128)S(1)}) custom-call(bf16[1280,256]{1,0:T(8,128)(2,1)S(1)} %get-tuple-element.45.tall, f32[1024,128]{1,0:T(8,128)S(1)} %get-tuple-element.46.norms, bf16[64,1024]{1,0:T(8,128)(2,1)S(1)} %copy-done.4, bf16[256,1024]{1,0:T(8,128)(2,1)S(1)} %collective-permute-done.2.back_wide, ...), custom_call_target="tpu_custom_call" | custom-call | flops 805306368 | bytes 2756608 | tf_op jit(solution)/shard_map/back_tile/pallas_call | solution.py:292
  22.7 1.4 %collective-permute-done.4.message.refs_1_ = bf16[384,128]{1,0:T(8,128)(2,1)S(1)} collective-permute-done((bf16[384,128]{1,0:T(8,128)(2,1)S(1)}, bf16[384,128]{1,0:T(8,128)(2,1)S(1)}, u32[]{:S(2)}, u32[]{:S(2)}) %collective-permute-start.4) | collective-permute-done | bytes 98336 | tf_op jit(solution)/shard_map/ppermute | solution.py:308
  24.0 0.2 join_level.6
  24.3 0.1 collective-permute-start.6
  24.4 0.0 collective-permute-done.5.side_tall
  24.4 0.2 pair_tile.1
  24.5 0.1 collective-permute-start.8
  24.6 1.7 %collective-permute-start.9 = (bf16[64,1024]{1,0:T(8,128)(2,1)S(1)}, bf16[64,1024]{1,0:T(8,128)(2,1)S(1)}, u32[]{:S(2)}, u32[]{:S(2)}) collective-permute-start(bf16[64,1024]{1,0:T(8,128)(2,1)S(1)} %get-tuple-element.76), channel_id=1, source_target_pairs={{0,2},{2,0},{4,6},{6,4},{8,10},{10,8},{12,14},{14,12},{16,18},{18,... | collective-permute-start | bytes 393224 | tf_op jit(solution)/shard_map/ppermute | solution.py:308
  26.3 8.5 %collective-permute-done.6.message.refs_3_ = bf16[384,128]{1,0:T(8,128)(2,1)S(1)} collective-permute-done((bf16[384,128]{1,0:T(8,128)(2,1)S(1)}, bf16[384,128]{1,0:T(8,128)(2,1)S(1)}, u32[]{:S(2)}, u32[]{:S(2)}) %collective-permute-start.6) | collective-permute-done | bytes 98336 | tf_op jit(solution)/shard_map/ppermute | solution.py:308
  34.8 0.2 join_level.7.own_top
  35.0 0.0 copy-start.2
  35.0 0.6 %collective-permute-start.7 = (bf16[320,128]{1,0:T(8,128)(2,1)S(1)}, bf16[320,128]{1,0:T(8,128)(2,1)S(1)}, u32[]{:S(2)}, u32[]{:S(2)}) collective-permute-start(bf16[320,128]{1,0:T(8,128)(2,1)S(1)} %join_level.7.own_top), channel_id=1, source_target_pairs={{0,1},{1,0},{2,3},{3,2},{4,5},{5,4},{6,7},{7,6},{8,9},{9,8},{10,11... | collective-permute-start | bytes 245768 | tf_op jit(solution)/shard_map/ppermute | solution.py:313
  35.6 0.9 %last_terms.1.potential = f32[64,128]{1,0:T(8,128)S(1)} custom-call(bf16[4,128,128]{2,1,0:T(8,128)(2,1)S(1)} %bitcast.10, bf16[256,128]{1,0:T(8,128)(2,1)S(1)} %get-tuple-element.54.coords.refs_0_, bf16[384,128]{1,0:T(8,128)(2,1)S(1)} %collective-permute-done.4.message.refs_1_, bf16[256,128]{1,0:T(8,128)(2,1)S(1)} %get-tuple-element.65.coords.refs_2_, ...), custom_call_target="tpu_custom_call" | custom-call | flops 33554432 | bytes 557056 | tf_op jit(solution)/shard_map/last_terms/pallas_call | solution.py:292
  36.6 0.0 collective-permute-done.7.refs_0_
  36.6 0.0 copy-done.2
  36.6 0.9 %far_field.1.here = f32[64,1024]{1,0:T(8,128)S(1)} custom-call(bf16[320,128]{1,0:T(8,128)(2,1)S(1)} %join_level.7.own_top, f32[64,128]{1,0:T(8,128)S(1)} %last_terms.1.potential, f32[128,128]{1,0:T(8,128)S(1)} %get-tuple-element.73.product, bf16[128,1024]{1,0:T(8,128)(2,1)S(1)} %copy-done.2, f32[64,1024]{1,0:T(8,128)S(1)} %get-tuple-element.74.near, ...), custom_call_target="tpu_custom_call" | custom-call | flops 33554432 | bytes 1048576 | tf_op jit(solution)/shard_map/far_field/pallas_call | solution.py:292
  37.5 0.0 collective-permute-done.8.back
  37.5 0.0 collective-permute-done.9.side
  37.5 0.8 %total.1 = f32[64,1024]{1,0:T(8,128)} custom-call(f32[64,1024]{1,0:T(8,128)S(1)} %far_field.1.here, bf16[64,1024]{1,0:T(8,128)(2,1)S(1)} %collective-permute-done.8.back, bf16[64,1024]{1,0:T(8,128)(2,1)S(1)} %collective-permute-done.9.side), custom_call_target="tpu_custom_call" | custom-call | flops 131072 | bytes 786432 | tf_op jit(solution)/shard_map/total/pallas_call | solution.py:292
Async XLA Ops:
  0.0 19.9 %collective-permute-start.2 = (bf16[256,1024]{1,0:T(8,128)(2,1)}, bf16[256,1024]{1,0:T(8,128)(2,1)S(1)}, u32[]{:S(2)}, u32[]{:S(2)}) collective-permute-start(bf16[256,1024]{1,0:T(8,128)(2,1)} %wide.3), channel_id=1, source_target_pairs={{0,4},{2,6},{4,8},{6,10},{8,12},{10,14},{12,16},{14,18},{16,20},{1... | collective-permute-start | bytes 1572872 | tf_op jit(solution)/shard_map/ppermute | solution.py:313
  1.2 4.3 %copy-start.1 = (bf16[256,1024]{1,0:T(8,128)(2,1)S(1)}, bf16[256,1024]{1,0:T(8,128)(2,1)}, u32[]{:S(2)}) copy-start(bf16[256,1024]{1,0:T(8,128)(2,1)} %wide.3) | copy-start | bytes 1572868
  4.3 4.3 %collective-permute-start = (bf16[400,128]{1,0:T(8,128)(2,1)}, bf16[400,128]{1,0:T(8,128)(2,1)S(1)}, u32[]{:S(2)}, u32[]{:S(2)}) collective-permute-start(bf16[400,128]{1,0:T(8,128)(2,1)} %get-tuple-element.43), channel_id=1, source_target_pairs={{0,2},{2,0},{4,6},{6,4},{8,10},{10,8},{12,14},{14,12},{16,18},{18,... | collective-permute-start | bytes 307208 | tf_op jit(solution)/shard_map/ppermute | solution.py:308
  5.6 0.9 %copy-start.3 = (bf16[64,1024]{1,0:T(8,128)(2,1)S(1)}, bf16[64,1024]{1,0:T(8,128)(2,1)}, u32[]{:S(2)}) copy-start(bf16[64,1024]{1,0:T(8,128)(2,1)} %get-tuple-element.58.ordered) | copy-start | bytes 393220
  6.8 17.5 %collective-permute-start.5 = (bf16[1280,256]{1,0:T(8,128)(2,1)S(1)}, bf16[1280,256]{1,0:T(8,128)(2,1)S(1)}, u32[]{:S(2)}, u32[]{:S(2)}) collective-permute-start(bf16[1280,256]{1,0:T(8,128)(2,1)S(1)} %get-tuple-element.45.tall), channel_id=1, source_target_pairs={{0,2},{2,0},{4,6},{6,4},{8,10},{10,8},{12,14},{14,12},{16,18},{18,... | collective-permute-start | bytes 1966088 | tf_op jit(solution)/shard_map/ppermute | solution.py:308
  7.1 1.5 %copy-start = (bf16[1,4,128,128]{3,2,1,0:T(8,128)(2,1)S(1)}, bf16[1,4,128,128]{3,2,1,0:T(8,128)(2,1)}, u32[]{:S(2)}) copy-start(bf16[1,4,128,128]{3,2,1,0:T(8,128)(2,1)} %param.13) | copy-start | bytes 393220
  7.1 1.5 %copy-start.5 = (bf16[256,128]{1,0:T(8,128)(2,1)S(1)}, bf16[256,128]{1,0:T(8,128)(2,1)}, u32[]{:S(2)}) copy-start(bf16[256,128]{1,0:T(8,128)(2,1)} %get-tuple-element.41.coords) | copy-start | bytes 196612
  7.1 1.5 %copy-start.7 = (f32[64,128]{1,0:T(8,128)S(1)}, f32[64,128]{1,0:T(8,128)}, u32[]{:S(2)}) copy-start(f32[64,128]{1,0:T(8,128)} %get-tuple-element.42.passed) | copy-start | bytes 98308
  8.6 0.7 %copy-start.6 = (s32[1,5,128]{2,0,1:T(1,128)S(1)}, s32[1,5,128]{2,0,1:T(1,128)}, u32[]{:S(2)}) copy-start(s32[1,5,128]{2,0,1:T(1,128)} %param.11) | copy-start | bytes 7684
  9.5 10.4 %collective-permute-start.1 = (bf16[384,128]{1,0:T(8,128)(2,1)S(1)}, bf16[384,128]{1,0:T(8,128)(2,1)S(1)}, u32[]{:S(2)}, u32[]{:S(2)}) collective-permute-start(bf16[384,128]{1,0:T(8,128)(2,1)S(1)} %get-tuple-element.52), channel_id=1, source_target_pairs={{0,4},{2,6},{4,0},{6,2},{8,12},{10,14},{12,8},{14,10},{16,20},{18,... | collective-permute-start | bytes 294920 | tf_op jit(solution)/shard_map/ppermute | solution.py:308
  9.6 0.9 %copy-start.4 = (bf16[64,1024]{1,0:T(8,128)(2,1)S(1)}, bf16[64,1024]{1,0:T(8,128)(2,1)}, u32[]{:S(2)}) copy-start(bf16[64,1024]{1,0:T(8,128)(2,1)} %get-tuple-element.58.ordered) | copy-start | bytes 393220
  10.5 10.2 %collective-permute-start.3 = (bf16[64,1024]{1,0:T(8,128)(2,1)S(1)}, bf16[64,1024]{1,0:T(8,128)(2,1)S(1)}, u32[]{:S(2)}, u32[]{:S(2)}) collective-permute-start(bf16[64,1024]{1,0:T(8,128)(2,1)S(1)} %copy-done.4), channel_id=1, source_target_pairs={{0,4},{2,6},{4,8},{6,10},{8,12},{10,14},{12,16},{14,18},{16,20},{1... | collective-permute-start | bytes 393224 | tf_op jit(solution)/shard_map/ppermute | solution.py:318
  20.1 0.7 %copy-start.8 = (bf16[16,128]{1,0:T(8,128)(2,1)S(1)}, bf16[16,128]{1,0:T(8,128)(2,1)}, u32[]{:S(2)}) copy-start(bf16[16,128]{1,0:T(8,128)(2,1)} %get-tuple-element.59.marks) | copy-start | bytes 12292
  20.1 3.9 %collective-permute-start.4 = (bf16[384,128]{1,0:T(8,128)(2,1)S(1)}, bf16[384,128]{1,0:T(8,128)(2,1)S(1)}, u32[]{:S(2)}, u32[]{:S(2)}) collective-permute-start(bf16[384,128]{1,0:T(8,128)(2,1)S(1)} %get-tuple-element.64), channel_id=1, source_target_pairs={{0,8},{2,10},{4,12},{6,14},{8,0},{10,2},{12,4},{14,6},{16,24},{18,... | collective-permute-start | bytes 294920 | tf_op jit(solution)/shard_map/ppermute | solution.py:308
  24.3 10.6 %collective-permute-start.6 = (bf16[384,128]{1,0:T(8,128)(2,1)S(1)}, bf16[384,128]{1,0:T(8,128)(2,1)S(1)}, u32[]{:S(2)}, u32[]{:S(2)}) collective-permute-start(bf16[384,128]{1,0:T(8,128)(2,1)S(1)} %get-tuple-element.72), channel_id=1, source_target_pairs={{0,16},{2,18},{4,20},{6,22},{8,24},{10,26},{12,28},{14,30},{16,0},... | collective-permute-start | bytes 294920 | tf_op jit(solution)/shard_map/ppermute | solution.py:308
  24.5 12.9 %collective-permute-start.8 = (bf16[64,1024]{1,0:T(8,128)(2,1)S(1)}, bf16[64,1024]{1,0:T(8,128)(2,1)S(1)}, u32[]{:S(2)}, u32[]{:S(2)}) collective-permute-start(bf16[64,1024]{1,0:T(8,128)(2,1)S(1)} %get-tuple-element.75), channel_id=1, source_target_pairs={{0,28},{2,30},{4,0},{6,2},{8,4},{10,6},{12,8},{14,10},{16,12},{18,... | collective-permute-start | bytes 393224 | tf_op jit(solution)/shard_map/ppermute | solution.py:313
  24.6 12.9 %collective-permute-start.9 = (bf16[64,1024]{1,0:T(8,128)(2,1)S(1)}, bf16[64,1024]{1,0:T(8,128)(2,1)S(1)}, u32[]{:S(2)}, u32[]{:S(2)}) collective-permute-start(bf16[64,1024]{1,0:T(8,128)(2,1)S(1)} %get-tuple-element.76), channel_id=1, source_target_pairs={{0,2},{2,0},{4,6},{6,4},{8,10},{10,8},{12,14},{14,12},{16,18},{18,... | collective-permute-start | bytes 393224 | tf_op jit(solution)/shard_map/ppermute | solution.py:308
  35.0 1.6 %copy-start.2 = (bf16[128,1024]{1,0:T(8,128)(2,1)S(1)}, bf16[128,1024]{1,0:T(8,128)(2,1)}, u32[]{:S(2)}) copy-start(bf16[128,1024]{1,0:T(8,128)(2,1)} %interp.1) | copy-start | bytes 786436
  35.0 1.6 %collective-permute-start.7 = (bf16[320,128]{1,0:T(8,128)(2,1)S(1)}, bf16[320,128]{1,0:T(8,128)(2,1)S(1)}, u32[]{:S(2)}, u32[]{:S(2)}) collective-permute-start(bf16[320,128]{1,0:T(8,128)(2,1)S(1)} %join_level.7.own_top), channel_id=1, source_target_pairs={{0,1},{1,0},{2,3},{3,2},{4,5},{5,4},{6,7},{7,6},{8,9},{9,8},{10,11... | collective-permute-start | bytes 245768 | tf_op jit(solution)/shard_map/ppermute | solution.py:313

commit v2 on v1

--- a/solution.py
+++ b/solution.py
@@ -362,18 +362,10 @@
         [points, ordered],
         name="turn",
     )
-    (near,) = call(
-        self_kernel,
-        [block_sums],
-        [tall, norms, points, ordered],
-        name="self_tile",
-    )
-
     history, terms = [], []
     for level in range(levels):
         received = swapped(message, "leaf", 1 << level)
         if level == 0:
-            received, near = lax.optimization_barrier((received, near))
             first_received = received
             side_tall = swapped(tall, "leaf", 1)
         if level == 1:
@@ -431,7 +423,13 @@
         if not last:
             coords, message, passed = results
         if level == 0:
-            sent = lax.optimization_barrier((ordered, results[-1]))[0]
+            (near,) = call(
+                self_kernel,
+                [block_sums],
+                [tall, norms, points, lax.optimization_barrier((ordered, results[-1]))[0]],
+                name="self_tile",
+            )
+            sent = lax.optimization_barrier((ordered, near))[0]
             back_ordered = shifted(sent, "leaf", 2)
     own_top = results[0]
     tops = [rotated(own_top, "grp", turn) for turn in range(1, groups)]

time: 38.5 us -> 37.3 us (0.969)
  the two profiles are of different devices: /device:TPU:25 before, /device:TPU:0 now
where the time goes in v2:
time: 37.3 us; the launch traced here: 37 us
  starting transfers between devices  16.9 us (45%)
  Pallas kernels  9.75 us (26%)
  waiting for transfers between devices  9.05 us (24%)
  local copies, waits for them, and re-layouts  1.13 us (3%)
    pallas_call x14, Pallas kernels, call(): pl.pallas_call(kernel, out_shape=outs, in_specs=[rest] * len(args), out_s...  9.75 us
    ppermute x6, waiting for transfers between devices, swapped(): lax.ppermute(value, axis, [(place, place ^ flip) for place in range(count)])  8.72 us
    ppermute x6, starting transfers between devices, swapped(): lax.ppermute(value, axis, [(place, place ^ flip) for place in range(count)])  8.6 us
    ppermute x3, starting transfers between devices, rotated(): lax.ppermute(value, axis, [(place, (place + turn) % count) for place in r...  5.9 us
    ppermute x1, starting transfers between devices, shifted(): lax.ppermute(value, axis, [(place, place + step) for place in places if p...  2.41 us
    unnamed x18, local copies, waits for them, and re-layouts  1.13 us
  transfers between devices with their start and end apart: 10, of which 5 were waited for; matrix products, arithmetic and copies ran while one was open for 0% of the time, Pallas kernels for 24%

profile of v2, /device:TPU:0, one launch (start us, length us, event | category | flops | bytes accessed | tf_op | source)
XLA Modules:
  0.0 37.0 jit_solution(12880950654967279225)
XLA Ops:
  0.0 3.0 %collective-permute-start.2 = (bf16[256,1024]{1,0:T(8,128)(2,1)}, bf16[256,1024]{1,0:T(8,128)(2,1)S(1)}, u32[]{:S(2)}, u32[]{:S(2)}) collective-permute-start(bf16[256,1024]{1,0:T(8,128)(2,1)} %wide.3), channel_id=1, source_target_pairs={{0,4},{2,6},{4,8},{6,10},{8,12},{10,14},{12,16},{14,18},{16,20},{1... | collective-permute-start | bytes 1572872 | tf_op jit(solution)/shard_map/ppermute | solution.py:313
  3.0 0.0 copy-start.1
  3.0 3.0 %start.1 = (bf16[64,1024]{1,0:T(8,128)(2,1)}, bf16[256,128]{1,0:T(8,128)(2,1)}, bf16[16,128]{1,0:T(8,128)(2,1)}, bf16[400,128]{1,0:T(8,128)(2,1)}, f32[64,128]{1,0:T(8,128)}) custom-call(s32[1,1024]{1,0:T(1,128)} %bitcast.16, s32[5,1,128]{2,1,0:T(1,128)} %bitcast.11, s32[1,5]{1,0:T(1,128)} %refs_2_.1, bf16[64,1024]{1,0:T(8,128)(2,1)} %refs_3_.1, ...), custom_call_target="tpu_custom_call" | custom-call | tf_op jit(solution)/shard_map/start/pallas_call | solution.py:292
  6.0 1.6 %collective-permute-start = (bf16[400,128]{1,0:T(8,128)(2,1)}, bf16[400,128]{1,0:T(8,128)(2,1)S(1)}, u32[]{:S(2)}, u32[]{:S(2)}) collective-permute-start(bf16[400,128]{1,0:T(8,128)(2,1)} %get-tuple-element.42), channel_id=1, source_target_pairs={{0,2},{2,0},{4,6},{6,4},{8,10},{10,8},{12,14},{14,12},{16,18},{18,... | collective-permute-start | bytes 307208 | tf_op jit(solution)/shard_map/ppermute | solution.py:308
  7.5 0.0 copy-done.1
  7.6 0.0 copy-start.3
  7.6 0.9 %copy-done.3 = bf16[64,1024]{1,0:T(8,128)(2,1)S(1)} copy-done((bf16[64,1024]{1,0:T(8,128)(2,1)S(1)}, bf16[64,1024]{1,0:T(8,128)(2,1)}, u32[]{:S(2)}) %copy-start.3) | copy-done | bytes 131096
  8.5 0.0 copy-start
  8.5 0.0 copy-start.5
  8.5 0.0 copy-start.7
  8.5 0.3 turn.1
  8.8 0.0 copy-start.6
  8.8 0.6 %collective-permute-start.5 = (bf16[1280,256]{1,0:T(8,128)(2,1)S(1)}, bf16[1280,256]{1,0:T(8,128)(2,1)S(1)}, u32[]{:S(2)}, u32[]{:S(2)}) collective-permute-start(bf16[1280,256]{1,0:T(8,128)(2,1)S(1)} %get-tuple-element.53.tall), channel_id=1, source_target_pairs={{0,2},{2,0},{4,6},{6,4},{8,10},{10,8},{12,14},{14,12},{16,18},{18,... | collective-permute-start | bytes 1966088 | tf_op jit(solution)/shard_map/ppermute | solution.py:308
  9.4 1.7 %collective-permute-done.message = bf16[400,128]{1,0:T(8,128)(2,1)S(1)} collective-permute-done((bf16[400,128]{1,0:T(8,128)(2,1)}, bf16[400,128]{1,0:T(8,128)(2,1)S(1)}, u32[]{:S(2)}, u32[]{:S(2)}) %collective-permute-start) | collective-permute-done | bytes 102432 | tf_op jit(solution)/shard_map/ppermute | solution.py:308
  11.1 0.0 copy-done
  11.1 0.0 copy-done.5
  11.1 0.0 copy-done.7
  11.1 0.0 copy-done.6
  11.2 0.2 join_level.4
  11.4 1.6 %collective-permute-start.1 = (bf16[384,128]{1,0:T(8,128)(2,1)S(1)}, bf16[384,128]{1,0:T(8,128)(2,1)S(1)}, u32[]{:S(2)}, u32[]{:S(2)}) collective-permute-start(bf16[384,128]{1,0:T(8,128)(2,1)S(1)} %get-tuple-element.47), channel_id=1, source_target_pairs={{0,4},{2,6},{4,0},{6,2},{8,12},{10,14},{12,8},{14,10},{16,20},{18,... | collective-permute-start | bytes 294920 | tf_op jit(solution)/shard_map/ppermute | solution.py:308
  13.0 0.0 copy-start.4
  13.0 0.8 %sibling_term.2 = (f32[64,128]{1,0:T(8,128)S(1)}, f32[128,128]{1,0:T(8,128)S(1)}) custom-call(bf16[4,128,128]{2,1,0:T(8,128)(2,1)S(1)} %bitcast.5, bf16[256,128]{1,0:T(8,128)(2,1)S(1)} %copy-done.5, bf16[400,128]{1,0:T(8,128)(2,1)S(1)} %collective-permute-done.message), custom_call_target="tpu_custom_call" | custom-call | flops 33554432 | bytes 397312 | tf_op jit(solution)/shard_map/sibling_term/pallas_call | solution.py:292
  13.8 0.1 copy-done.4
  13.9 1.4 %self_tile.1.near = f32[64,1024]{1,0:T(8,128)S(1)} custom-call(bf16[1280,256]{1,0:T(8,128)(2,1)S(1)} %get-tuple-element.53.tall, f32[1024,128]{1,0:T(8,128)S(1)} %get-tuple-element.54.norms, bf16[256,1024]{1,0:T(8,128)(2,1)S(1)} %copy-done.1, bf16[64,1024]{1,0:T(8,128)(2,1)S(1)} %copy-done.4), custom_call_target="tpu_custom_call" | custom-call | tf_op jit(solution)/shard_map/self_tile/pallas_call | solution.py:292
  15.3 2.4 %collective-permute-start.3 = (bf16[64,1024]{1,0:T(8,128)(2,1)S(1)}, bf16[64,1024]{1,0:T(8,128)(2,1)S(1)}, u32[]{:S(2)}, u32[]{:S(2)}) collective-permute-start(bf16[64,1024]{1,0:T(8,128)(2,1)S(1)} %copy-done.4), channel_id=1, source_target_pairs={{0,4},{2,6},{4,8},{6,10},{8,12},{10,14},{12,16},{14,18},{16,20},{1... | collective-permute-start | bytes 393224 | tf_op jit(solution)/shard_map/ppermute | solution.py:318
  17.7 2.5 %collective-permute-done.1.message = bf16[384,128]{1,0:T(8,128)(2,1)S(1)} collective-permute-done((bf16[384,128]{1,0:T(8,128)(2,1)S(1)}, bf16[384,128]{1,0:T(8,128)(2,1)S(1)}, u32[]{:S(2)}, u32[]{:S(2)}) %collective-permute-start.1) | collective-permute-done | bytes 98336 | tf_op jit(solution)/shard_map/ppermute | solution.py:308
  20.2 0.0 collective-permute-done.2.back_wide
  20.2 0.2 join_level.5
  20.5 0.0 copy-start.8
  20.5 0.1 collective-permute-start.4
  20.6 0.5 %sibling_term.3.refs_5_ = f32[64,128]{1,0:T(8,128)S(1)} custom-call(bf16[4,128,128]{2,1,0:T(8,128)(2,1)S(1)} %bitcast.7, bf16[256,128]{1,0:T(8,128)(2,1)S(1)} %get-tuple-element.43.coords, bf16[384,128]{1,0:T(8,128)(2,1)S(1)} %collective-permute-done.1.message), custom_call_target="tpu_custom_call" | custom-call | flops 33554432 | bytes 327680 | tf_op jit(solution)/shard_map/sibling_term/pallas_call | solution.py:292
  21.0 0.0 collective-permute-done.3.back_ordered
  21.0 0.1 copy-done.8
  21.1 0.2 back_tile.1
  21.3 4.0 %collective-permute-done.4.message.refs_1_ = bf16[384,128]{1,0:T(8,128)(2,1)S(1)} collective-permute-done((bf16[384,128]{1,0:T(8,128)(2,1)S(1)}, bf16[384,128]{1,0:T(8,128)(2,1)S(1)}, u32[]{:S(2)}, u32[]{:S(2)}) %collective-permute-start.4) | collective-permute-done | bytes 98336 | tf_op jit(solution)/shard_map/ppermute | solution.py:308
  25.3 0.2 join_level.6
  25.5 2.4 %collective-permute-start.6 = (bf16[384,128]{1,0:T(8,128)(2,1)S(1)}, bf16[384,128]{1,0:T(8,128)(2,1)S(1)}, u32[]{:S(2)}, u32[]{:S(2)}) collective-permute-start(bf16[384,128]{1,0:T(8,128)(2,1)S(1)} %get-tuple-element.70), channel_id=1, source_target_pairs={{0,16},{2,18},{4,20},{6,22},{8,24},{10,26},{12,28},{14,30},{16,0},... | collective-permute-start | bytes 294920 | tf_op jit(solution)/shard_map/ppermute | solution.py:308
  27.9 0.0 collective-permute-done.5.side_tall
  27.9 0.2 pair_tile.1
  28.1 2.9 %collective-permute-start.8 = (bf16[64,1024]{1,0:T(8,128)(2,1)S(1)}, bf16[64,1024]{1,0:T(8,128)(2,1)S(1)}, u32[]{:S(2)}, u32[]{:S(2)}) collective-permute-start(bf16[64,1024]{1,0:T(8,128)(2,1)S(1)} %get-tuple-element.73), channel_id=1, source_target_pairs={{0,28},{2,30},{4,0},{6,2},{8,4},{10,6},{12,8},{14,10},{16,12},{18,... | collective-permute-start | bytes 393224 | tf_op jit(solution)/shard_map/ppermute | solution.py:313
  30.9 2.4 %collective-permute-start.9 = (bf16[64,1024]{1,0:T(8,128)(2,1)S(1)}, bf16[64,1024]{1,0:T(8,128)(2,1)S(1)}, u32[]{:S(2)}, u32[]{:S(2)}) collective-permute-start(bf16[64,1024]{1,0:T(8,128)(2,1)S(1)} %get-tuple-element.74), channel_id=1, source_target_pairs={{0,2},{2,0},{4,6},{6,4},{8,10},{10,8},{12,14},{14,12},{16,18},{18,... | collective-permute-start | bytes 393224 | tf_op jit(solution)/shard_map/ppermute | solution.py:308
  33.3 0.0 collective-permute-done.6.message.refs_3_
  33.3 0.2 join_level.7.own_top
  33.5 0.0 copy-start.2
  33.5 0.1 collective-permute-start.7
  33.6 0.9 %last_terms.1.potential = f32[64,128]{1,0:T(8,128)S(1)} custom-call(bf16[4,128,128]{2,1,0:T(8,128)(2,1)S(1)} %bitcast.10, bf16[256,128]{1,0:T(8,128)(2,1)S(1)} %get-tuple-element.49.coords.refs_0_, bf16[384,128]{1,0:T(8,128)(2,1)S(1)} %collective-permute-done.4.message.refs_1_, bf16[256,128]{1,0:T(8,128)(2,1)S(1)} %get-tuple-element.63.coords.refs_2_, ...), custom_call_target="tpu_custom_call" | custom-call | flops 33554432 | bytes 557056 | tf_op jit(solution)/shard_map/last_terms/pallas_call | solution.py:292
  34.5 0.3 collective-permute-done.7.refs_0_
  34.9 0.0 copy-done.2
  34.9 0.9 %far_field.1.here = f32[64,1024]{1,0:T(8,128)S(1)} custom-call(bf16[320,128]{1,0:T(8,128)(2,1)S(1)} %join_level.7.own_top, f32[64,128]{1,0:T(8,128)S(1)} %last_terms.1.potential, f32[128,128]{1,0:T(8,128)S(1)} %get-tuple-element.71.product, bf16[128,1024]{1,0:T(8,128)(2,1)S(1)} %copy-done.2, f32[64,1024]{1,0:T(8,128)S(1)} %get-tuple-element.72.near, ...), custom_call_target="tpu_custom_call" | custom-call | flops 33554432 | bytes 1048576 | tf_op jit(solution)/shard_map/far_field/pallas_call | solution.py:292
  35.7 0.0 collective-permute-done.8.back
  35.7 0.5 %collective-permute-done.9.side = bf16[64,1024]{1,0:T(8,128)(2,1)S(1)} collective-permute-done((bf16[64,1024]{1,0:T(8,128)(2,1)S(1)}, bf16[64,1024]{1,0:T(8,128)(2,1)S(1)}, u32[]{:S(2)}, u32[]{:S(2)}) %collective-permute-start.9) | collective-permute-done | bytes 131104 | tf_op jit(solution)/shard_map/ppermute | solution.py:308
  36.3 0.7 %total.1 = f32[64,1024]{1,0:T(8,128)} custom-call(f32[64,1024]{1,0:T(8,128)S(1)} %far_field.1.here, bf16[64,1024]{1,0:T(8,128)(2,1)S(1)} %collective-permute-done.8.back, bf16[64,1024]{1,0:T(8,128)(2,1)S(1)} %collective-permute-done.9.side), custom_call_target="tpu_custom_call" | custom-call | flops 131072 | bytes 786432 | tf_op jit(solution)/shard_map/total/pallas_call | solution.py:292
Async XLA Ops:
  0.0 20.2 %collective-permute-start.2 = (bf16[256,1024]{1,0:T(8,128)(2,1)}, bf16[256,1024]{1,0:T(8,128)(2,1)S(1)}, u32[]{:S(2)}, u32[]{:S(2)}) collective-permute-start(bf16[256,1024]{1,0:T(8,128)(2,1)} %wide.3), channel_id=1, source_target_pairs={{0,4},{2,6},{4,8},{6,10},{8,12},{10,14},{12,16},{14,18},{16,20},{1... | collective-permute-start | bytes 1572872 | tf_op jit(solution)/shard_map/ppermute | solution.py:313
  3.0 4.6 %copy-start.1 = (bf16[256,1024]{1,0:T(8,128)(2,1)S(1)}, bf16[256,1024]{1,0:T(8,128)(2,1)}, u32[]{:S(2)}) copy-start(bf16[256,1024]{1,0:T(8,128)(2,1)} %wide.3) | copy-start | bytes 1572868
  6.0 5.1 %collective-permute-start = (bf16[400,128]{1,0:T(8,128)(2,1)}, bf16[400,128]{1,0:T(8,128)(2,1)S(1)}, u32[]{:S(2)}, u32[]{:S(2)}) collective-permute-start(bf16[400,128]{1,0:T(8,128)(2,1)} %get-tuple-element.42), channel_id=1, source_target_pairs={{0,2},{2,0},{4,6},{6,4},{8,10},{10,8},{12,14},{14,12},{16,18},{18,... | collective-permute-start | bytes 307208 | tf_op jit(solution)/shard_map/ppermute | solution.py:308
  7.6 0.9 %copy-start.3 = (bf16[64,1024]{1,0:T(8,128)(2,1)S(1)}, bf16[64,1024]{1,0:T(8,128)(2,1)}, u32[]{:S(2)}) copy-start(bf16[64,1024]{1,0:T(8,128)(2,1)} %get-tuple-element.57.ordered) | copy-start | bytes 393220
  8.5 2.7 %copy-start = (bf16[1,4,128,128]{3,2,1,0:T(8,128)(2,1)S(1)}, bf16[1,4,128,128]{3,2,1,0:T(8,128)(2,1)}, u32[]{:S(2)}) copy-start(bf16[1,4,128,128]{3,2,1,0:T(8,128)(2,1)} %param.13) | copy-start | bytes 393220
  8.5 2.7 %copy-start.5 = (bf16[256,128]{1,0:T(8,128)(2,1)S(1)}, bf16[256,128]{1,0:T(8,128)(2,1)}, u32[]{:S(2)}) copy-start(bf16[256,128]{1,0:T(8,128)(2,1)} %get-tuple-element.40.coords) | copy-start | bytes 196612
  8.5 2.7 %copy-start.7 = (f32[64,128]{1,0:T(8,128)S(1)}, f32[64,128]{1,0:T(8,128)}, u32[]{:S(2)}) copy-start(f32[64,128]{1,0:T(8,128)} %get-tuple-element.41.passed) | copy-start | bytes 98308
  8.8 2.3 %copy-start.6 = (s32[1,5,128]{2,0,1:T(1,128)S(1)}, s32[1,5,128]{2,0,1:T(1,128)}, u32[]{:S(2)}) copy-start(s32[1,5,128]{2,0,1:T(1,128)} %param.11) | copy-start | bytes 7684
  8.8 19.1 %collective-permute-start.5 = (bf16[1280,256]{1,0:T(8,128)(2,1)S(1)}, bf16[1280,256]{1,0:T(8,128)(2,1)S(1)}, u32[]{:S(2)}, u32[]{:S(2)}) collective-permute-start(bf16[1280,256]{1,0:T(8,128)(2,1)S(1)} %get-tuple-element.53.tall), channel_id=1, source_target_pairs={{0,2},{2,0},{4,6},{6,4},{8,10},{10,8},{12,14},{14,12},{16,18},{18,... | collective-permute-start | bytes 1966088 | tf_op jit(solution)/shard_map/ppermute | solution.py:308
  11.4 8.9 %collective-permute-start.1 = (bf16[384,128]{1,0:T(8,128)(2,1)S(1)}, bf16[384,128]{1,0:T(8,128)(2,1)S(1)}, u32[]{:S(2)}, u32[]{:S(2)}) collective-permute-start(bf16[384,128]{1,0:T(8,128)(2,1)S(1)} %get-tuple-element.47), channel_id=1, source_target_pairs={{0,4},{2,6},{4,0},{6,2},{8,12},{10,14},{12,8},{14,10},{16,20},{18,... | collective-permute-start | bytes 294920 | tf_op jit(solution)/shard_map/ppermute | solution.py:308
  13.0 0.9 %copy-start.4 = (bf16[64,1024]{1,0:T(8,128)(2,1)S(1)}, bf16[64,1024]{1,0:T(8,128)(2,1)}, u32[]{:S(2)}) copy-start(bf16[64,1024]{1,0:T(8,128)(2,1)} %get-tuple-element.57.ordered) | copy-start | bytes 393220
  15.3 5.7 %collective-permute-start.3 = (bf16[64,1024]{1,0:T(8,128)(2,1)S(1)}, bf16[64,1024]{1,0:T(8,128)(2,1)S(1)}, u32[]{:S(2)}, u32[]{:S(2)}) collective-permute-start(bf16[64,1024]{1,0:T(8,128)(2,1)S(1)} %copy-done.4), channel_id=1, source_target_pairs={{0,4},{2,6},{4,8},{6,10},{8,12},{10,14},{12,16},{14,18},{16,20},{1... | collective-permute-start | bytes 393224 | tf_op jit(solution)/shard_map/ppermute | solution.py:318
  20.5 0.7 %copy-start.8 = (bf16[16,128]{1,0:T(8,128)(2,1)S(1)}, bf16[16,128]{1,0:T(8,128)(2,1)}, u32[]{:S(2)}) copy-start(bf16[16,128]{1,0:T(8,128)(2,1)} %get-tuple-element.58.marks) | copy-start | bytes 12292
  20.5 4.8 %collective-permute-start.4 = (bf16[384,128]{1,0:T(8,128)(2,1)S(1)}, bf16[384,128]{1,0:T(8,128)(2,1)S(1)}, u32[]{:S(2)}, u32[]{:S(2)}) collective-permute-start(bf16[384,128]{1,0:T(8,128)(2,1)S(1)} %get-tuple-element.62), channel_id=1, source_target_pairs={{0,8},{2,10},{4,12},{6,14},{8,0},{10,2},{12,4},{14,6},{16,24},{18,... | collective-permute-start | bytes 294920 | tf_op jit(solution)/shard_map/ppermute | solution.py:308
  25.5 7.8 %collective-permute-start.6 = (bf16[384,128]{1,0:T(8,128)(2,1)S(1)}, bf16[384,128]{1,0:T(8,128)(2,1)S(1)}, u32[]{:S(2)}, u32[]{:S(2)}) collective-permute-start(bf16[384,128]{1,0:T(8,128)(2,1)S(1)} %get-tuple-element.70), channel_id=1, source_target_pairs={{0,16},{2,18},{4,20},{6,22},{8,24},{10,26},{12,28},{14,30},{16,0},... | collective-permute-start | bytes 294920 | tf_op jit(solution)/shard_map/ppermute | solution.py:308
  28.1 7.7 %collective-permute-start.8 = (bf16[64,1024]{1,0:T(8,128)(2,1)S(1)}, bf16[64,1024]{1,0:T(8,128)(2,1)S(1)}, u32[]{:S(2)}, u32[]{:S(2)}) collective-permute-start(bf16[64,1024]{1,0:T(8,128)(2,1)S(1)} %get-tuple-element.73), channel_id=1, source_target_pairs={{0,28},{2,30},{4,0},{6,2},{8,4},{10,6},{12,8},{14,10},{16,12},{18,... | collective-permute-start | bytes 393224 | tf_op jit(solution)/shard_map/ppermute | solution.py:313
  30.9 5.3 %collective-permute-start.9 = (bf16[64,1024]{1,0:T(8,128)(2,1)S(1)}, bf16[64,1024]{1,0:T(8,128)(2,1)S(1)}, u32[]{:S(2)}, u32[]{:S(2)}) collective-permute-start(bf16[64,1024]{1,0:T(8,128)(2,1)S(1)} %get-tuple-element.74), channel_id=1, source_target_pairs={{0,2},{2,0},{4,6},{6,4},{8,10},{10,8},{12,14},{14,12},{16,18},{18,... | collective-permute-start | bytes 393224 | tf_op jit(solution)/shard_map/ppermute | solution.py:308
  33.5 1.4 %copy-start.2 = (bf16[128,1024]{1,0:T(8,128)(2,1)S(1)}, bf16[128,1024]{1,0:T(8,128)(2,1)}, u32[]{:S(2)}) copy-start(bf16[128,1024]{1,0:T(8,128)(2,1)} %interp.1) | copy-start | bytes 786436
  33.5 1.3 %collective-permute-start.7 = (bf16[320,128]{1,0:T(8,128)(2,1)S(1)}, bf16[320,128]{1,0:T(8,128)(2,1)S(1)}, u32[]{:S(2)}, u32[]{:S(2)}) collective-permute-start(bf16[320,128]{1,0:T(8,128)(2,1)S(1)} %join_level.7.own_top), channel_id=1, source_target_pairs={{0,1},{1,0},{2,3},{3,2},{4,5},{5,4},{6,7},{7,6},{8,9},{9,8},{10,11... | collective-permute-start | bytes 245768 | tf_op jit(solution)/shard_map/ppermute | solution.py:313

commit v3 on v2

--- a/solution.py
+++ b/solution.py
@@ -11,7 +11,6 @@
 BF16 = jnp.bfloat16
 F32 = jnp.float32
 LOG2E = 1.4426950408889634
-HIGHEST = lax.Precision.HIGHEST
 PAD = 16
 JOIN_FLOPS = 500
 VMEM_LIMIT = 40 * 1024 * 1024
@@ -37,6 +36,17 @@
     rows = left.shape[0]
     both = dot(jnp.concatenate(halves(left), axis=0), right, contract)
     return both[:rows] + both[rows:]
+
+
+def dot_parts(left, right):
+    rows, columns = left.shape[0], right.shape[1]
+    if left.dtype != BF16:
+        left = jnp.concatenate(halves(left), axis=0)
+    both = dot(left, jnp.concatenate(halves(right), axis=1))
+    total = both[:rows, :columns] + both[:rows, columns:]
+    if left.shape[0] > rows:
+        total = total + (both[rows:, :columns] + both[rows:, columns:])
+    return total
 
 
 def row_norms(points):
@@ -149,8 +159,8 @@
 
 def sibling_term(coords, message, sides):
     dimension = coords.shape[0]
-    weights = message[dimension : dimension + sides].astype(F32)
-    return dot(weights, small_kernel(message[:dimension], coords[...]), NN, HIGHEST)
+    weights = message[dimension : dimension + sides]
+    return dot_parts(weights, small_kernel(message[:dimension], coords[...]))
 
 
 def term_kernel(sides, levels, transfer, coords, message, term_ref, *product_ref):
@@ -158,7 +168,7 @@
     if product_ref:
         product = transfer[levels - 1].astype(F32)
         for level in range(levels - 2, -1, -1):
-            product = dot(product, transfer[level].astype(F32), NN, HIGHEST)
+            product = dot_split(product, transfer[level])
         product_ref[0][...] = product
 
 
@@ -262,27 +272,22 @@
         side_ref[...] = jnp.zeros_like(side_ref)
 
 
-def far_kernel(others, own_top, potential, product, interp, near, *refs):
+def far_kernel(others, own_top, potential, product, interp, near, side, *refs):
     tops, out_ref = refs[:others], refs[-1]
     sides = out_ref.shape[0]
     dimension = own_top.shape[0] - sides
     total = potential[...]
     above = None
     for top in tops:
-        part = dot(
-            top[dimension:].astype(F32),
-            small_kernel(top[:dimension], own_top[:dimension]),
-            NN,
-            HIGHEST,
-        )
+        part = dot_parts(top[dimension:], small_kernel(top[:dimension], own_top[:dimension]))
         above = part if above is None else above + part
     if above is not None:
-        total = total + dot(above, product[...], NN, HIGHEST)
-    out_ref[...] = near[...] + dot_split(total, interp[...])
-
-
-def total_kernel(here, back, side, out_ref):
-    out_ref[...] = here[...] + (back[...].astype(F32) + side[...].astype(F32))
+        total = total + dot_parts(above, product[...])
+    out_ref[...] = (near[...] + side[...].astype(F32)) + dot_split(total, interp[...])
+
+
+def total_kernel(here, back, out_ref):
+    out_ref[...] = here[...] + back[...].astype(F32)
 
 
 def call(kernel, outs, args, scratch=(), anywhere=False, flops=0, exps=0, name=None):
@@ -444,11 +449,11 @@
     (here,) = call(
         functools.partial(far_kernel, len(tops)),
         [block_sums],
-        [own_top, potential, product, leaf_interp, near] + tops,
+        [own_top, potential, product, leaf_interp, near, side] + tops,
         flops=4 * sides * rows * count,
         name="far_field",
     )
-    (out,) = call(total_kernel, [block_sums], [here, back, side], flops=2 * sides * rows, name="total")
+    (out,) = call(total_kernel, [block_sums], [here, back], flops=2 * sides * rows, name="total")
     return out
 
 

time: 37.3 us -> 36.9 us (0.989)
  starting transfers between devices: 16.9 us -> 13.3 us
  Pallas kernels: 9.75 us -> 11.3 us
  waiting for transfers between devices: 9.05 us -> 10.4 us
    ppermute x6, starting transfers between devices: 8.6 us -> 6.28 us  [swapped(): lax.ppermute(value, axis, [(place, place ^ flip) for place in range(count)])]
    ppermute x6, waiting for transfers between devices: 8.72 us -> 10.4 us  [swapped(): lax.ppermute(value, axis, [(place, place ^ flip) for place in range(count)])]
    pallas_call x14, Pallas kernels: 9.75 us -> 11.3 us  [call(): pl.pallas_call(kernel, out_shape=outs, in_specs=[rest] * len(args), out_s...]
    ppermute x3, starting transfers between devices: 5.9 us -> 4.57 us  [rotated(): lax.ppermute(value, axis, [(place, (place + turn) % count) for place in r...]
  transfers between devices with their start and end apart: 10 -> 10, of which waited for: 5 -> 5; matrix products, arithmetic and copies ran while one was open for 0% -> 0% of each run, Pallas kernels for 24% -> 29%
where the time goes in v3:
time: 36.9 us; the launch traced here: 36.4 us
  starting transfers between devices  13.3 us (36%)
  Pallas kernels  11.3 us (31%)
  waiting for transfers between devices  10.4 us (28%)
  local copies, waits for them, and re-layouts  1.31 us (4%)
    pallas_call x14, Pallas kernels, call(): pl.pallas_call(kernel, out_shape=outs, in_specs=[rest] * len(args), out_s...  11.3 us
    ppermute x6, waiting for transfers between devices, swapped(): lax.ppermute(value, axis, [(place, place ^ flip) for place in range(count)])  10.4 us
    ppermute x6, starting transfers between devices, swapped(): lax.ppermute(value, axis, [(place, place ^ flip) for place in range(count)])  6.28 us
    ppermute x3, starting transfers between devices, rotated(): lax.ppermute(value, axis, [(place, (place + turn) % count) for place in r...  4.57 us
    ppermute x1, starting transfers between devices, shifted(): lax.ppermute(value, axis, [(place, place + step) for place in places if p...  2.41 us
    unnamed x18, local copies, waits for them, and re-layouts  1.31 us
  transfers between devices with their start and end apart: 10, of which 5 were waited for; matrix products, arithmetic and copies ran while one was open for 0% of the time, Pallas kernels for 29%

profile of v3, /device:TPU:0, one launch (start us, length us, event | category | flops | bytes accessed | tf_op | source)
XLA Modules:
  0.0 36.4 jit_solution(15229122917401407913)
XLA Ops:
  0.0 3.0 %collective-permute-start.2 = (bf16[256,1024]{1,0:T(8,128)(2,1)}, bf16[256,1024]{1,0:T(8,128)(2,1)S(1)}, u32[]{:S(2)}, u32[]{:S(2)}) collective-permute-start(bf16[256,1024]{1,0:T(8,128)(2,1)} %wide.3), channel_id=1, source_target_pairs={{0,4},{2,6},{4,8},{6,10},{8,12},{10,14},{12,16},{14,18},{16,20},{1... | collective-permute-start | bytes 1572872 | tf_op jit(solution)/shard_map/ppermute | solution.py:318
  3.0 0.0 copy-start.1
  3.0 3.0 %start.1 = (bf16[64,1024]{1,0:T(8,128)(2,1)}, bf16[256,128]{1,0:T(8,128)(2,1)}, bf16[16,128]{1,0:T(8,128)(2,1)}, bf16[400,128]{1,0:T(8,128)(2,1)}, f32[64,128]{1,0:T(8,128)}) custom-call(s32[1,1024]{1,0:T(1,128)} %bitcast.16, s32[5,1,128]{2,1,0:T(1,128)} %bitcast.11, s32[1,5]{1,0:T(1,128)} %refs_2_.1, bf16[64,1024]{1,0:T(8,128)(2,1)} %refs_3_.1, ...), custom_call_target="tpu_custom_call" | custom-call | tf_op jit(solution)/shard_map/start/pallas_call | solution.py:297
  6.0 1.6 %collective-permute-start = (bf16[400,128]{1,0:T(8,128)(2,1)}, bf16[400,128]{1,0:T(8,128)(2,1)S(1)}, u32[]{:S(2)}, u32[]{:S(2)}) collective-permute-start(bf16[400,128]{1,0:T(8,128)(2,1)} %get-tuple-element.42), channel_id=1, source_target_pairs={{0,2},{2,0},{4,6},{6,4},{8,10},{10,8},{12,14},{14,12},{16,18},{18,... | collective-permute-start | bytes 307208 | tf_op jit(solution)/shard_map/ppermute | solution.py:313
  7.5 0.0 copy-done.1
  7.6 0.0 copy-start.3
  7.6 0.9 %copy-done.3 = bf16[64,1024]{1,0:T(8,128)(2,1)S(1)} copy-done((bf16[64,1024]{1,0:T(8,128)(2,1)S(1)}, bf16[64,1024]{1,0:T(8,128)(2,1)}, u32[]{:S(2)}) %copy-start.3) | copy-done | bytes 131096
  8.5 0.0 copy-start
  8.5 0.0 copy-start.5
  8.5 0.0 copy-start.7
  8.5 0.3 turn.1
  8.8 0.0 copy-start.6
  8.8 0.6 %collective-permute-start.5 = (bf16[1280,256]{1,0:T(8,128)(2,1)S(1)}, bf16[1280,256]{1,0:T(8,128)(2,1)S(1)}, u32[]{:S(2)}, u32[]{:S(2)}) collective-permute-start(bf16[1280,256]{1,0:T(8,128)(2,1)S(1)} %get-tuple-element.53.tall), channel_id=1, source_target_pairs={{0,2},{2,0},{4,6},{6,4},{8,10},{10,8},{12,14},{14,12},{16,18},{18,... | collective-permute-start | bytes 1966088 | tf_op jit(solution)/shard_map/ppermute | solution.py:313
  9.4 1.7 %collective-permute-done.message = bf16[400,128]{1,0:T(8,128)(2,1)S(1)} collective-permute-done((bf16[400,128]{1,0:T(8,128)(2,1)}, bf16[400,128]{1,0:T(8,128)(2,1)S(1)}, u32[]{:S(2)}, u32[]{:S(2)}) %collective-permute-start) | collective-permute-done | bytes 102432 | tf_op jit(solution)/shard_map/ppermute | solution.py:313
  11.1 0.0 copy-done
  11.1 0.0 copy-done.5
  11.1 0.0 copy-done.7
  11.1 0.0 copy-done.6
  11.2 0.2 join_level.4
  11.4 1.6 %collective-permute-start.1 = (bf16[384,128]{1,0:T(8,128)(2,1)S(1)}, bf16[384,128]{1,0:T(8,128)(2,1)S(1)}, u32[]{:S(2)}, u32[]{:S(2)}) collective-permute-start(bf16[384,128]{1,0:T(8,128)(2,1)S(1)} %get-tuple-element.47), channel_id=1, source_target_pairs={{0,4},{2,6},{4,0},{6,2},{8,12},{10,14},{12,8},{14,10},{16,20},{18,... | collective-permute-start | bytes 294920 | tf_op jit(solution)/shard_map/ppermute | solution.py:313
  13.0 0.0 copy-start.4
  13.0 0.7 %sibling_term.2 = (f32[64,128]{1,0:T(8,128)S(1)}, f32[128,128]{1,0:T(8,128)S(1)}) custom-call(bf16[4,128,128]{2,1,0:T(8,128)(2,1)S(1)} %bitcast.5, bf16[256,128]{1,0:T(8,128)(2,1)S(1)} %copy-done.5, bf16[400,128]{1,0:T(8,128)(2,1)S(1)} %collective-permute-done.message), custom_call_target="tpu_custom_call" | custom-call | flops 33554432 | bytes 397312 | tf_op jit(solution)/shard_map/sibling_term/pallas_call | solution.py:297
  13.7 0.2 copy-done.4
  13.9 1.4 %self_tile.1.near = f32[64,1024]{1,0:T(8,128)S(1)} custom-call(bf16[1280,256]{1,0:T(8,128)(2,1)S(1)} %get-tuple-element.53.tall, f32[1024,128]{1,0:T(8,128)S(1)} %get-tuple-element.54.norms, bf16[256,1024]{1,0:T(8,128)(2,1)S(1)} %copy-done.1, bf16[64,1024]{1,0:T(8,128)(2,1)S(1)} %copy-done.4), custom_call_target="tpu_custom_call" | custom-call | tf_op jit(solution)/shard_map/self_tile/pallas_call | solution.py:297
  15.3 2.4 %collective-permute-start.3 = (bf16[64,1024]{1,0:T(8,128)(2,1)S(1)}, bf16[64,1024]{1,0:T(8,128)(2,1)S(1)}, u32[]{:S(2)}, u32[]{:S(2)}) collective-permute-start(bf16[64,1024]{1,0:T(8,128)(2,1)S(1)} %copy-done.4), channel_id=1, source_target_pairs={{0,4},{2,6},{4,8},{6,10},{8,12},{10,14},{12,16},{14,18},{16,20},{1... | collective-permute-start | bytes 393224 | tf_op jit(solution)/shard_map/ppermute | solution.py:323
  17.7 2.5 %collective-permute-done.1.message = bf16[384,128]{1,0:T(8,128)(2,1)S(1)} collective-permute-done((bf16[384,128]{1,0:T(8,128)(2,1)S(1)}, bf16[384,128]{1,0:T(8,128)(2,1)S(1)}, u32[]{:S(2)}, u32[]{:S(2)}) %collective-permute-start.1) | collective-permute-done | bytes 98336 | tf_op jit(solution)/shard_map/ppermute | solution.py:313
  20.2 0.0 collective-permute-done.2.back_wide
  20.2 0.2 join_level.5
  20.5 0.0 copy-start.8
  20.5 0.1 collective-permute-start.4
  20.6 0.4 %sibling_term.3.refs_5_ = f32[64,128]{1,0:T(8,128)S(1)} custom-call(bf16[4,128,128]{2,1,0:T(8,128)(2,1)S(1)} %bitcast.7, bf16[256,128]{1,0:T(8,128)(2,1)S(1)} %get-tuple-element.43.coords, bf16[384,128]{1,0:T(8,128)(2,1)S(1)} %collective-permute-done.1.message), custom_call_target="tpu_custom_call" | custom-call | flops 33554432 | bytes 327680 | tf_op jit(solution)/shard_map/sibling_term/pallas_call | solution.py:297
  21.0 0.0 collective-permute-done.3.back_ordered
  21.0 0.2 copy-done.8
  21.1 0.2 back_tile.1
  21.3 4.0 %collective-permute-done.4.message.refs_1_ = bf16[384,128]{1,0:T(8,128)(2,1)S(1)} collective-permute-done((bf16[384,128]{1,0:T(8,128)(2,1)S(1)}, bf16[384,128]{1,0:T(8,128)(2,1)S(1)}, u32[]{:S(2)}, u32[]{:S(2)}) %collective-permute-start.4) | collective-permute-done | bytes 98336 | tf_op jit(solution)/shard_map/ppermute | solution.py:313
  25.3 0.2 join_level.6
  25.5 2.4 %collective-permute-start.6 = (bf16[384,128]{1,0:T(8,128)(2,1)S(1)}, bf16[384,128]{1,0:T(8,128)(2,1)S(1)}, u32[]{:S(2)}, u32[]{:S(2)}) collective-permute-start(bf16[384,128]{1,0:T(8,128)(2,1)S(1)} %get-tuple-element.70), channel_id=1, source_target_pairs={{0,16},{2,18},{4,20},{6,22},{8,24},{10,26},{12,28},{14,30},{16,0},... | collective-permute-start | bytes 294920 | tf_op jit(solution)/shard_map/ppermute | solution.py:313
  27.9 0.0 collective-permute-done.5.side_tall
  27.9 2.0 %pair_tile.1 = (f32[64,1024]{1,0:T(8,128)S(1)}, bf16[64,1024]{1,0:T(8,128)(2,1)S(1)}, bf16[64,1024]{1,0:T(8,128)(2,1)S(1)}) custom-call(bf16[256,1024]{1,0:T(8,128)(2,1)S(1)} %copy-done.1, bf16[64,1024]{1,0:T(8,128)(2,1)S(1)} %copy-done.4, bf16[1280,256]{1,0:T(8,128)(2,1)S(1)} %collective-permute-done.5.side_tall, ...), custom_call_target="tpu_custom_call" | custom-call | flops 805306368 | bytes 3121152 | tf_op jit(solution)/shard_map/pair_tile/pallas_call | solution.py:297
  29.9 0.1 collective-permute-start.7
  30.0 1.5 %collective-permute-start.9 = (bf16[64,1024]{1,0:T(8,128)(2,1)S(1)}, bf16[64,1024]{1,0:T(8,128)(2,1)S(1)}, u32[]{:S(2)}, u32[]{:S(2)}) collective-permute-start(bf16[64,1024]{1,0:T(8,128)(2,1)S(1)} %get-tuple-element.74), channel_id=1, source_target_pairs={{0,28},{2,30},{4,0},{6,2},{8,4},{10,6},{12,8},{14,10},{16,12},{18,... | collective-permute-start | bytes 393224 | tf_op jit(solution)/shard_map/ppermute | solution.py:318
  31.5 1.0 %collective-permute-done.6.message.refs_3_ = bf16[384,128]{1,0:T(8,128)(2,1)S(1)} collective-permute-done((bf16[384,128]{1,0:T(8,128)(2,1)S(1)}, bf16[384,128]{1,0:T(8,128)(2,1)S(1)}, u32[]{:S(2)}, u32[]{:S(2)}) %collective-permute-start.6) | collective-permute-done | bytes 98336 | tf_op jit(solution)/shard_map/ppermute | solution.py:313
  32.5 0.2 join_level.7.own_top
  32.7 0.0 copy-start.2
  32.7 0.1 collective-permute-start.8
  32.8 1.0 %last_terms.1.potential = f32[64,128]{1,0:T(8,128)S(1)} custom-call(bf16[4,128,128]{2,1,0:T(8,128)(2,1)S(1)} %bitcast.10, bf16[256,128]{1,0:T(8,128)(2,1)S(1)} %get-tuple-element.49.coords.refs_0_, bf16[384,128]{1,0:T(8,128)(2,1)S(1)} %collective-permute-done.4.message.refs_1_, bf16[256,128]{1,0:T(8,128)(2,1)S(1)} %get-tuple-element.63.coords.refs_2_, ...), custom_call_target="tpu_custom_call" | custom-call | flops 33554432 | bytes 557056 | tf_op jit(solution)/shard_map/last_terms/pallas_call | solution.py:297
  33.8 1.1 %collective-permute-done.7.side = bf16[64,1024]{1,0:T(8,128)(2,1)S(1)} collective-permute-done((bf16[64,1024]{1,0:T(8,128)(2,1)S(1)}, bf16[64,1024]{1,0:T(8,128)(2,1)S(1)}, u32[]{:S(2)}, u32[]{:S(2)}) %collective-permute-start.7) | collective-permute-done | bytes 131104 | tf_op jit(solution)/shard_map/ppermute | solution.py:313
  34.9 0.0 collective-permute-done.8.refs_0_
  34.9 0.0 copy-done.2
  34.9 0.7 %far_field.1.here = f32[64,1024]{1,0:T(8,128)S(1)} custom-call(bf16[320,128]{1,0:T(8,128)(2,1)S(1)} %join_level.7.own_top, f32[64,128]{1,0:T(8,128)S(1)} %last_terms.1.potential, f32[128,128]{1,0:T(8,128)S(1)} %get-tuple-element.71.product, bf16[128,1024]{1,0:T(8,128)(2,1)S(1)} %copy-done.2, f32[64,1024]{1,0:T(8,128)S(1)} %get-tuple-element.72.near, ...), custom_call_target="tpu_custom_call" | custom-call | flops 33554432 | bytes 1179648 | tf_op jit(solution)/shard_map/far_field/pallas_call | solution.py:297
  35.7 0.0 collective-permute-done.9.back
  35.7 0.7 %total.1 = f32[64,1024]{1,0:T(8,128)} custom-call(f32[64,1024]{1,0:T(8,128)S(1)} %far_field.1.here, bf16[64,1024]{1,0:T(8,128)(2,1)S(1)} %collective-permute-done.9.back), custom_call_target="tpu_custom_call" | custom-call | flops 131072 | bytes 655360 | tf_op jit(solution)/shard_map/total/pallas_call | solution.py:297
Async XLA Ops:
  0.0 20.2 %collective-permute-start.2 = (bf16[256,1024]{1,0:T(8,128)(2,1)}, bf16[256,1024]{1,0:T(8,128)(2,1)S(1)}, u32[]{:S(2)}, u32[]{:S(2)}) collective-permute-start(bf16[256,1024]{1,0:T(8,128)(2,1)} %wide.3), channel_id=1, source_target_pairs={{0,4},{2,6},{4,8},{6,10},{8,12},{10,14},{12,16},{14,18},{16,20},{1... | collective-permute-start | bytes 1572872 | tf_op jit(solution)/shard_map/ppermute | solution.py:318
  3.0 4.6 %copy-start.1 = (bf16[256,1024]{1,0:T(8,128)(2,1)S(1)}, bf16[256,1024]{1,0:T(8,128)(2,1)}, u32[]{:S(2)}) copy-start(bf16[256,1024]{1,0:T(8,128)(2,1)} %wide.3) | copy-start | bytes 1572868
  6.0 5.1 %collective-permute-start = (bf16[400,128]{1,0:T(8,128)(2,1)}, bf16[400,128]{1,0:T(8,128)(2,1)S(1)}, u32[]{:S(2)}, u32[]{:S(2)}) collective-permute-start(bf16[400,128]{1,0:T(8,128)(2,1)} %get-tuple-element.42), channel_id=1, source_target_pairs={{0,2},{2,0},{4,6},{6,4},{8,10},{10,8},{12,14},{14,12},{16,18},{18,... | collective-permute-start | bytes 307208 | tf_op jit(solution)/shard_map/ppermute | solution.py:313
  7.6 0.9 %copy-start.3 = (bf16[64,1024]{1,0:T(8,128)(2,1)S(1)}, bf16[64,1024]{1,0:T(8,128)(2,1)}, u32[]{:S(2)}) copy-start(bf16[64,1024]{1,0:T(8,128)(2,1)} %get-tuple-element.57.ordered) | copy-start | bytes 393220
  8.5 2.7 %copy-start = (bf16[1,4,128,128]{3,2,1,0:T(8,128)(2,1)S(1)}, bf16[1,4,128,128]{3,2,1,0:T(8,128)(2,1)}, u32[]{:S(2)}) copy-start(bf16[1,4,128,128]{3,2,1,0:T(8,128)(2,1)} %param.13) | copy-start | bytes 393220
  8.5 2.7 %copy-start.5 = (bf16[256,128]{1,0:T(8,128)(2,1)S(1)}, bf16[256,128]{1,0:T(8,128)(2,1)}, u32[]{:S(2)}) copy-start(bf16[256,128]{1,0:T(8,128)(2,1)} %get-tuple-element.40.coords) | copy-start | bytes 196612
  8.5 2.7 %copy-start.7 = (f32[64,128]{1,0:T(8,128)S(1)}, f32[64,128]{1,0:T(8,128)}, u32[]{:S(2)}) copy-start(f32[64,128]{1,0:T(8,128)} %get-tuple-element.41.passed) | copy-start | bytes 98308
  8.8 2.3 %copy-start.6 = (s32[1,5,128]{2,0,1:T(1,128)S(1)}, s32[1,5,128]{2,0,1:T(1,128)}, u32[]{:S(2)}) copy-start(s32[1,5,128]{2,0,1:T(1,128)} %param.11) | copy-start | bytes 7684
  8.8 19.1 %collective-permute-start.5 = (bf16[1280,256]{1,0:T(8,128)(2,1)S(1)}, bf16[1280,256]{1,0:T(8,128)(2,1)S(1)}, u32[]{:S(2)}, u32[]{:S(2)}) collective-permute-start(bf16[1280,256]{1,0:T(8,128)(2,1)S(1)} %get-tuple-element.53.tall), channel_id=1, source_target_pairs={{0,2},{2,0},{4,6},{6,4},{8,10},{10,8},{12,14},{14,12},{16,18},{18,... | collective-permute-start | bytes 1966088 | tf_op jit(solution)/shard_map/ppermute | solution.py:313
  11.4 8.9 %collective-permute-start.1 = (bf16[384,128]{1,0:T(8,128)(2,1)S(1)}, bf16[384,128]{1,0:T(8,128)(2,1)S(1)}, u32[]{:S(2)}, u32[]{:S(2)}) collective-permute-start(bf16[384,128]{1,0:T(8,128)(2,1)S(1)} %get-tuple-element.47), channel_id=1, source_target_pairs={{0,4},{2,6},{4,0},{6,2},{8,12},{10,14},{12,8},{14,10},{16,20},{18,... | collective-permute-start | bytes 294920 | tf_op jit(solution)/shard_map/ppermute | solution.py:313
  13.0 0.9 %copy-start.4 = (bf16[64,1024]{1,0:T(8,128)(2,1)S(1)}, bf16[64,1024]{1,0:T(8,128)(2,1)}, u32[]{:S(2)}) copy-start(bf16[64,1024]{1,0:T(8,128)(2,1)} %get-tuple-element.57.ordered) | copy-start | bytes 393220
  15.3 5.6 %collective-permute-start.3 = (bf16[64,1024]{1,0:T(8,128)(2,1)S(1)}, bf16[64,1024]{1,0:T(8,128)(2,1)S(1)}, u32[]{:S(2)}, u32[]{:S(2)}) collective-permute-start(bf16[64,1024]{1,0:T(8,128)(2,1)S(1)} %copy-done.4), channel_id=1, source_target_pairs={{0,4},{2,6},{4,8},{6,10},{8,12},{10,14},{12,16},{14,18},{16,20},{1... | collective-permute-start | bytes 393224 | tf_op jit(solution)/shard_map/ppermute | solution.py:323
  20.5 0.7 %copy-start.8 = (bf16[16,128]{1,0:T(8,128)(2,1)S(1)}, bf16[16,128]{1,0:T(8,128)(2,1)}, u32[]{:S(2)}) copy-start(bf16[16,128]{1,0:T(8,128)(2,1)} %get-tuple-element.58.marks) | copy-start | bytes 12292
  20.5 4.8 %collective-permute-start.4 = (bf16[384,128]{1,0:T(8,128)(2,1)S(1)}, bf16[384,128]{1,0:T(8,128)(2,1)S(1)}, u32[]{:S(2)}, u32[]{:S(2)}) collective-permute-start(bf16[384,128]{1,0:T(8,128)(2,1)S(1)} %get-tuple-element.62), channel_id=1, source_target_pairs={{0,8},{2,10},{4,12},{6,14},{8,0},{10,2},{12,4},{14,6},{16,24},{18,... | collective-permute-start | bytes 294920 | tf_op jit(solution)/shard_map/ppermute | solution.py:313
  25.5 7.0 %collective-permute-start.6 = (bf16[384,128]{1,0:T(8,128)(2,1)S(1)}, bf16[384,128]{1,0:T(8,128)(2,1)S(1)}, u32[]{:S(2)}, u32[]{:S(2)}) collective-permute-start(bf16[384,128]{1,0:T(8,128)(2,1)S(1)} %get-tuple-element.70), channel_id=1, source_target_pairs={{0,16},{2,18},{4,20},{6,22},{8,24},{10,26},{12,28},{14,30},{16,0},... | collective-permute-start | bytes 294920 | tf_op jit(solution)/shard_map/ppermute | solution.py:313
  29.9 5.0 %collective-permute-start.7 = (bf16[64,1024]{1,0:T(8,128)(2,1)S(1)}, bf16[64,1024]{1,0:T(8,128)(2,1)S(1)}, u32[]{:S(2)}, u32[]{:S(2)}) collective-permute-start(bf16[64,1024]{1,0:T(8,128)(2,1)S(1)} %get-tuple-element.73), channel_id=1, source_target_pairs={{0,2},{2,0},{4,6},{6,4},{8,10},{10,8},{12,14},{14,12},{16,18},{18,... | collective-permute-start | bytes 393224 | tf_op jit(solution)/shard_map/ppermute | solution.py:313
  30.0 5.7 %collective-permute-start.9 = (bf16[64,1024]{1,0:T(8,128)(2,1)S(1)}, bf16[64,1024]{1,0:T(8,128)(2,1)S(1)}, u32[]{:S(2)}, u32[]{:S(2)}) collective-permute-start(bf16[64,1024]{1,0:T(8,128)(2,1)S(1)} %get-tuple-element.74), channel_id=1, source_target_pairs={{0,28},{2,30},{4,0},{6,2},{8,4},{10,6},{12,8},{14,10},{16,12},{18,... | collective-permute-start | bytes 393224 | tf_op jit(solution)/shard_map/ppermute | solution.py:318
  32.7 2.2 %copy-start.2 = (bf16[128,1024]{1,0:T(8,128)(2,1)S(1)}, bf16[128,1024]{1,0:T(8,128)(2,1)}, u32[]{:S(2)}) copy-start(bf16[128,1024]{1,0:T(8,128)(2,1)} %interp.1) | copy-start | bytes 786436
  32.7 2.2 %collective-permute-start.8 = (bf16[320,128]{1,0:T(8,128)(2,1)S(1)}, bf16[320,128]{1,0:T(8,128)(2,1)S(1)}, u32[]{:S(2)}, u32[]{:S(2)}) collective-permute-start(bf16[320,128]{1,0:T(8,128)(2,1)S(1)} %join_level.7.own_top), channel_id=1, source_target_pairs={{0,1},{1,0},{2,3},{3,2},{4,5},{5,4},{6,7},{7,6},{8,9},{9,8},{10,11... | collective-permute-start | bytes 245768 | tf_op jit(solution)/shard_map/ppermute | solution.py:318

commit v4 on v3

--- a/solution.py
+++ b/solution.py
@@ -211,9 +211,14 @@
         yield band, jnp.exp2((2.0 * scale) * inner - squares).astype(BF16)
 
 
+def gathered(tile, turned):
+    return jnp.transpose(dot(tile, turned))
+
+
 def self_kernel(tall, norms, wide, ordered, near_ref):
+    turned = jnp.transpose(ordered[...])
     for band, tile in bands(tall, norms, wide):
-        near_ref[:, band] = dot(ordered[...], tile, NT)
+        near_ref[:, band] = gathered(tile, turned)
 
 
 def back_kernel(tall, norms, ordered, back_wide, back_ordered, marks, near, near_ref, held_ref):
@@ -222,8 +227,9 @@
 
     @pl.when(used)
     def _():
+        turned = jnp.transpose(back_ordered[...])
         for band, tile in bands(tall, norms, back_wide):
-            near_ref[:, band] += dot(back_ordered[...], tile, NT)
+            near_ref[:, band] += gathered(tile, turned)
             part = dot(ordered[:, band], tile)
             if band.start:
                 held_ref[...] += part
@@ -244,8 +250,9 @@
     go_even = jnp.logical_and(odd == 0, marked(marks[...], 1))
 
     def pair(other_wide, other_ordered):
+        turned = jnp.transpose(other_ordered[...])
         for band, tile in bands(side_tall, None, other_wide):
-            side_ref[:, band] = dot(other_ordered[...], tile, NT).astype(BF16)
+            side_ref[:, band] = gathered(tile, turned).astype(BF16)
             first = rows + band.start // dimension * sides
             part = dot(side_tall[first : first + sides], tile)
             if band.start:

time: 36.9 us -> 36.9 us (level)
  starting transfers between devices: 13.3 us -> 15.1 us
  waiting for transfers between devices: 10.4 us -> 8.72 us
    ppermute x3, starting transfers between devices: 4.57 us -> 6.81 us  [rotated(): lax.ppermute(value, axis, [(place, (place + turn) % count) for place in r...]
    ppermute x6, waiting for transfers between devices: 10.4 us -> 8.19 us  [swapped(): lax.ppermute(value, axis, [(place, place ^ flip) for place in range(count)])]
    ppermute x3, waiting for transfers between devices: 0.01 us -> 0.52 us  [rotated(): lax.ppermute(value, axis, [(place, (place + turn) % count) for place in r...]
    ppermute x6, starting transfers between devices: 6.28 us -> 5.87 us  [swapped(): lax.ppermute(value, axis, [(place, place ^ flip) for place in range(count)])]
where the time goes in v4:
time: 36.9 us; the launch traced here: 36.6 us
  starting transfers between devices  15.1 us (41%)
  Pallas kernels  11.3 us (31%)
  waiting for transfers between devices  8.72 us (24%)
  local copies, waits for them, and re-layouts  1.31 us (4%)
    pallas_call x14, Pallas kernels, call(): pl.pallas_call(kernel, out_shape=outs, in_specs=[rest] * len(args), out_s...  11.3 us
    ppermute x6, waiting for transfers between devices, swapped(): lax.ppermute(value, axis, [(place, place ^ flip) for place in range(count)])  8.19 us
    ppermute x3, starting transfers between devices, rotated(): lax.ppermute(value, axis, [(place, (place + turn) % count) for place in r...  6.81 us
    ppermute x6, starting transfers between devices, swapped(): lax.ppermute(value, axis, [(place, place ^ flip) for place in range(count)])  5.87 us
    ppermute x1, starting transfers between devices, shifted(): lax.ppermute(value, axis, [(place, place + step) for place in places if p...  2.4 us
    unnamed x18, local copies, waits for them, and re-layouts  1.31 us
  transfers between devices with their start and end apart: 10, of which 5 were waited for; matrix products, arithmetic and copies ran while one was open for 0% of the time, Pallas kernels for 29%

profile of v4, /device:TPU:0, one launch (start us, length us, event | category | flops | bytes accessed | tf_op | source)
XLA Modules:
  0.0 36.6 jit_solution(11185806209084863413)
XLA Ops:
  0.0 3.0 %collective-permute-start.2 = (bf16[256,1024]{1,0:T(8,128)(2,1)}, bf16[256,1024]{1,0:T(8,128)(2,1)S(1)}, u32[]{:S(2)}, u32[]{:S(2)}) collective-permute-start(bf16[256,1024]{1,0:T(8,128)(2,1)} %wide.3), channel_id=1, source_target_pairs={{0,4},{2,6},{4,8},{6,10},{8,12},{10,14},{12,16},{14,18},{16,20},{1... | collective-permute-start | bytes 1572872 | tf_op jit(solution)/shard_map/ppermute | solution.py:325
  3.0 0.0 copy-start.1
  3.0 3.0 %start.1 = (bf16[64,1024]{1,0:T(8,128)(2,1)}, bf16[256,128]{1,0:T(8,128)(2,1)}, bf16[16,128]{1,0:T(8,128)(2,1)}, bf16[400,128]{1,0:T(8,128)(2,1)}, f32[64,128]{1,0:T(8,128)}) custom-call(s32[1,1024]{1,0:T(1,128)} %bitcast.16, s32[5,1,128]{2,1,0:T(1,128)} %bitcast.11, s32[1,5]{1,0:T(1,128)} %refs_2_.1, bf16[64,1024]{1,0:T(8,128)(2,1)} %refs_3_.1, ...), custom_call_target="tpu_custom_call" | custom-call | tf_op jit(solution)/shard_map/start/pallas_call | solution.py:304
  6.0 1.6 %collective-permute-start = (bf16[400,128]{1,0:T(8,128)(2,1)}, bf16[400,128]{1,0:T(8,128)(2,1)S(1)}, u32[]{:S(2)}, u32[]{:S(2)}) collective-permute-start(bf16[400,128]{1,0:T(8,128)(2,1)} %get-tuple-element.42), channel_id=1, source_target_pairs={{0,2},{2,0},{4,6},{6,4},{8,10},{10,8},{12,14},{14,12},{16,18},{18,... | collective-permute-start | bytes 307208 | tf_op jit(solution)/shard_map/ppermute | solution.py:320
  7.5 0.0 copy-done.1
  7.6 0.0 copy-start.3
  7.6 0.9 %copy-done.3 = bf16[64,1024]{1,0:T(8,128)(2,1)S(1)} copy-done((bf16[64,1024]{1,0:T(8,128)(2,1)S(1)}, bf16[64,1024]{1,0:T(8,128)(2,1)}, u32[]{:S(2)}) %copy-start.3) | copy-done | bytes 131096
  8.5 0.0 copy-start
  8.5 0.0 copy-start.5
  8.5 0.0 copy-start.7
  8.5 0.3 turn.1
  8.8 0.0 copy-start.6
  8.8 0.6 %collective-permute-start.5 = (bf16[1280,256]{1,0:T(8,128)(2,1)S(1)}, bf16[1280,256]{1,0:T(8,128)(2,1)S(1)}, u32[]{:S(2)}, u32[]{:S(2)}) collective-permute-start(bf16[1280,256]{1,0:T(8,128)(2,1)S(1)} %get-tuple-element.53.tall), channel_id=1, source_target_pairs={{0,2},{2,0},{4,6},{6,4},{8,10},{10,8},{12,14},{14,12},{16,18},{18,... | collective-permute-start | bytes 1966088 | tf_op jit(solution)/shard_map/ppermute | solution.py:320
  9.4 1.7 %collective-permute-done.message = bf16[400,128]{1,0:T(8,128)(2,1)S(1)} collective-permute-done((bf16[400,128]{1,0:T(8,128)(2,1)}, bf16[400,128]{1,0:T(8,128)(2,1)S(1)}, u32[]{:S(2)}, u32[]{:S(2)}) %collective-permute-start) | collective-permute-done | bytes 102432 | tf_op jit(solution)/shard_map/ppermute | solution.py:320
  11.1 0.0 copy-done
  11.1 0.0 copy-done.5
  11.1 0.0 copy-done.7
  11.1 0.0 copy-done.6
  11.2 0.2 join_level.4
  11.4 1.6 %collective-permute-start.1 = (bf16[384,128]{1,0:T(8,128)(2,1)S(1)}, bf16[384,128]{1,0:T(8,128)(2,1)S(1)}, u32[]{:S(2)}, u32[]{:S(2)}) collective-permute-start(bf16[384,128]{1,0:T(8,128)(2,1)S(1)} %get-tuple-element.47), channel_id=1, source_target_pairs={{0,4},{2,6},{4,0},{6,2},{8,12},{10,14},{12,8},{14,10},{16,20},{18,... | collective-permute-start | bytes 294920 | tf_op jit(solution)/shard_map/ppermute | solution.py:320
  13.0 0.0 copy-start.4
  13.0 0.7 %sibling_term.2 = (f32[64,128]{1,0:T(8,128)S(1)}, f32[128,128]{1,0:T(8,128)S(1)}) custom-call(bf16[4,128,128]{2,1,0:T(8,128)(2,1)S(1)} %bitcast.5, bf16[256,128]{1,0:T(8,128)(2,1)S(1)} %copy-done.5, bf16[400,128]{1,0:T(8,128)(2,1)S(1)} %collective-permute-done.message), custom_call_target="tpu_custom_call" | custom-call | flops 33554432 | bytes 397312 | tf_op jit(solution)/shard_map/sibling_term/pallas_call | solution.py:304
  13.7 0.2 copy-done.4
  13.9 1.4 %self_tile.1.near = f32[64,1024]{1,0:T(8,128)S(1)} custom-call(bf16[1280,256]{1,0:T(8,128)(2,1)S(1)} %get-tuple-element.53.tall, f32[1024,128]{1,0:T(8,128)S(1)} %get-tuple-element.54.norms, bf16[256,1024]{1,0:T(8,128)(2,1)S(1)} %copy-done.1, bf16[64,1024]{1,0:T(8,128)(2,1)S(1)} %copy-done.4), custom_call_target="tpu_custom_call" | custom-call | tf_op jit(solution)/shard_map/self_tile/pallas_call | solution.py:304
  15.3 2.4 %collective-permute-start.3 = (bf16[64,1024]{1,0:T(8,128)(2,1)S(1)}, bf16[64,1024]{1,0:T(8,128)(2,1)S(1)}, u32[]{:S(2)}, u32[]{:S(2)}) collective-permute-start(bf16[64,1024]{1,0:T(8,128)(2,1)S(1)} %copy-done.4), channel_id=1, source_target_pairs={{0,4},{2,6},{4,8},{6,10},{8,12},{10,14},{12,16},{14,18},{16,20},{1... | collective-permute-start | bytes 393224 | tf_op jit(solution)/shard_map/ppermute | solution.py:330
  17.7 2.5 %collective-permute-done.1.message = bf16[384,128]{1,0:T(8,128)(2,1)S(1)} collective-permute-done((bf16[384,128]{1,0:T(8,128)(2,1)S(1)}, bf16[384,128]{1,0:T(8,128)(2,1)S(1)}, u32[]{:S(2)}, u32[]{:S(2)}) %collective-permute-start.1) | collective-permute-done | bytes 98336 | tf_op jit(solution)/shard_map/ppermute | solution.py:320
  20.2 0.0 collective-permute-done.2.back_wide
  20.2 0.2 join_level.5
  20.5 0.0 copy-start.8
  20.5 0.1 collective-permute-start.4
  20.6 0.4 %sibling_term.3.refs_5_ = f32[64,128]{1,0:T(8,128)S(1)} custom-call(bf16[4,128,128]{2,1,0:T(8,128)(2,1)S(1)} %bitcast.7, bf16[256,128]{1,0:T(8,128)(2,1)S(1)} %get-tuple-element.43.coords, bf16[384,128]{1,0:T(8,128)(2,1)S(1)} %collective-permute-done.1.message), custom_call_target="tpu_custom_call" | custom-call | flops 33554432 | bytes 327680 | tf_op jit(solution)/shard_map/sibling_term/pallas_call | solution.py:304
  21.0 0.0 collective-permute-done.3.back_ordered
  21.0 0.2 copy-done.8
  21.1 0.2 back_tile.1
  21.3 4.0 %collective-permute-done.4.message.refs_1_ = bf16[384,128]{1,0:T(8,128)(2,1)S(1)} collective-permute-done((bf16[384,128]{1,0:T(8,128)(2,1)S(1)}, bf16[384,128]{1,0:T(8,128)(2,1)S(1)}, u32[]{:S(2)}, u32[]{:S(2)}) %collective-permute-start.4) | collective-permute-done | bytes 98336 | tf_op jit(solution)/shard_map/ppermute | solution.py:320
  25.3 0.2 join_level.6
  25.5 2.0 %collective-permute-start.6 = (bf16[384,128]{1,0:T(8,128)(2,1)S(1)}, bf16[384,128]{1,0:T(8,128)(2,1)S(1)}, u32[]{:S(2)}, u32[]{:S(2)}) collective-permute-start(bf16[384,128]{1,0:T(8,128)(2,1)S(1)} %get-tuple-element.70), channel_id=1, source_target_pairs={{0,16},{2,18},{4,20},{6,22},{8,24},{10,26},{12,28},{14,30},{16,0},... | collective-permute-start | bytes 294920 | tf_op jit(solution)/shard_map/ppermute | solution.py:320
  27.5 0.0 collective-permute-done.5.side_tall
  27.5 2.1 %pair_tile.1 = (f32[64,1024]{1,0:T(8,128)S(1)}, bf16[64,1024]{1,0:T(8,128)(2,1)S(1)}, bf16[64,1024]{1,0:T(8,128)(2,1)S(1)}) custom-call(bf16[256,1024]{1,0:T(8,128)(2,1)S(1)} %copy-done.1, bf16[64,1024]{1,0:T(8,128)(2,1)S(1)} %copy-done.4, bf16[1280,256]{1,0:T(8,128)(2,1)S(1)} %collective-permute-done.5.side_tall, ...), custom_call_target="tpu_custom_call" | custom-call | flops 805306368 | bytes 3121152 | tf_op jit(solution)/shard_map/pair_tile/pallas_call | solution.py:304
  29.5 0.1 collective-permute-start.7
  29.6 3.8 %collective-permute-start.9 = (bf16[64,1024]{1,0:T(8,128)(2,1)S(1)}, bf16[64,1024]{1,0:T(8,128)(2,1)S(1)}, u32[]{:S(2)}, u32[]{:S(2)}) collective-permute-start(bf16[64,1024]{1,0:T(8,128)(2,1)S(1)} %get-tuple-element.74), channel_id=1, source_target_pairs={{0,28},{2,30},{4,0},{6,2},{8,4},{10,6},{12,8},{14,10},{16,12},{18,... | collective-permute-start | bytes 393224 | tf_op jit(solution)/shard_map/ppermute | solution.py:325
  33.4 0.0 collective-permute-done.6.message.refs_3_
  33.4 0.2 join_level.7.own_top
  33.6 0.0 copy-start.2
  33.6 0.1 collective-permute-start.8
  33.7 1.0 %last_terms.1.potential = f32[64,128]{1,0:T(8,128)S(1)} custom-call(bf16[4,128,128]{2,1,0:T(8,128)(2,1)S(1)} %bitcast.10, bf16[256,128]{1,0:T(8,128)(2,1)S(1)} %get-tuple-element.49.coords.refs_0_, bf16[384,128]{1,0:T(8,128)(2,1)S(1)} %collective-permute-done.4.message.refs_1_, bf16[256,128]{1,0:T(8,128)(2,1)S(1)} %get-tuple-element.63.coords.refs_2_, ...), custom_call_target="tpu_custom_call" | custom-call | flops 33554432 | bytes 557056 | tf_op jit(solution)/shard_map/last_terms/pallas_call | solution.py:304
  34.7 0.0 collective-permute-done.7.side
  34.7 0.3 collective-permute-done.8.refs_0_
  34.9 0.0 copy-done.2
  34.9 0.7 %far_field.1.here = f32[64,1024]{1,0:T(8,128)S(1)} custom-call(bf16[320,128]{1,0:T(8,128)(2,1)S(1)} %join_level.7.own_top, f32[64,128]{1,0:T(8,128)S(1)} %last_terms.1.potential, f32[128,128]{1,0:T(8,128)S(1)} %get-tuple-element.71.product, bf16[128,1024]{1,0:T(8,128)(2,1)S(1)} %copy-done.2, f32[64,1024]{1,0:T(8,128)S(1)} %get-tuple-element.72.near, ...), custom_call_target="tpu_custom_call" | custom-call | flops 33554432 | bytes 1179648 | tf_op jit(solution)/shard_map/far_field/pallas_call | solution.py:304
  35.7 0.3 collective-permute-done.9.back
  35.9 0.7 %total.1 = f32[64,1024]{1,0:T(8,128)} custom-call(f32[64,1024]{1,0:T(8,128)S(1)} %far_field.1.here, bf16[64,1024]{1,0:T(8,128)(2,1)S(1)} %collective-permute-done.9.back), custom_call_target="tpu_custom_call" | custom-call | flops 131072 | bytes 655360 | tf_op jit(solution)/shard_map/total/pallas_call | solution.py:304
Async XLA Ops:
  0.0 20.2 %collective-permute-start.2 = (bf16[256,1024]{1,0:T(8,128)(2,1)}, bf16[256,1024]{1,0:T(8,128)(2,1)S(1)}, u32[]{:S(2)}, u32[]{:S(2)}) collective-permute-start(bf16[256,1024]{1,0:T(8,128)(2,1)} %wide.3), channel_id=1, source_target_pairs={{0,4},{2,6},{4,8},{6,10},{8,12},{10,14},{12,16},{14,18},{16,20},{1... | collective-permute-start | bytes 1572872 | tf_op jit(solution)/shard_map/ppermute | solution.py:325
  3.0 4.6 %copy-start.1 = (bf16[256,1024]{1,0:T(8,128)(2,1)S(1)}, bf16[256,1024]{1,0:T(8,128)(2,1)}, u32[]{:S(2)}) copy-start(bf16[256,1024]{1,0:T(8,128)(2,1)} %wide.3) | copy-start | bytes 1572868
  6.0 5.1 %collective-permute-start = (bf16[400,128]{1,0:T(8,128)(2,1)}, bf16[400,128]{1,0:T(8,128)(2,1)S(1)}, u32[]{:S(2)}, u32[]{:S(2)}) collective-permute-start(bf16[400,128]{1,0:T(8,128)(2,1)} %get-tuple-element.42), channel_id=1, source_target_pairs={{0,2},{2,0},{4,6},{6,4},{8,10},{10,8},{12,14},{14,12},{16,18},{18,... | collective-permute-start | bytes 307208 | tf_op jit(solution)/shard_map/ppermute | solution.py:320
  7.6 0.9 %copy-start.3 = (bf16[64,1024]{1,0:T(8,128)(2,1)S(1)}, bf16[64,1024]{1,0:T(8,128)(2,1)}, u32[]{:S(2)}) copy-start(bf16[64,1024]{1,0:T(8,128)(2,1)} %get-tuple-element.57.ordered) | copy-start | bytes 393220
  8.5 2.7 %copy-start = (bf16[1,4,128,128]{3,2,1,0:T(8,128)(2,1)S(1)}, bf16[1,4,128,128]{3,2,1,0:T(8,128)(2,1)}, u32[]{:S(2)}) copy-start(bf16[1,4,128,128]{3,2,1,0:T(8,128)(2,1)} %param.13) | copy-start | bytes 393220
  8.5 2.7 %copy-start.5 = (bf16[256,128]{1,0:T(8,128)(2,1)S(1)}, bf16[256,128]{1,0:T(8,128)(2,1)}, u32[]{:S(2)}) copy-start(bf16[256,128]{1,0:T(8,128)(2,1)} %get-tuple-element.40.coords) | copy-start | bytes 196612
  8.5 2.7 %copy-start.7 = (f32[64,128]{1,0:T(8,128)S(1)}, f32[64,128]{1,0:T(8,128)}, u32[]{:S(2)}) copy-start(f32[64,128]{1,0:T(8,128)} %get-tuple-element.41.passed) | copy-start | bytes 98308
  8.8 2.3 %copy-start.6 = (s32[1,5,128]{2,0,1:T(1,128)S(1)}, s32[1,5,128]{2,0,1:T(1,128)}, u32[]{:S(2)}) copy-start(s32[1,5,128]{2,0,1:T(1,128)} %param.11) | copy-start | bytes 7684
  8.8 18.6 %collective-permute-start.5 = (bf16[1280,256]{1,0:T(8,128)(2,1)S(1)}, bf16[1280,256]{1,0:T(8,128)(2,1)S(1)}, u32[]{:S(2)}, u32[]{:S(2)}) collective-permute-start(bf16[1280,256]{1,0:T(8,128)(2,1)S(1)} %get-tuple-element.53.tall), channel_id=1, source_target_pairs={{0,2},{2,0},{4,6},{6,4},{8,10},{10,8},{12,14},{14,12},{16,18},{18,... | collective-permute-start | bytes 1966088 | tf_op jit(solution)/shard_map/ppermute | solution.py:320
  11.4 8.9 %collective-permute-start.1 = (bf16[384,128]{1,0:T(8,128)(2,1)S(1)}, bf16[384,128]{1,0:T(8,128)(2,1)S(1)}, u32[]{:S(2)}, u32[]{:S(2)}) collective-permute-start(bf16[384,128]{1,0:T(8,128)(2,1)S(1)} %get-tuple-element.47), channel_id=1, source_target_pairs={{0,4},{2,6},{4,0},{6,2},{8,12},{10,14},{12,8},{14,10},{16,20},{18,... | collective-permute-start | bytes 294920 | tf_op jit(solution)/shard_map/ppermute | solution.py:320
  13.0 0.9 %copy-start.4 = (bf16[64,1024]{1,0:T(8,128)(2,1)S(1)}, bf16[64,1024]{1,0:T(8,128)(2,1)}, u32[]{:S(2)}) copy-start(bf16[64,1024]{1,0:T(8,128)(2,1)} %get-tuple-element.57.ordered) | copy-start | bytes 393220
  15.3 5.6 %collective-permute-start.3 = (bf16[64,1024]{1,0:T(8,128)(2,1)S(1)}, bf16[64,1024]{1,0:T(8,128)(2,1)S(1)}, u32[]{:S(2)}, u32[]{:S(2)}) collective-permute-start(bf16[64,1024]{1,0:T(8,128)(2,1)S(1)} %copy-done.4), channel_id=1, source_target_pairs={{0,4},{2,6},{4,8},{6,10},{8,12},{10,14},{12,16},{14,18},{16,20},{1... | collective-permute-start | bytes 393224 | tf_op jit(solution)/shard_map/ppermute | solution.py:330
  20.5 0.7 %copy-start.8 = (bf16[16,128]{1,0:T(8,128)(2,1)S(1)}, bf16[16,128]{1,0:T(8,128)(2,1)}, u32[]{:S(2)}) copy-start(bf16[16,128]{1,0:T(8,128)(2,1)} %get-tuple-element.58.marks) | copy-start | bytes 12292
  20.5 4.8 %collective-permute-start.4 = (bf16[384,128]{1,0:T(8,128)(2,1)S(1)}, bf16[384,128]{1,0:T(8,128)(2,1)S(1)}, u32[]{:S(2)}, u32[]{:S(2)}) collective-permute-start(bf16[384,128]{1,0:T(8,128)(2,1)S(1)} %get-tuple-element.62), channel_id=1, source_target_pairs={{0,8},{2,10},{4,12},{6,14},{8,0},{10,2},{12,4},{14,6},{16,24},{18,... | collective-permute-start | bytes 294920 | tf_op jit(solution)/shard_map/ppermute | solution.py:320
  25.5 7.9 %collective-permute-start.6 = (bf16[384,128]{1,0:T(8,128)(2,1)S(1)}, bf16[384,128]{1,0:T(8,128)(2,1)S(1)}, u32[]{:S(2)}, u32[]{:S(2)}) collective-permute-start(bf16[384,128]{1,0:T(8,128)(2,1)S(1)} %get-tuple-element.70), channel_id=1, source_target_pairs={{0,16},{2,18},{4,20},{6,22},{8,24},{10,26},{12,28},{14,30},{16,0},... | collective-permute-start | bytes 294920 | tf_op jit(solution)/shard_map/ppermute | solution.py:320
  29.5 5.1 %collective-permute-start.7 = (bf16[64,1024]{1,0:T(8,128)(2,1)S(1)}, bf16[64,1024]{1,0:T(8,128)(2,1)S(1)}, u32[]{:S(2)}, u32[]{:S(2)}) collective-permute-start(bf16[64,1024]{1,0:T(8,128)(2,1)S(1)} %get-tuple-element.73), channel_id=1, source_target_pairs={{0,2},{2,0},{4,6},{6,4},{8,10},{10,8},{12,14},{14,12},{16,18},{18,... | collective-permute-start | bytes 393224 | tf_op jit(solution)/shard_map/ppermute | solution.py:320
  29.6 6.3 %collective-permute-start.9 = (bf16[64,1024]{1,0:T(8,128)(2,1)S(1)}, bf16[64,1024]{1,0:T(8,128)(2,1)S(1)}, u32[]{:S(2)}, u32[]{:S(2)}) collective-permute-start(bf16[64,1024]{1,0:T(8,128)(2,1)S(1)} %get-tuple-element.74), channel_id=1, source_target_pairs={{0,28},{2,30},{4,0},{6,2},{8,4},{10,6},{12,8},{14,10},{16,12},{18,... | collective-permute-start | bytes 393224 | tf_op jit(solution)/shard_map/ppermute | solution.py:325
  33.6 1.4 %copy-start.2 = (bf16[128,1024]{1,0:T(8,128)(2,1)S(1)}, bf16[128,1024]{1,0:T(8,128)(2,1)}, u32[]{:S(2)}) copy-start(bf16[128,1024]{1,0:T(8,128)(2,1)} %interp.1) | copy-start | bytes 786436
  33.6 1.3 %collective-permute-start.8 = (bf16[320,128]{1,0:T(8,128)(2,1)S(1)}, bf16[320,128]{1,0:T(8,128)(2,1)S(1)}, u32[]{:S(2)}, u32[]{:S(2)}) collective-permute-start(bf16[320,128]{1,0:T(8,128)(2,1)S(1)} %join_level.7.own_top), channel_id=1, source_target_pairs={{0,1},{1,0},{2,3},{3,2},{4,5},{5,4},{6,7},{7,6},{8,9},{9,8},{10,11... | collective-permute-start | bytes 245768 | tf_op jit(solution)/shard_map/ppermute | solution.py:325

commit v5 on v3

--- a/solution.py
+++ b/solution.py
@@ -316,13 +316,6 @@
 def rotated(value, axis, turn):
     count = lax.axis_size(axis)
     return lax.ppermute(value, axis, [(place, (place + turn) % count) for place in range(count)])
-
-
-def shifted(value, axis, step):
-    places = range(lax.axis_size(axis))
-    return lax.ppermute(
-        value, axis, [(place, place + step) for place in places if place + step in places]
-    )
 
 
 def shape(dims, dtype):
@@ -435,7 +428,7 @@
                 name="self_tile",
             )
             sent = lax.optimization_barrier((ordered, near))[0]
-            back_ordered = shifted(sent, "leaf", 2)
+            back_ordered = rotated(sent, "leaf", 2)
     own_top = results[0]
     tops = [rotated(own_top, "grp", turn) for turn in range(1, groups)]
     (potential,) = call(

time: 36.9 us -> 38.3 us (1.038)
  waiting for transfers between devices: 10.4 us -> 15.4 us
  starting transfers between devices: 13.3 us -> 9.7 us
    ppermute x6, waiting for transfers between devices: 10.4 us -> 14.4 us  [swapped(): lax.ppermute(value, axis, [(place, place ^ flip) for place in range(count)])]
    ppermute x1 -> x0, starting transfers between devices: 2.41 us -> none  [shifted(): lax.ppermute(value, axis, [(place, place + step) for place in places if p...]
    ppermute x3 -> x4, waiting for transfers between devices: 0.01 us -> 0.95 us  [rotated(): lax.ppermute(value, axis, [(place, (place + turn) % count) for place in r...]
    ppermute x3 -> x4, starting transfers between devices: 4.57 us -> 3.82 us  [rotated(): lax.ppermute(value, axis, [(place, (place + turn) % count) for place in r...]
    ppermute x6, starting transfers between devices: 6.28 us -> 5.87 us  [swapped(): lax.ppermute(value, axis, [(place, place ^ flip) for place in range(count)])]
  transfers between devices with their start and end apart: 10 -> 10, of which waited for: 5 -> 6; matrix products, arithmetic and copies ran while one was open for 0% -> 0% of each run, Pallas kernels for 29% -> 28%
where the time goes in v5:
time: 38.3 us; the launch traced here: 37.6 us
  waiting for transfers between devices  15.4 us (40%)
  Pallas kernels  11.3 us (30%)
  starting transfers between devices  9.7 us (25%)
  local copies, waits for them, and re-layouts  1.14 us (3%)
    ppermute x6, waiting for transfers between devices, swapped(): lax.ppermute(value, axis, [(place, place ^ flip) for place in range(count)])  14.4 us
    pallas_call x14, Pallas kernels, call(): pl.pallas_call(kernel, out_shape=outs, in_specs=[rest] * len(args), out_s...  11.3 us
    ppermute x6, starting transfers between devices, swapped(): lax.ppermute(value, axis, [(place, place ^ flip) for place in range(count)])  5.87 us
    ppermute x4, starting transfers between devices, rotated(): lax.ppermute(value, axis, [(place, (place + turn) % count) for place in r...  3.82 us
    unnamed x18, local copies, waits for them, and re-layouts  1.14 us
    ppermute x4, waiting for transfers between devices, rotated(): lax.ppermute(value, axis, [(place, (place + turn) % count) for place in r...  0.95 us
  transfers between devices with their start and end apart: 10, of which 6 were waited for; matrix products, arithmetic and copies ran while one was open for 0% of the time, Pallas kernels for 28%

profile of v5, /device:TPU:0, one launch (start us, length us, event | category | flops | bytes accessed | tf_op | source)
XLA Modules:
  0.0 37.6 jit_solution(6549291187411962926)
XLA Ops:
  0.0 3.0 %collective-permute-start.2 = (bf16[256,1024]{1,0:T(8,128)(2,1)}, bf16[256,1024]{1,0:T(8,128)(2,1)S(1)}, u32[]{:S(2)}, u32[]{:S(2)}) collective-permute-start(bf16[256,1024]{1,0:T(8,128)(2,1)} %wide.3), channel_id=1, source_target_pairs={{0,4},{2,6},{4,8},{6,10},{8,12},{10,14},{12,16},{14,18},{16,20},{1... | collective-permute-start | bytes 1572872 | tf_op jit(solution)/shard_map/ppermute | solution.py:318
  3.0 0.0 copy-start.1
  3.0 3.0 %start.1 = (bf16[64,1024]{1,0:T(8,128)(2,1)}, bf16[256,128]{1,0:T(8,128)(2,1)}, bf16[16,128]{1,0:T(8,128)(2,1)}, bf16[400,128]{1,0:T(8,128)(2,1)}, f32[64,128]{1,0:T(8,128)}) custom-call(s32[1,1024]{1,0:T(1,128)} %bitcast.16, s32[5,1,128]{2,1,0:T(1,128)} %bitcast.11, s32[1,5]{1,0:T(1,128)} %refs_2_.1, bf16[64,1024]{1,0:T(8,128)(2,1)} %refs_3_.1, ...), custom_call_target="tpu_custom_call" | custom-call | tf_op jit(solution)/shard_map/start/pallas_call | solution.py:297
  6.0 1.6 %collective-permute-start = (bf16[400,128]{1,0:T(8,128)(2,1)}, bf16[400,128]{1,0:T(8,128)(2,1)S(1)}, u32[]{:S(2)}, u32[]{:S(2)}) collective-permute-start(bf16[400,128]{1,0:T(8,128)(2,1)} %get-tuple-element.42), channel_id=1, source_target_pairs={{0,2},{2,0},{4,6},{6,4},{8,10},{10,8},{12,14},{14,12},{16,18},{18,... | collective-permute-start | bytes 307208 | tf_op jit(solution)/shard_map/ppermute | solution.py:313
  7.5 0.0 copy-done.1
  7.6 0.0 copy-start.3
  7.6 0.9 %copy-done.3 = bf16[64,1024]{1,0:T(8,128)(2,1)S(1)} copy-done((bf16[64,1024]{1,0:T(8,128)(2,1)S(1)}, bf16[64,1024]{1,0:T(8,128)(2,1)}, u32[]{:S(2)}) %copy-start.3) | copy-done | bytes 131096
  8.5 0.0 copy-start
  8.5 0.0 copy-start.5
  8.5 0.0 copy-start.7
  8.5 0.3 turn.1
  8.8 0.0 copy-start.6
  8.8 0.6 %collective-permute-start.5 = (bf16[1280,256]{1,0:T(8,128)(2,1)S(1)}, bf16[1280,256]{1,0:T(8,128)(2,1)S(1)}, u32[]{:S(2)}, u32[]{:S(2)}) collective-permute-start(bf16[1280,256]{1,0:T(8,128)(2,1)S(1)} %get-tuple-element.53.tall), channel_id=1, source_target_pairs={{0,2},{2,0},{4,6},{6,4},{8,10},{10,8},{12,14},{14,12},{16,18},{18,... | collective-permute-start | bytes 1966088 | tf_op jit(solution)/shard_map/ppermute | solution.py:313
  9.4 1.7 %collective-permute-done.message = bf16[400,128]{1,0:T(8,128)(2,1)S(1)} collective-permute-done((bf16[400,128]{1,0:T(8,128)(2,1)}, bf16[400,128]{1,0:T(8,128)(2,1)S(1)}, u32[]{:S(2)}, u32[]{:S(2)}) %collective-permute-start) | collective-permute-done | bytes 102432 | tf_op jit(solution)/shard_map/ppermute | solution.py:313
  11.1 0.0 copy-done
  11.1 0.0 copy-done.5
  11.1 0.0 copy-done.7
  11.1 0.0 copy-done.6
  11.2 0.2 join_level.4
  11.4 1.6 %collective-permute-start.1 = (bf16[384,128]{1,0:T(8,128)(2,1)S(1)}, bf16[384,128]{1,0:T(8,128)(2,1)S(1)}, u32[]{:S(2)}, u32[]{:S(2)}) collective-permute-start(bf16[384,128]{1,0:T(8,128)(2,1)S(1)} %get-tuple-element.47), channel_id=1, source_target_pairs={{0,4},{2,6},{4,0},{6,2},{8,12},{10,14},{12,8},{14,10},{16,20},{18,... | collective-permute-start | bytes 294920 | tf_op jit(solution)/shard_map/ppermute | solution.py:313
  13.0 0.0 copy-start.4
  13.0 0.7 %sibling_term.2 = (f32[64,128]{1,0:T(8,128)S(1)}, f32[128,128]{1,0:T(8,128)S(1)}) custom-call(bf16[4,128,128]{2,1,0:T(8,128)(2,1)S(1)} %bitcast.5, bf16[256,128]{1,0:T(8,128)(2,1)S(1)} %copy-done.5, bf16[400,128]{1,0:T(8,128)(2,1)S(1)} %collective-permute-done.message), custom_call_target="tpu_custom_call" | custom-call | flops 33554432 | bytes 397312 | tf_op jit(solution)/shard_map/sibling_term/pallas_call | solution.py:297
  13.7 0.2 copy-done.4
  13.9 1.4 %self_tile.1.near = f32[64,1024]{1,0:T(8,128)S(1)} custom-call(bf16[1280,256]{1,0:T(8,128)(2,1)S(1)} %get-tuple-element.53.tall, f32[1024,128]{1,0:T(8,128)S(1)} %get-tuple-element.54.norms, bf16[256,1024]{1,0:T(8,128)(2,1)S(1)} %copy-done.1, bf16[64,1024]{1,0:T(8,128)(2,1)S(1)} %copy-done.4), custom_call_target="tpu_custom_call" | custom-call | tf_op jit(solution)/shard_map/self_tile/pallas_call | solution.py:297
  15.3 0.5 %collective-permute-start.3 = (bf16[64,1024]{1,0:T(8,128)(2,1)S(1)}, bf16[64,1024]{1,0:T(8,128)(2,1)S(1)}, u32[]{:S(2)}, u32[]{:S(2)}) collective-permute-start(bf16[64,1024]{1,0:T(8,128)(2,1)S(1)} %copy-done.4), channel_id=1, source_target_pairs={{0,4},{2,6},{4,8},{6,10},{8,12},{10,14},{12,16},{14,18},{16,20},{1... | collective-permute-start | bytes 393224 | tf_op jit(solution)/shard_map/ppermute | solution.py:318
  15.9 5.8 %collective-permute-done.1.message = bf16[384,128]{1,0:T(8,128)(2,1)S(1)} collective-permute-done((bf16[384,128]{1,0:T(8,128)(2,1)S(1)}, bf16[384,128]{1,0:T(8,128)(2,1)S(1)}, u32[]{:S(2)}, u32[]{:S(2)}) %collective-permute-start.1) | collective-permute-done | bytes 98336 | tf_op jit(solution)/shard_map/ppermute | solution.py:313
  21.7 0.0 collective-permute-done.2.back_wide
  21.7 0.2 join_level.5
  21.9 0.0 copy-start.8
  21.9 0.1 collective-permute-start.4
  22.0 0.4 %sibling_term.3.refs_5_ = f32[64,128]{1,0:T(8,128)S(1)} custom-call(bf16[4,128,128]{2,1,0:T(8,128)(2,1)S(1)} %bitcast.7, bf16[256,128]{1,0:T(8,128)(2,1)S(1)} %get-tuple-element.43.coords, bf16[384,128]{1,0:T(8,128)(2,1)S(1)} %collective-permute-done.1.message), custom_call_target="tpu_custom_call" | custom-call | flops 33554432 | bytes 327680 | tf_op jit(solution)/shard_map/sibling_term/pallas_call | solution.py:297
  22.4 0.7 %collective-permute-done.3.back_ordered = bf16[64,1024]{1,0:T(8,128)(2,1)S(1)} collective-permute-done((bf16[64,1024]{1,0:T(8,128)(2,1)S(1)}, bf16[64,1024]{1,0:T(8,128)(2,1)S(1)}, u32[]{:S(2)}, u32[]{:S(2)}) %collective-permute-start.3) | collective-permute-done | bytes 131104 | tf_op jit(solution)/shard_map/ppermute | solution.py:318
  23.1 0.0 copy-done.8
  23.1 0.2 back_tile.1
  23.2 3.4 %collective-permute-done.4.message.refs_1_ = bf16[384,128]{1,0:T(8,128)(2,1)S(1)} collective-permute-done((bf16[384,128]{1,0:T(8,128)(2,1)S(1)}, bf16[384,128]{1,0:T(8,128)(2,1)S(1)}, u32[]{:S(2)}, u32[]{:S(2)}) %collective-permute-start.4) | collective-permute-done | bytes 98336 | tf_op jit(solution)/shard_map/ppermute | solution.py:313
  26.7 0.2 join_level.6
  26.9 2.0 %collective-permute-start.6 = (bf16[384,128]{1,0:T(8,128)(2,1)S(1)}, bf16[384,128]{1,0:T(8,128)(2,1)S(1)}, u32[]{:S(2)}, u32[]{:S(2)}) collective-permute-start(bf16[384,128]{1,0:T(8,128)(2,1)S(1)} %get-tuple-element.70), channel_id=1, source_target_pairs={{0,16},{2,18},{4,20},{6,22},{8,24},{10,26},{12,28},{14,30},{16,0},... | collective-permute-start | bytes 294920 | tf_op jit(solution)/shard_map/ppermute | solution.py:313
  28.9 0.0 collective-permute-done.5.side_tall
  28.9 2.0 %pair_tile.1 = (f32[64,1024]{1,0:T(8,128)S(1)}, bf16[64,1024]{1,0:T(8,128)(2,1)S(1)}, bf16[64,1024]{1,0:T(8,128)(2,1)S(1)}) custom-call(bf16[256,1024]{1,0:T(8,128)(2,1)S(1)} %copy-done.1, bf16[64,1024]{1,0:T(8,128)(2,1)S(1)} %copy-done.4, bf16[1280,256]{1,0:T(8,128)(2,1)S(1)} %collective-permute-done.5.side_tall, ...), custom_call_target="tpu_custom_call" | custom-call | flops 805306368 | bytes 3121152 | tf_op jit(solution)/shard_map/pair_tile/pallas_call | solution.py:297
  30.9 0.1 collective-permute-start.7
  31.0 0.2 collective-permute-start.9
  31.2 3.5 %collective-permute-done.6.message.refs_3_ = bf16[384,128]{1,0:T(8,128)(2,1)S(1)} collective-permute-done((bf16[384,128]{1,0:T(8,128)(2,1)S(1)}, bf16[384,128]{1,0:T(8,128)(2,1)S(1)}, u32[]{:S(2)}, u32[]{:S(2)}) %collective-permute-start.6) | collective-permute-done | bytes 98336 | tf_op jit(solution)/shard_map/ppermute | solution.py:313
  34.6 0.2 join_level.7.own_top
  34.8 0.0 copy-start.2
  34.8 0.1 collective-permute-start.8
  34.9 1.0 %last_terms.1.potential = f32[64,128]{1,0:T(8,128)S(1)} custom-call(bf16[4,128,128]{2,1,0:T(8,128)(2,1)S(1)} %bitcast.10, bf16[256,128]{1,0:T(8,128)(2,1)S(1)} %get-tuple-element.49.coords.refs_0_, bf16[384,128]{1,0:T(8,128)(2,1)S(1)} %collective-permute-done.4.message.refs_1_, bf16[256,128]{1,0:T(8,128)(2,1)S(1)} %get-tuple-element.63.coords.refs_2_, ...), custom_call_target="tpu_custom_call" | custom-call | flops 33554432 | bytes 557056 | tf_op jit(solution)/shard_map/last_terms/pallas_call | solution.py:297
  35.9 0.0 collective-permute-done.7.side
  35.9 0.3 collective-permute-done.8.refs_0_
  36.2 0.0 copy-done.2
  36.2 0.7 %far_field.1.here = f32[64,1024]{1,0:T(8,128)S(1)} custom-call(bf16[320,128]{1,0:T(8,128)(2,1)S(1)} %join_level.7.own_top, f32[64,128]{1,0:T(8,128)S(1)} %last_terms.1.potential, f32[128,128]{1,0:T(8,128)S(1)} %get-tuple-element.71.product, bf16[128,1024]{1,0:T(8,128)(2,1)S(1)} %copy-done.2, f32[64,1024]{1,0:T(8,128)S(1)} %get-tuple-element.72.near, ...), custom_call_target="tpu_custom_call" | custom-call | flops 33554432 | bytes 1179648 | tf_op jit(solution)/shard_map/far_field/pallas_call | solution.py:297
  36.9 0.0 collective-permute-done.9.back
  36.9 0.7 %total.1 = f32[64,1024]{1,0:T(8,128)} custom-call(f32[64,1024]{1,0:T(8,128)S(1)} %far_field.1.here, bf16[64,1024]{1,0:T(8,128)(2,1)S(1)} %collective-permute-done.9.back), custom_call_target="tpu_custom_call" | custom-call | flops 131072 | bytes 655360 | tf_op jit(solution)/shard_map/total/pallas_call | solution.py:297
Async XLA Ops:
  0.0 21.7 %collective-permute-start.2 = (bf16[256,1024]{1,0:T(8,128)(2,1)}, bf16[256,1024]{1,0:T(8,128)(2,1)S(1)}, u32[]{:S(2)}, u32[]{:S(2)}) collective-permute-start(bf16[256,1024]{1,0:T(8,128)(2,1)} %wide.3), channel_id=1, source_target_pairs={{0,4},{2,6},{4,8},{6,10},{8,12},{10,14},{12,16},{14,18},{16,20},{1... | collective-permute-start | bytes 1572872 | tf_op jit(solution)/shard_map/ppermute | solution.py:318
  3.0 4.6 %copy-start.1 = (bf16[256,1024]{1,0:T(8,128)(2,1)S(1)}, bf16[256,1024]{1,0:T(8,128)(2,1)}, u32[]{:S(2)}) copy-start(bf16[256,1024]{1,0:T(8,128)(2,1)} %wide.3) | copy-start | bytes 1572868
  6.0 5.1 %collective-permute-start = (bf16[400,128]{1,0:T(8,128)(2,1)}, bf16[400,128]{1,0:T(8,128)(2,1)S(1)}, u32[]{:S(2)}, u32[]{:S(2)}) collective-permute-start(bf16[400,128]{1,0:T(8,128)(2,1)} %get-tuple-element.42), channel_id=1, source_target_pairs={{0,2},{2,0},{4,6},{6,4},{8,10},{10,8},{12,14},{14,12},{16,18},{18,... | collective-permute-start | bytes 307208 | tf_op jit(solution)/shard_map/ppermute | solution.py:313
  7.6 0.9 %copy-start.3 = (bf16[64,1024]{1,0:T(8,128)(2,1)S(1)}, bf16[64,1024]{1,0:T(8,128)(2,1)}, u32[]{:S(2)}) copy-start(bf16[64,1024]{1,0:T(8,128)(2,1)} %get-tuple-element.57.ordered) | copy-start | bytes 393220
  8.5 2.7 %copy-start = (bf16[1,4,128,128]{3,2,1,0:T(8,128)(2,1)S(1)}, bf16[1,4,128,128]{3,2,1,0:T(8,128)(2,1)}, u32[]{:S(2)}) copy-start(bf16[1,4,128,128]{3,2,1,0:T(8,128)(2,1)} %param.13) | copy-start | bytes 393220
  8.5 2.7 %copy-start.5 = (bf16[256,128]{1,0:T(8,128)(2,1)S(1)}, bf16[256,128]{1,0:T(8,128)(2,1)}, u32[]{:S(2)}) copy-start(bf16[256,128]{1,0:T(8,128)(2,1)} %get-tuple-element.40.coords) | copy-start | bytes 196612
  8.5 2.7 %copy-start.7 = (f32[64,128]{1,0:T(8,128)S(1)}, f32[64,128]{1,0:T(8,128)}, u32[]{:S(2)}) copy-start(f32[64,128]{1,0:T(8,128)} %get-tuple-element.41.passed) | copy-start | bytes 98308
  8.8 2.3 %copy-start.6 = (s32[1,5,128]{2,0,1:T(1,128)S(1)}, s32[1,5,128]{2,0,1:T(1,128)}, u32[]{:S(2)}) copy-start(s32[1,5,128]{2,0,1:T(1,128)} %param.11) | copy-start | bytes 7684
  8.8 20.1 %collective-permute-start.5 = (bf16[1280,256]{1,0:T(8,128)(2,1)S(1)}, bf16[1280,256]{1,0:T(8,128)(2,1)S(1)}, u32[]{:S(2)}, u32[]{:S(2)}) collective-permute-start(bf16[1280,256]{1,0:T(8,128)(2,1)S(1)} %get-tuple-element.53.tall), channel_id=1, source_target_pairs={{0,2},{2,0},{4,6},{6,4},{8,10},{10,8},{12,14},{14,12},{16,18},{18,... | collective-permute-start | bytes 1966088 | tf_op jit(solution)/shard_map/ppermute | solution.py:313
  11.4 10.3 %collective-permute-start.1 = (bf16[384,128]{1,0:T(8,128)(2,1)S(1)}, bf16[384,128]{1,0:T(8,128)(2,1)S(1)}, u32[]{:S(2)}, u32[]{:S(2)}) collective-permute-start(bf16[384,128]{1,0:T(8,128)(2,1)S(1)} %get-tuple-element.47), channel_id=1, source_target_pairs={{0,4},{2,6},{4,0},{6,2},{8,12},{10,14},{12,8},{14,10},{16,20},{18,... | collective-permute-start | bytes 294920 | tf_op jit(solution)/shard_map/ppermute | solution.py:313
  13.0 0.9 %copy-start.4 = (bf16[64,1024]{1,0:T(8,128)(2,1)S(1)}, bf16[64,1024]{1,0:T(8,128)(2,1)}, u32[]{:S(2)}) copy-start(bf16[64,1024]{1,0:T(8,128)(2,1)} %get-tuple-element.57.ordered) | copy-start | bytes 393220
  15.3 7.7 %collective-permute-start.3 = (bf16[64,1024]{1,0:T(8,128)(2,1)S(1)}, bf16[64,1024]{1,0:T(8,128)(2,1)S(1)}, u32[]{:S(2)}, u32[]{:S(2)}) collective-permute-start(bf16[64,1024]{1,0:T(8,128)(2,1)S(1)} %copy-done.4), channel_id=1, source_target_pairs={{0,4},{2,6},{4,8},{6,10},{8,12},{10,14},{12,16},{14,18},{16,20},{1... | collective-permute-start | bytes 393224 | tf_op jit(solution)/shard_map/ppermute | solution.py:318
  21.9 1.2 %copy-start.8 = (bf16[16,128]{1,0:T(8,128)(2,1)S(1)}, bf16[16,128]{1,0:T(8,128)(2,1)}, u32[]{:S(2)}) copy-start(bf16[16,128]{1,0:T(8,128)(2,1)} %get-tuple-element.58.marks) | copy-start | bytes 12292
  21.9 4.8 %collective-permute-start.4 = (bf16[384,128]{1,0:T(8,128)(2,1)S(1)}, bf16[384,128]{1,0:T(8,128)(2,1)S(1)}, u32[]{:S(2)}, u32[]{:S(2)}) collective-permute-start(bf16[384,128]{1,0:T(8,128)(2,1)S(1)} %get-tuple-element.62), channel_id=1, source_target_pairs={{0,8},{2,10},{4,12},{6,14},{8,0},{10,2},{12,4},{14,6},{16,24},{18,... | collective-permute-start | bytes 294920 | tf_op jit(solution)/shard_map/ppermute | solution.py:313
  26.9 7.7 %collective-permute-start.6 = (bf16[384,128]{1,0:T(8,128)(2,1)S(1)}, bf16[384,128]{1,0:T(8,128)(2,1)S(1)}, u32[]{:S(2)}, u32[]{:S(2)}) collective-permute-start(bf16[384,128]{1,0:T(8,128)(2,1)S(1)} %get-tuple-element.70), channel_id=1, source_target_pairs={{0,16},{2,18},{4,20},{6,22},{8,24},{10,26},{12,28},{14,30},{16,0},... | collective-permute-start | bytes 294920 | tf_op jit(solution)/shard_map/ppermute | solution.py:313
  30.9 5.0 %collective-permute-start.7 = (bf16[64,1024]{1,0:T(8,128)(2,1)S(1)}, bf16[64,1024]{1,0:T(8,128)(2,1)S(1)}, u32[]{:S(2)}, u32[]{:S(2)}) collective-permute-start(bf16[64,1024]{1,0:T(8,128)(2,1)S(1)} %get-tuple-element.73), channel_id=1, source_target_pairs={{0,2},{2,0},{4,6},{6,4},{8,10},{10,8},{12,14},{14,12},{16,18},{18,... | collective-permute-start | bytes 393224 | tf_op jit(solution)/shard_map/ppermute | solution.py:313
  31.0 6.0 %collective-permute-start.9 = (bf16[64,1024]{1,0:T(8,128)(2,1)S(1)}, bf16[64,1024]{1,0:T(8,128)(2,1)S(1)}, u32[]{:S(2)}, u32[]{:S(2)}) collective-permute-start(bf16[64,1024]{1,0:T(8,128)(2,1)S(1)} %get-tuple-element.74), channel_id=1, source_target_pairs={{0,28},{2,30},{4,0},{6,2},{8,4},{10,6},{12,8},{14,10},{16,12},{18,... | collective-permute-start | bytes 393224 | tf_op jit(solution)/shard_map/ppermute | solution.py:318
  34.8 1.4 %copy-start.2 = (bf16[128,1024]{1,0:T(8,128)(2,1)S(1)}, bf16[128,1024]{1,0:T(8,128)(2,1)}, u32[]{:S(2)}) copy-start(bf16[128,1024]{1,0:T(8,128)(2,1)} %interp.1) | copy-start | bytes 786436
  34.8 1.3 %collective-permute-start.8 = (bf16[320,128]{1,0:T(8,128)(2,1)S(1)}, bf16[320,128]{1,0:T(8,128)(2,1)S(1)}, u32[]{:S(2)}, u32[]{:S(2)}) collective-permute-start(bf16[320,128]{1,0:T(8,128)(2,1)S(1)} %join_level.7.own_top), channel_id=1, source_target_pairs={{0,1},{1,0},{2,3},{3,2},{4,5},{5,4},{6,7},{7,6},{8,9},{9,8},{10,11... | collective-permute-start | bytes 245768 | tf_op jit(solution)/shard_map/ppermute | solution.py:318

commit v6 on v3

--- a/solution.py
+++ b/solution.py
@@ -272,7 +272,7 @@
         side_ref[...] = jnp.zeros_like(side_ref)
 
 
-def far_kernel(others, own_top, potential, product, interp, near, side, *refs):
+def far_kernel(others, own_top, potential, product, interp, near, side, back, *refs):
     tops, out_ref = refs[:others], refs[-1]
     sides = out_ref.shape[0]
     dimension = own_top.shape[0] - sides
@@ -283,11 +283,8 @@
         above = part if above is None else above + part
     if above is not None:
         total = total + dot_parts(above, product[...])
-    out_ref[...] = (near[...] + side[...].astype(F32)) + dot_split(total, interp[...])
-
-
-def total_kernel(here, back, out_ref):
-    out_ref[...] = here[...] + back[...].astype(F32)
+    here = near[...] + (side[...].astype(F32) + back[...].astype(F32))
+    out_ref[...] = here + dot_split(total, interp[...])
 
 
 def call(kernel, outs, args, scratch=(), anywhere=False, flops=0, exps=0, name=None):
@@ -446,14 +443,13 @@
         exps=count * count,
         name="last_terms",
     )
-    (here,) = call(
+    (out,) = call(
         functools.partial(far_kernel, len(tops)),
         [block_sums],
-        [own_top, potential, product, leaf_interp, near, side] + tops,
+        [own_top, potential, product, leaf_interp, near, side, back] + tops,
         flops=4 * sides * rows * count,
         name="far_field",
     )
-    (out,) = call(total_kernel, [block_sums], [here, back], flops=2 * sides * rows, name="total")
     return out
 
 

time: 36.9 us -> 37.1 us (level)
  waiting for transfers between devices: 10.4 us -> 10.9 us
    ppermute x3, waiting for transfers between devices: 0.01 us -> 0.97 us  [rotated(): lax.ppermute(value, axis, [(place, (place + turn) % count) for place in r...]
    ppermute x6, starting transfers between devices: 6.28 us -> 6.84 us  [swapped(): lax.ppermute(value, axis, [(place, place ^ flip) for place in range(count)])]
    ppermute x3, starting transfers between devices: 4.57 us -> 4.02 us  [rotated(): lax.ppermute(value, axis, [(place, (place + turn) % count) for place in r...]
    ppermute x6, waiting for transfers between devices: 10.4 us -> 9.95 us  [swapped(): lax.ppermute(value, axis, [(place, place ^ flip) for place in range(count)])]
    pallas_call x14 -> x13, Pallas kernels: 11.3 us -> 11.2 us  [call(): pl.pallas_call(kernel, out_shape=outs, in_specs=[rest] * len(args), out_s...]
  transfers between devices with their start and end apart: 10 -> 10, of which waited for: 5 -> 5; matrix products, arithmetic and copies ran while one was open for 0% -> 0% of each run, Pallas kernels for 29% -> 27%
where the time goes in v6:
time: 37.1 us; the launch traced here: 36.9 us
  starting transfers between devices  13.3 us (36%)
  Pallas kernels  11.2 us (30%)
  waiting for transfers between devices  10.9 us (29%)
  local copies, waits for them, and re-layouts  1.31 us (4%)
    pallas_call x13, Pallas kernels, call(): pl.pallas_call(kernel, out_shape=outs, in_specs=[rest] * len(args), out_s...  11.2 us
    ppermute x6, waiting for transfers between devices, swapped(): lax.ppermute(value, axis, [(place, place ^ flip) for place in range(count)])  9.95 us
    ppermute x6, starting transfers between devices, swapped(): lax.ppermute(value, axis, [(place, place ^ flip) for place in range(count)])  6.84 us
    ppermute x3, starting transfers between devices, rotated(): lax.ppermute(value, axis, [(place, (place + turn) % count) for place in r...  4.02 us
    ppermute x1, starting transfers between devices, shifted(): lax.ppermute(value, axis, [(place, place + step) for place in places if p...  2.41 us
    unnamed x18, local copies, waits for them, and re-layouts  1.31 us
    ppermute x3, waiting for transfers between devices, rotated(): lax.ppermute(value, axis, [(place, (place + turn) % count) for place in r...  0.97 us
  transfers between devices with their start and end apart: 10, of which 5 were waited for; matrix products, arithmetic and copies ran while one was open for 0% of the time, Pallas kernels for 27%

profile of v6, /device:TPU:0, one launch (start us, length us, event | category | flops | bytes accessed | tf_op | source)
XLA Modules:
  0.0 36.9 jit_solution(3795769294710293521)
XLA Ops:
  0.0 3.0 %collective-permute-start.2 = (bf16[256,1024]{1,0:T(8,128)(2,1)}, bf16[256,1024]{1,0:T(8,128)(2,1)S(1)}, u32[]{:S(2)}, u32[]{:S(2)}) collective-permute-start(bf16[256,1024]{1,0:T(8,128)(2,1)} %wide.3), channel_id=1, source_target_pairs={{0,4},{2,6},{4,8},{6,10},{8,12},{10,14},{12,16},{14,18},{16,20},{1... | collective-permute-start | bytes 1572872 | tf_op jit(solution)/shard_map/ppermute | solution.py:315
  3.0 0.0 copy-start.1
  3.0 3.0 %start.1 = (bf16[64,1024]{1,0:T(8,128)(2,1)}, bf16[256,128]{1,0:T(8,128)(2,1)}, bf16[16,128]{1,0:T(8,128)(2,1)}, bf16[400,128]{1,0:T(8,128)(2,1)}, f32[64,128]{1,0:T(8,128)}) custom-call(s32[1,1024]{1,0:T(1,128)} %bitcast.16, s32[5,1,128]{2,1,0:T(1,128)} %bitcast.11, s32[1,5]{1,0:T(1,128)} %refs_2_.1, bf16[64,1024]{1,0:T(8,128)(2,1)} %refs_3_.1, ...), custom_call_target="tpu_custom_call" | custom-call | tf_op jit(solution)/shard_map/start/pallas_call | solution.py:294
  6.0 1.6 %collective-permute-start = (bf16[400,128]{1,0:T(8,128)(2,1)}, bf16[400,128]{1,0:T(8,128)(2,1)S(1)}, u32[]{:S(2)}, u32[]{:S(2)}) collective-permute-start(bf16[400,128]{1,0:T(8,128)(2,1)} %get-tuple-element.42), channel_id=1, source_target_pairs={{0,2},{2,0},{4,6},{6,4},{8,10},{10,8},{12,14},{14,12},{16,18},{18,... | collective-permute-start | bytes 307208 | tf_op jit(solution)/shard_map/ppermute | solution.py:310
  7.5 0.0 copy-done.1
  7.6 0.0 copy-start.3
  7.6 0.9 %copy-done.3 = bf16[64,1024]{1,0:T(8,128)(2,1)S(1)} copy-done((bf16[64,1024]{1,0:T(8,128)(2,1)S(1)}, bf16[64,1024]{1,0:T(8,128)(2,1)}, u32[]{:S(2)}) %copy-start.3) | copy-done | bytes 131096
  8.5 0.0 copy-start
  8.5 0.0 copy-start.5
  8.5 0.0 copy-start.7
  8.5 0.3 turn.1
  8.8 0.0 copy-start.6
  8.8 0.6 %collective-permute-start.5 = (bf16[1280,256]{1,0:T(8,128)(2,1)S(1)}, bf16[1280,256]{1,0:T(8,128)(2,1)S(1)}, u32[]{:S(2)}, u32[]{:S(2)}) collective-permute-start(bf16[1280,256]{1,0:T(8,128)(2,1)S(1)} %get-tuple-element.53.tall), channel_id=1, source_target_pairs={{0,2},{2,0},{4,6},{6,4},{8,10},{10,8},{12,14},{14,12},{16,18},{18,... | collective-permute-start | bytes 1966088 | tf_op jit(solution)/shard_map/ppermute | solution.py:310
  9.4 1.7 %collective-permute-done.message = bf16[400,128]{1,0:T(8,128)(2,1)S(1)} collective-permute-done((bf16[400,128]{1,0:T(8,128)(2,1)}, bf16[400,128]{1,0:T(8,128)(2,1)S(1)}, u32[]{:S(2)}, u32[]{:S(2)}) %collective-permute-start) | collective-permute-done | bytes 102432 | tf_op jit(solution)/shard_map/ppermute | solution.py:310
  11.1 0.0 copy-done
  11.1 0.0 copy-done.5
  11.1 0.0 copy-done.7
  11.1 0.0 copy-done.6
  11.2 0.2 join_level.4
  11.4 1.6 %collective-permute-start.1 = (bf16[384,128]{1,0:T(8,128)(2,1)S(1)}, bf16[384,128]{1,0:T(8,128)(2,1)S(1)}, u32[]{:S(2)}, u32[]{:S(2)}) collective-permute-start(bf16[384,128]{1,0:T(8,128)(2,1)S(1)} %get-tuple-element.47), channel_id=1, source_target_pairs={{0,4},{2,6},{4,0},{6,2},{8,12},{10,14},{12,8},{14,10},{16,20},{18,... | collective-permute-start | bytes 294920 | tf_op jit(solution)/shard_map/ppermute | solution.py:310
  13.0 0.0 copy-start.4
  13.0 0.7 %sibling_term.2 = (f32[64,128]{1,0:T(8,128)S(1)}, f32[128,128]{1,0:T(8,128)S(1)}) custom-call(bf16[4,128,128]{2,1,0:T(8,128)(2,1)S(1)} %bitcast.5, bf16[256,128]{1,0:T(8,128)(2,1)S(1)} %copy-done.5, bf16[400,128]{1,0:T(8,128)(2,1)S(1)} %collective-permute-done.message), custom_call_target="tpu_custom_call" | custom-call | flops 33554432 | bytes 397312 | tf_op jit(solution)/shard_map/sibling_term/pallas_call | solution.py:294
  13.7 0.2 copy-done.4
  13.9 1.4 %self_tile.1.near = f32[64,1024]{1,0:T(8,128)S(1)} custom-call(bf16[1280,256]{1,0:T(8,128)(2,1)S(1)} %get-tuple-element.53.tall, f32[1024,128]{1,0:T(8,128)S(1)} %get-tuple-element.54.norms, bf16[256,1024]{1,0:T(8,128)(2,1)S(1)} %copy-done.1, bf16[64,1024]{1,0:T(8,128)(2,1)S(1)} %copy-done.4), custom_call_target="tpu_custom_call" | custom-call | tf_op jit(solution)/shard_map/self_tile/pallas_call | solution.py:294
  15.3 2.4 %collective-permute-start.3 = (bf16[64,1024]{1,0:T(8,128)(2,1)S(1)}, bf16[64,1024]{1,0:T(8,128)(2,1)S(1)}, u32[]{:S(2)}, u32[]{:S(2)}) collective-permute-start(bf16[64,1024]{1,0:T(8,128)(2,1)S(1)} %copy-done.4), channel_id=1, source_target_pairs={{0,4},{2,6},{4,8},{6,10},{8,12},{10,14},{12,16},{14,18},{16,20},{1... | collective-permute-start | bytes 393224 | tf_op jit(solution)/shard_map/ppermute | solution.py:320
  17.7 2.5 %collective-permute-done.1.message = bf16[384,128]{1,0:T(8,128)(2,1)S(1)} collective-permute-done((bf16[384,128]{1,0:T(8,128)(2,1)S(1)}, bf16[384,128]{1,0:T(8,128)(2,1)S(1)}, u32[]{:S(2)}, u32[]{:S(2)}) %collective-permute-start.1) | collective-permute-done | bytes 98336 | tf_op jit(solution)/shard_map/ppermute | solution.py:310
  20.2 0.0 collective-permute-done.2.back_wide
  20.2 0.2 join_level.5
  20.5 0.0 copy-start.8
  20.5 0.1 collective-permute-start.4
  20.6 0.4 %sibling_term.3.refs_5_ = f32[64,128]{1,0:T(8,128)S(1)} custom-call(bf16[4,128,128]{2,1,0:T(8,128)(2,1)S(1)} %bitcast.7, bf16[256,128]{1,0:T(8,128)(2,1)S(1)} %get-tuple-element.43.coords, bf16[384,128]{1,0:T(8,128)(2,1)S(1)} %collective-permute-done.1.message), custom_call_target="tpu_custom_call" | custom-call | flops 33554432 | bytes 327680 | tf_op jit(solution)/shard_map/sibling_term/pallas_call | solution.py:294
  21.0 0.0 collective-permute-done.3.back_ordered
  21.0 0.2 copy-done.8
  21.1 0.2 back_tile.1
  21.3 4.0 %collective-permute-done.4.message.refs_1_ = bf16[384,128]{1,0:T(8,128)(2,1)S(1)} collective-permute-done((bf16[384,128]{1,0:T(8,128)(2,1)S(1)}, bf16[384,128]{1,0:T(8,128)(2,1)S(1)}, u32[]{:S(2)}, u32[]{:S(2)}) %collective-permute-start.4) | collective-permute-done | bytes 98336 | tf_op jit(solution)/shard_map/ppermute | solution.py:310
  25.3 0.2 join_level.6
  25.5 2.0 %collective-permute-start.6 = (bf16[384,128]{1,0:T(8,128)(2,1)S(1)}, bf16[384,128]{1,0:T(8,128)(2,1)S(1)}, u32[]{:S(2)}, u32[]{:S(2)}) collective-permute-start(bf16[384,128]{1,0:T(8,128)(2,1)S(1)} %get-tuple-element.70), channel_id=1, source_target_pairs={{0,16},{2,18},{4,20},{6,22},{8,24},{10,26},{12,28},{14,30},{16,0},... | collective-permute-start | bytes 294920 | tf_op jit(solution)/shard_map/ppermute | solution.py:310
  27.5 0.0 collective-permute-done.5.side_tall
  27.5 2.0 %pair_tile.1 = (f32[64,1024]{1,0:T(8,128)S(1)}, bf16[64,1024]{1,0:T(8,128)(2,1)S(1)}, bf16[64,1024]{1,0:T(8,128)(2,1)S(1)}) custom-call(bf16[256,1024]{1,0:T(8,128)(2,1)S(1)} %copy-done.1, bf16[64,1024]{1,0:T(8,128)(2,1)S(1)} %copy-done.4, bf16[1280,256]{1,0:T(8,128)(2,1)S(1)} %collective-permute-done.5.side_tall, ...), custom_call_target="tpu_custom_call" | custom-call | flops 805306368 | bytes 3121152 | tf_op jit(solution)/shard_map/pair_tile/pallas_call | solution.py:294
  29.5 1.0 %collective-permute-start.7 = (bf16[64,1024]{1,0:T(8,128)(2,1)S(1)}, bf16[64,1024]{1,0:T(8,128)(2,1)S(1)}, u32[]{:S(2)}, u32[]{:S(2)}) collective-permute-start(bf16[64,1024]{1,0:T(8,128)(2,1)S(1)} %get-tuple-element.73), channel_id=1, source_target_pairs={{0,2},{2,0},{4,6},{6,4},{8,10},{10,8},{12,14},{14,12},{16,18},{18,... | collective-permute-start | bytes 393224 | tf_op jit(solution)/shard_map/ppermute | solution.py:310
  30.5 1.0 %collective-permute-start.8 = (bf16[64,1024]{1,0:T(8,128)(2,1)S(1)}, bf16[64,1024]{1,0:T(8,128)(2,1)S(1)}, u32[]{:S(2)}, u32[]{:S(2)}) collective-permute-start(bf16[64,1024]{1,0:T(8,128)(2,1)S(1)} %get-tuple-element.74), channel_id=1, source_target_pairs={{0,28},{2,30},{4,0},{6,2},{8,4},{10,6},{12,8},{14,10},{16,12},{18,... | collective-permute-start | bytes 393224 | tf_op jit(solution)/shard_map/ppermute | solution.py:315
  31.5 1.7 %collective-permute-done.6.message.refs_3_ = bf16[384,128]{1,0:T(8,128)(2,1)S(1)} collective-permute-done((bf16[384,128]{1,0:T(8,128)(2,1)S(1)}, bf16[384,128]{1,0:T(8,128)(2,1)S(1)}, u32[]{:S(2)}, u32[]{:S(2)}) %collective-permute-start.6) | collective-permute-done | bytes 98336 | tf_op jit(solution)/shard_map/ppermute | solution.py:310
  33.2 0.2 join_level.7.own_top
  33.4 0.0 copy-start.2
  33.4 0.1 collective-permute-start.9
  33.5 1.0 %last_terms.1.potential = f32[64,128]{1,0:T(8,128)S(1)} custom-call(bf16[4,128,128]{2,1,0:T(8,128)(2,1)S(1)} %bitcast.10, bf16[256,128]{1,0:T(8,128)(2,1)S(1)} %get-tuple-element.49.coords.refs_0_, bf16[384,128]{1,0:T(8,128)(2,1)S(1)} %collective-permute-done.4.message.refs_1_, bf16[256,128]{1,0:T(8,128)(2,1)S(1)} %get-tuple-element.63.coords.refs_2_, ...), custom_call_target="tpu_custom_call" | custom-call | flops 33554432 | bytes 557056 | tf_op jit(solution)/shard_map/last_terms/pallas_call | solution.py:294
  34.5 0.0 collective-permute-done.7.side
  34.5 1.0 %collective-permute-done.8.back = bf16[64,1024]{1,0:T(8,128)(2,1)S(1)} collective-permute-done((bf16[64,1024]{1,0:T(8,128)(2,1)S(1)}, bf16[64,1024]{1,0:T(8,128)(2,1)S(1)}, u32[]{:S(2)}, u32[]{:S(2)}) %collective-permute-start.8) | collective-permute-done | bytes 131104 | tf_op jit(solution)/shard_map/ppermute | solution.py:315
  35.5 0.0 collective-permute-done.9.refs_0_
  35.5 0.0 copy-done.2
  35.5 1.4 %far_field.1 = f32[64,1024]{1,0:T(8,128)} custom-call(bf16[320,128]{1,0:T(8,128)(2,1)S(1)} %join_level.7.own_top, f32[64,128]{1,0:T(8,128)S(1)} %last_terms.1.potential, f32[128,128]{1,0:T(8,128)S(1)} %get-tuple-element.71.product, bf16[128,1024]{1,0:T(8,128)(2,1)S(1)} %copy-done.2, f32[64,1024]{1,0:T(8,128)S(1)} %get-tuple-element.72.near, ...), custom_call_target="tpu_custom_call" | custom-call | flops 33554432 | bytes 1310720 | tf_op jit(solution)/shard_map/far_field/pallas_call | solution.py:294
Async XLA Ops:
  0.0 20.2 %collective-permute-start.2 = (bf16[256,1024]{1,0:T(8,128)(2,1)}, bf16[256,1024]{1,0:T(8,128)(2,1)S(1)}, u32[]{:S(2)}, u32[]{:S(2)}) collective-permute-start(bf16[256,1024]{1,0:T(8,128)(2,1)} %wide.3), channel_id=1, source_target_pairs={{0,4},{2,6},{4,8},{6,10},{8,12},{10,14},{12,16},{14,18},{16,20},{1... | collective-permute-start | bytes 1572872 | tf_op jit(solution)/shard_map/ppermute | solution.py:315
  3.0 4.6 %copy-start.1 = (bf16[256,1024]{1,0:T(8,128)(2,1)S(1)}, bf16[256,1024]{1,0:T(8,128)(2,1)}, u32[]{:S(2)}) copy-start(bf16[256,1024]{1,0:T(8,128)(2,1)} %wide.3) | copy-start | bytes 1572868
  6.0 5.1 %collective-permute-start = (bf16[400,128]{1,0:T(8,128)(2,1)}, bf16[400,128]{1,0:T(8,128)(2,1)S(1)}, u32[]{:S(2)}, u32[]{:S(2)}) collective-permute-start(bf16[400,128]{1,0:T(8,128)(2,1)} %get-tuple-element.42), channel_id=1, source_target_pairs={{0,2},{2,0},{4,6},{6,4},{8,10},{10,8},{12,14},{14,12},{16,18},{18,... | collective-permute-start | bytes 307208 | tf_op jit(solution)/shard_map/ppermute | solution.py:310
  7.6 0.9 %copy-start.3 = (bf16[64,1024]{1,0:T(8,128)(2,1)S(1)}, bf16[64,1024]{1,0:T(8,128)(2,1)}, u32[]{:S(2)}) copy-start(bf16[64,1024]{1,0:T(8,128)(2,1)} %get-tuple-element.57.ordered) | copy-start | bytes 393220
  8.5 2.7 %copy-start = (bf16[1,4,128,128]{3,2,1,0:T(8,128)(2,1)S(1)}, bf16[1,4,128,128]{3,2,1,0:T(8,128)(2,1)}, u32[]{:S(2)}) copy-start(bf16[1,4,128,128]{3,2,1,0:T(8,128)(2,1)} %param.13) | copy-start | bytes 393220
  8.5 2.7 %copy-start.5 = (bf16[256,128]{1,0:T(8,128)(2,1)S(1)}, bf16[256,128]{1,0:T(8,128)(2,1)}, u32[]{:S(2)}) copy-start(bf16[256,128]{1,0:T(8,128)(2,1)} %get-tuple-element.40.coords) | copy-start | bytes 196612
  8.5 2.7 %copy-start.7 = (f32[64,128]{1,0:T(8,128)S(1)}, f32[64,128]{1,0:T(8,128)}, u32[]{:S(2)}) copy-start(f32[64,128]{1,0:T(8,128)} %get-tuple-element.41.passed) | copy-start | bytes 98308
  8.8 2.3 %copy-start.6 = (s32[1,5,128]{2,0,1:T(1,128)S(1)}, s32[1,5,128]{2,0,1:T(1,128)}, u32[]{:S(2)}) copy-start(s32[1,5,128]{2,0,1:T(1,128)} %param.11) | copy-start | bytes 7684
  8.8 18.6 %collective-permute-start.5 = (bf16[1280,256]{1,0:T(8,128)(2,1)S(1)}, bf16[1280,256]{1,0:T(8,128)(2,1)S(1)}, u32[]{:S(2)}, u32[]{:S(2)}) collective-permute-start(bf16[1280,256]{1,0:T(8,128)(2,1)S(1)} %get-tuple-element.53.tall), channel_id=1, source_target_pairs={{0,2},{2,0},{4,6},{6,4},{8,10},{10,8},{12,14},{14,12},{16,18},{18,... | collective-permute-start | bytes 1966088 | tf_op jit(solution)/shard_map/ppermute | solution.py:310
  11.4 8.9 %collective-permute-start.1 = (bf16[384,128]{1,0:T(8,128)(2,1)S(1)}, bf16[384,128]{1,0:T(8,128)(2,1)S(1)}, u32[]{:S(2)}, u32[]{:S(2)}) collective-permute-start(bf16[384,128]{1,0:T(8,128)(2,1)S(1)} %get-tuple-element.47), channel_id=1, source_target_pairs={{0,4},{2,6},{4,0},{6,2},{8,12},{10,14},{12,8},{14,10},{16,20},{18,... | collective-permute-start | bytes 294920 | tf_op jit(solution)/shard_map/ppermute | solution.py:310
  13.0 0.9 %copy-start.4 = (bf16[64,1024]{1,0:T(8,128)(2,1)S(1)}, bf16[64,1024]{1,0:T(8,128)(2,1)}, u32[]{:S(2)}) copy-start(bf16[64,1024]{1,0:T(8,128)(2,1)} %get-tuple-element.57.ordered) | copy-start | bytes 393220
  15.3 5.6 %collective-permute-start.3 = (bf16[64,1024]{1,0:T(8,128)(2,1)S(1)}, bf16[64,1024]{1,0:T(8,128)(2,1)S(1)}, u32[]{:S(2)}, u32[]{:S(2)}) collective-permute-start(bf16[64,1024]{1,0:T(8,128)(2,1)S(1)} %copy-done.4), channel_id=1, source_target_pairs={{0,4},{2,6},{4,8},{6,10},{8,12},{10,14},{12,16},{14,18},{16,20},{1... | collective-permute-start | bytes 393224 | tf_op jit(solution)/shard_map/ppermute | solution.py:320
  20.5 0.7 %copy-start.8 = (bf16[16,128]{1,0:T(8,128)(2,1)S(1)}, bf16[16,128]{1,0:T(8,128)(2,1)}, u32[]{:S(2)}) copy-start(bf16[16,128]{1,0:T(8,128)(2,1)} %get-tuple-element.58.marks) | copy-start | bytes 12292
  20.5 4.8 %collective-permute-start.4 = (bf16[384,128]{1,0:T(8,128)(2,1)S(1)}, bf16[384,128]{1,0:T(8,128)(2,1)S(1)}, u32[]{:S(2)}, u32[]{:S(2)}) collective-permute-start(bf16[384,128]{1,0:T(8,128)(2,1)S(1)} %get-tuple-element.62), channel_id=1, source_target_pairs={{0,8},{2,10},{4,12},{6,14},{8,0},{10,2},{12,4},{14,6},{16,24},{18,... | collective-permute-start | bytes 294920 | tf_op jit(solution)/shard_map/ppermute | solution.py:310
  25.5 7.7 %collective-permute-start.6 = (bf16[384,128]{1,0:T(8,128)(2,1)S(1)}, bf16[384,128]{1,0:T(8,128)(2,1)S(1)}, u32[]{:S(2)}, u32[]{:S(2)}) collective-permute-start(bf16[384,128]{1,0:T(8,128)(2,1)S(1)} %get-tuple-element.70), channel_id=1, source_target_pairs={{0,16},{2,18},{4,20},{6,22},{8,24},{10,26},{12,28},{14,30},{16,0},... | collective-permute-start | bytes 294920 | tf_op jit(solution)/shard_map/ppermute | solution.py:310
  29.5 5.0 %collective-permute-start.7 = (bf16[64,1024]{1,0:T(8,128)(2,1)S(1)}, bf16[64,1024]{1,0:T(8,128)(2,1)S(1)}, u32[]{:S(2)}, u32[]{:S(2)}) collective-permute-start(bf16[64,1024]{1,0:T(8,128)(2,1)S(1)} %get-tuple-element.73), channel_id=1, source_target_pairs={{0,2},{2,0},{4,6},{6,4},{8,10},{10,8},{12,14},{14,12},{16,18},{18,... | collective-permute-start | bytes 393224 | tf_op jit(solution)/shard_map/ppermute | solution.py:310
  30.5 5.0 %collective-permute-start.8 = (bf16[64,1024]{1,0:T(8,128)(2,1)S(1)}, bf16[64,1024]{1,0:T(8,128)(2,1)S(1)}, u32[]{:S(2)}, u32[]{:S(2)}) collective-permute-start(bf16[64,1024]{1,0:T(8,128)(2,1)S(1)} %get-tuple-element.74), channel_id=1, source_target_pairs={{0,28},{2,30},{4,0},{6,2},{8,4},{10,6},{12,8},{14,10},{16,12},{18,... | collective-permute-start | bytes 393224 | tf_op jit(solution)/shard_map/ppermute | solution.py:315
  33.4 2.1 %copy-start.2 = (bf16[128,1024]{1,0:T(8,128)(2,1)S(1)}, bf16[128,1024]{1,0:T(8,128)(2,1)}, u32[]{:S(2)}) copy-start(bf16[128,1024]{1,0:T(8,128)(2,1)} %interp.1) | copy-start | bytes 786436
  33.4 2.0 %collective-permute-start.9 = (bf16[320,128]{1,0:T(8,128)(2,1)S(1)}, bf16[320,128]{1,0:T(8,128)(2,1)S(1)}, u32[]{:S(2)}, u32[]{:S(2)}) collective-permute-start(bf16[320,128]{1,0:T(8,128)(2,1)S(1)} %join_level.7.own_top), channel_id=1, source_target_pairs={{0,1},{1,0},{2,3},{3,2},{4,5},{5,4},{6,7},{7,6},{8,9},{9,8},{10,11... | collective-permute-start | bytes 245768 | tf_op jit(solution)/shard_map/ppermute | solution.py:315

commit v7 on v3

--- a/solution.py
+++ b/solution.py
@@ -387,7 +387,7 @@
             terms.append(made[0])
             if level == 1:
                 product = made[1]
-            passed = lax.optimization_barrier((passed, made[0]))[0]
+                passed = lax.optimization_barrier((passed, made[0]))[0]
         history += [coords, received]
         if level == levels - 2:
             near, held = call(
@@ -411,7 +411,7 @@
                 exps=rows * rows,
                 name="pair_tile",
             )
-            passed, near = lax.optimization_barrier((passed, near))
+            passed, near, terms = lax.optimization_barrier((passed, near, terms))
             back = rotated(back, "leaf", -2)
             side = swapped(side, "leaf", 1)
         if last:

time: 36.9 us -> 36.6 us (level)
  waiting for transfers between devices: 10.4 us -> 9.57 us
  local copies, waits for them, and re-layouts: 1.31 us -> 1.7 us
    ppermute x6, waiting for transfers between devices: 10.4 us -> 9.56 us  [swapped(): lax.ppermute(value, axis, [(place, place ^ flip) for place in range(count)])]
    ppermute x6, starting transfers between devices: 6.28 us -> 5.87 us  [swapped(): lax.ppermute(value, axis, [(place, place ^ flip) for place in range(count)])]
    ppermute x3, starting transfers between devices: 4.57 us -> 4.97 us  [rotated(): lax.ppermute(value, axis, [(place, (place + turn) % count) for place in r...]
    unnamed x18, local copies, waits for them, and re-layouts: 1.31 us -> 1.7 us
where the time goes in v7:
time: 36.6 us; the launch traced here: 36 us
  starting transfers between devices  13.3 us (36%)
  Pallas kernels  11.3 us (31%)
  waiting for transfers between devices  9.57 us (26%)
  local copies, waits for them, and re-layouts  1.7 us (5%)
    pallas_call x14, Pallas kernels, call(): pl.pallas_call(kernel, out_shape=outs, in_specs=[rest] * len(args), out_s...  11.3 us
    ppermute x6, waiting for transfers between devices, swapped(): lax.ppermute(value, axis, [(place, place ^ flip) for place in range(count)])  9.56 us
    ppermute x6, starting transfers between devices, swapped(): lax.ppermute(value, axis, [(place, place ^ flip) for place in range(count)])  5.87 us
    ppermute x3, starting transfers between devices, rotated(): lax.ppermute(value, axis, [(place, (place + turn) % count) for place in r...  4.97 us
    ppermute x1, starting transfers between devices, shifted(): lax.ppermute(value, axis, [(place, place + step) for place in places if p...  2.41 us
    unnamed x18, local copies, waits for them, and re-layouts  1.7 us
  transfers between devices with their start and end apart: 10, of which 5 were waited for; matrix products, arithmetic and copies ran while one was open for 0% of the time, Pallas kernels for 29%

profile of v7, /device:TPU:0, one launch (start us, length us, event | category | flops | bytes accessed | tf_op | source)
XLA Modules:
  0.0 36.0 jit_solution(2735866244314543745)
XLA Ops:
  0.0 3.0 %collective-permute-start.2 = (bf16[256,1024]{1,0:T(8,128)(2,1)}, bf16[256,1024]{1,0:T(8,128)(2,1)S(1)}, u32[]{:S(2)}, u32[]{:S(2)}) collective-permute-start(bf16[256,1024]{1,0:T(8,128)(2,1)} %wide.3), channel_id=1, source_target_pairs={{0,4},{2,6},{4,8},{6,10},{8,12},{10,14},{12,16},{14,18},{16,20},{1... | collective-permute-start | bytes 1572872 | tf_op jit(solution)/shard_map/ppermute | solution.py:318
  3.0 0.0 copy-start.1
  3.0 3.0 %start.1 = (bf16[64,1024]{1,0:T(8,128)(2,1)}, bf16[256,128]{1,0:T(8,128)(2,1)}, bf16[16,128]{1,0:T(8,128)(2,1)}, bf16[400,128]{1,0:T(8,128)(2,1)}, f32[64,128]{1,0:T(8,128)}) custom-call(s32[1,1024]{1,0:T(1,128)} %bitcast.16, s32[5,1,128]{2,1,0:T(1,128)} %bitcast.11, s32[1,5]{1,0:T(1,128)} %refs_2_.1, bf16[64,1024]{1,0:T(8,128)(2,1)} %refs_3_.1, ...), custom_call_target="tpu_custom_call" | custom-call | tf_op jit(solution)/shard_map/start/pallas_call | solution.py:297
  6.0 1.6 %collective-permute-start = (bf16[400,128]{1,0:T(8,128)(2,1)}, bf16[400,128]{1,0:T(8,128)(2,1)S(1)}, u32[]{:S(2)}, u32[]{:S(2)}) collective-permute-start(bf16[400,128]{1,0:T(8,128)(2,1)} %get-tuple-element.43), channel_id=1, source_target_pairs={{0,2},{2,0},{4,6},{6,4},{8,10},{10,8},{12,14},{14,12},{16,18},{18,... | collective-permute-start | bytes 307208 | tf_op jit(solution)/shard_map/ppermute | solution.py:313
  7.5 0.0 copy-done.1
  7.6 0.0 copy-start.3
  7.6 0.9 %copy-done.3 = bf16[64,1024]{1,0:T(8,128)(2,1)S(1)} copy-done((bf16[64,1024]{1,0:T(8,128)(2,1)S(1)}, bf16[64,1024]{1,0:T(8,128)(2,1)}, u32[]{:S(2)}) %copy-start.3) | copy-done | bytes 131096
  8.5 0.0 copy-start
  8.5 0.0 copy-start.5
  8.5 0.0 copy-start.7
  8.5 0.3 turn.1
  8.8 0.0 copy-start.6
  8.8 0.6 %collective-permute-start.5 = (bf16[1280,256]{1,0:T(8,128)(2,1)S(1)}, bf16[1280,256]{1,0:T(8,128)(2,1)S(1)}, u32[]{:S(2)}, u32[]{:S(2)}) collective-permute-start(bf16[1280,256]{1,0:T(8,128)(2,1)S(1)} %get-tuple-element.53.tall), channel_id=1, source_target_pairs={{0,2},{2,0},{4,6},{6,4},{8,10},{10,8},{12,14},{14,12},{16,18},{18,... | collective-permute-start | bytes 1966088 | tf_op jit(solution)/shard_map/ppermute | solution.py:313
  9.4 1.7 %collective-permute-done.message = bf16[400,128]{1,0:T(8,128)(2,1)S(1)} collective-permute-done((bf16[400,128]{1,0:T(8,128)(2,1)}, bf16[400,128]{1,0:T(8,128)(2,1)S(1)}, u32[]{:S(2)}, u32[]{:S(2)}) %collective-permute-start) | collective-permute-done | bytes 102432 | tf_op jit(solution)/shard_map/ppermute | solution.py:313
  11.1 0.0 copy-done
  11.1 0.0 copy-done.5
  11.1 0.0 copy-done.7
  11.1 0.0 copy-done.6
  11.2 0.2 join_level.4
  11.4 1.6 %collective-permute-start.1 = (bf16[384,128]{1,0:T(8,128)(2,1)S(1)}, bf16[384,128]{1,0:T(8,128)(2,1)S(1)}, u32[]{:S(2)}, u32[]{:S(2)}) collective-permute-start(bf16[384,128]{1,0:T(8,128)(2,1)S(1)} %get-tuple-element.48), channel_id=1, source_target_pairs={{0,4},{2,6},{4,0},{6,2},{8,12},{10,14},{12,8},{14,10},{16,20},{18,... | collective-permute-start | bytes 294920 | tf_op jit(solution)/shard_map/ppermute | solution.py:313
  13.0 0.0 copy-start.4
  13.0 0.7 %sibling_term.2 = (f32[64,128]{1,0:T(8,128)S(1)}, f32[128,128]{1,0:T(8,128)S(1)}) custom-call(bf16[4,128,128]{2,1,0:T(8,128)(2,1)S(1)} %bitcast.5, bf16[256,128]{1,0:T(8,128)(2,1)S(1)} %copy-done.5, bf16[400,128]{1,0:T(8,128)(2,1)S(1)} %collective-permute-done.message), custom_call_target="tpu_custom_call" | custom-call | flops 33554432 | bytes 397312 | tf_op jit(solution)/shard_map/sibling_term/pallas_call | solution.py:297
  13.7 0.2 copy-done.4
  13.9 1.4 %self_tile.1.near = f32[64,1024]{1,0:T(8,128)S(1)} custom-call(bf16[1280,256]{1,0:T(8,128)(2,1)S(1)} %get-tuple-element.53.tall, f32[1024,128]{1,0:T(8,128)S(1)} %get-tuple-element.54.norms, bf16[256,1024]{1,0:T(8,128)(2,1)S(1)} %copy-done.1, bf16[64,1024]{1,0:T(8,128)(2,1)S(1)} %copy-done.4), custom_call_target="tpu_custom_call" | custom-call | tf_op jit(solution)/shard_map/self_tile/pallas_call | solution.py:297
  15.3 2.4 %collective-permute-start.3 = (bf16[64,1024]{1,0:T(8,128)(2,1)S(1)}, bf16[64,1024]{1,0:T(8,128)(2,1)S(1)}, u32[]{:S(2)}, u32[]{:S(2)}) collective-permute-start(bf16[64,1024]{1,0:T(8,128)(2,1)S(1)} %copy-done.4), channel_id=1, source_target_pairs={{0,4},{2,6},{4,8},{6,10},{8,12},{10,14},{12,16},{14,18},{16,20},{1... | collective-permute-start | bytes 393224 | tf_op jit(solution)/shard_map/ppermute | solution.py:323
  17.7 2.5 %collective-permute-done.1.message = bf16[384,128]{1,0:T(8,128)(2,1)S(1)} collective-permute-done((bf16[384,128]{1,0:T(8,128)(2,1)S(1)}, bf16[384,128]{1,0:T(8,128)(2,1)S(1)}, u32[]{:S(2)}, u32[]{:S(2)}) %collective-permute-start.1) | collective-permute-done | bytes 98336 | tf_op jit(solution)/shard_map/ppermute | solution.py:313
  20.2 0.0 collective-permute-done.2.back_wide
  20.2 0.2 join_level.5
  20.5 0.0 copy-start.8
  20.5 0.1 collective-permute-start.4
  20.6 0.0 collective-permute-done.3.back_ordered
  20.6 0.6 %copy-done.8 = bf16[16,128]{1,0:T(8,128)(2,1)S(1)} copy-done((bf16[16,128]{1,0:T(8,128)(2,1)S(1)}, bf16[16,128]{1,0:T(8,128)(2,1)}, u32[]{:S(2)}) %copy-start.8) | copy-done | bytes 4120
  21.1 0.2 back_tile.1
  21.3 4.0 %collective-permute-done.4.message.refs_1_ = bf16[384,128]{1,0:T(8,128)(2,1)S(1)} collective-permute-done((bf16[384,128]{1,0:T(8,128)(2,1)S(1)}, bf16[384,128]{1,0:T(8,128)(2,1)S(1)}, u32[]{:S(2)}, u32[]{:S(2)}) %collective-permute-start.4) | collective-permute-done | bytes 98336 | tf_op jit(solution)/shard_map/ppermute | solution.py:313
  25.3 0.2 join_level.6
  25.5 2.0 %collective-permute-start.6 = (bf16[384,128]{1,0:T(8,128)(2,1)S(1)}, bf16[384,128]{1,0:T(8,128)(2,1)S(1)}, u32[]{:S(2)}, u32[]{:S(2)}) collective-permute-start(bf16[384,128]{1,0:T(8,128)(2,1)S(1)} %get-tuple-element.70), channel_id=1, source_target_pairs={{0,16},{2,18},{4,20},{6,22},{8,24},{10,26},{12,28},{14,30},{16,0},... | collective-permute-start | bytes 294920 | tf_op jit(solution)/shard_map/ppermute | solution.py:313
  27.5 0.0 collective-permute-done.5.side_tall
  27.5 2.0 %pair_tile.1 = (f32[64,1024]{1,0:T(8,128)S(1)}, bf16[64,1024]{1,0:T(8,128)(2,1)S(1)}, bf16[64,1024]{1,0:T(8,128)(2,1)S(1)}) custom-call(bf16[256,1024]{1,0:T(8,128)(2,1)S(1)} %copy-done.1, bf16[64,1024]{1,0:T(8,128)(2,1)S(1)} %copy-done.4, bf16[1280,256]{1,0:T(8,128)(2,1)S(1)} %collective-permute-done.5.side_tall, ...), custom_call_target="tpu_custom_call" | custom-call | flops 805306368 | bytes 3121152 | tf_op jit(solution)/shard_map/pair_tile/pallas_call | solution.py:297
  29.5 0.1 collective-permute-start.7
  29.6 1.9 %collective-permute-start.9 = (bf16[64,1024]{1,0:T(8,128)(2,1)S(1)}, bf16[64,1024]{1,0:T(8,128)(2,1)S(1)}, u32[]{:S(2)}, u32[]{:S(2)}) collective-permute-start(bf16[64,1024]{1,0:T(8,128)(2,1)S(1)} %get-tuple-element.76), channel_id=1, source_target_pairs={{0,28},{2,30},{4,0},{6,2},{8,4},{10,6},{12,8},{14,10},{16,12},{18,... | collective-permute-start | bytes 393224 | tf_op jit(solution)/shard_map/ppermute | solution.py:318
  31.5 0.4 %sibling_term.3.refs_5_ = f32[64,128]{1,0:T(8,128)S(1)} custom-call(bf16[4,128,128]{2,1,0:T(8,128)(2,1)S(1)} %bitcast.8, bf16[256,128]{1,0:T(8,128)(2,1)S(1)} %get-tuple-element.44.coords, bf16[384,128]{1,0:T(8,128)(2,1)S(1)} %collective-permute-done.1.message), custom_call_target="tpu_custom_call" | custom-call | flops 33554432 | bytes 327680 | tf_op jit(solution)/shard_map/sibling_term/pallas_call | solution.py:297
  31.9 0.6 %collective-permute-done.6.message.refs_3_ = bf16[384,128]{1,0:T(8,128)(2,1)S(1)} collective-permute-done((bf16[384,128]{1,0:T(8,128)(2,1)S(1)}, bf16[384,128]{1,0:T(8,128)(2,1)S(1)}, u32[]{:S(2)}, u32[]{:S(2)}) %collective-permute-start.6) | collective-permute-done | bytes 98336 | tf_op jit(solution)/shard_map/ppermute | solution.py:313
  32.5 0.2 join_level.7.own_top
  32.6 0.0 copy-start.2
  32.6 0.1 collective-permute-start.8
  32.7 1.0 %last_terms.1.potential = f32[64,128]{1,0:T(8,128)S(1)} custom-call(bf16[4,128,128]{2,1,0:T(8,128)(2,1)S(1)} %bitcast.10, bf16[256,128]{1,0:T(8,128)(2,1)S(1)} %get-tuple-element.50.coords.refs_0_, bf16[384,128]{1,0:T(8,128)(2,1)S(1)} %collective-permute-done.4.message.refs_1_, bf16[256,128]{1,0:T(8,128)(2,1)S(1)} %get-tuple-element.63.coords.refs_2_, ...), custom_call_target="tpu_custom_call" | custom-call | flops 33554432 | bytes 557056 | tf_op jit(solution)/shard_map/last_terms/pallas_call | solution.py:297
  33.7 0.8 %collective-permute-done.7.side = bf16[64,1024]{1,0:T(8,128)(2,1)S(1)} collective-permute-done((bf16[64,1024]{1,0:T(8,128)(2,1)S(1)}, bf16[64,1024]{1,0:T(8,128)(2,1)S(1)}, u32[]{:S(2)}, u32[]{:S(2)}) %collective-permute-start.7) | collective-permute-done | bytes 131104 | tf_op jit(solution)/shard_map/ppermute | solution.py:313
  34.5 0.0 collective-permute-done.8.refs_0_
  34.5 0.0 copy-done.2
  34.5 0.7 %far_field.1.here = f32[64,1024]{1,0:T(8,128)S(1)} custom-call(bf16[320,128]{1,0:T(8,128)(2,1)S(1)} %join_level.7.own_top, f32[64,128]{1,0:T(8,128)S(1)} %last_terms.1.potential, f32[128,128]{1,0:T(8,128)S(1)} %get-tuple-element.73.product, bf16[128,1024]{1,0:T(8,128)(2,1)S(1)} %copy-done.2, f32[64,1024]{1,0:T(8,128)S(1)} %get-tuple-element.74.near, ...), custom_call_target="tpu_custom_call" | custom-call | flops 33554432 | bytes 1179648 | tf_op jit(solution)/shard_map/far_field/pallas_call | solution.py:297
  35.3 0.0 collective-permute-done.9.back
  35.3 0.7 %total.1 = f32[64,1024]{1,0:T(8,128)} custom-call(f32[64,1024]{1,0:T(8,128)S(1)} %far_field.1.here, bf16[64,1024]{1,0:T(8,128)(2,1)S(1)} %collective-permute-done.9.back), custom_call_target="tpu_custom_call" | custom-call | flops 131072 | bytes 655360 | tf_op jit(solution)/shard_map/total/pallas_call | solution.py:297
Async XLA Ops:
  0.0 20.2 %collective-permute-start.2 = (bf16[256,1024]{1,0:T(8,128)(2,1)}, bf16[256,1024]{1,0:T(8,128)(2,1)S(1)}, u32[]{:S(2)}, u32[]{:S(2)}) collective-permute-start(bf16[256,1024]{1,0:T(8,128)(2,1)} %wide.3), channel_id=1, source_target_pairs={{0,4},{2,6},{4,8},{6,10},{8,12},{10,14},{12,16},{14,18},{16,20},{1... | collective-permute-start | bytes 1572872 | tf_op jit(solution)/shard_map/ppermute | solution.py:318
  3.0 4.6 %copy-start.1 = (bf16[256,1024]{1,0:T(8,128)(2,1)S(1)}, bf16[256,1024]{1,0:T(8,128)(2,1)}, u32[]{:S(2)}) copy-start(bf16[256,1024]{1,0:T(8,128)(2,1)} %wide.3) | copy-start | bytes 1572868
  6.0 5.1 %collective-permute-start = (bf16[400,128]{1,0:T(8,128)(2,1)}, bf16[400,128]{1,0:T(8,128)(2,1)S(1)}, u32[]{:S(2)}, u32[]{:S(2)}) collective-permute-start(bf16[400,128]{1,0:T(8,128)(2,1)} %get-tuple-element.43), channel_id=1, source_target_pairs={{0,2},{2,0},{4,6},{6,4},{8,10},{10,8},{12,14},{14,12},{16,18},{18,... | collective-permute-start | bytes 307208 | tf_op jit(solution)/shard_map/ppermute | solution.py:313
  7.6 0.9 %copy-start.3 = (bf16[64,1024]{1,0:T(8,128)(2,1)S(1)}, bf16[64,1024]{1,0:T(8,128)(2,1)}, u32[]{:S(2)}) copy-start(bf16[64,1024]{1,0:T(8,128)(2,1)} %get-tuple-element.57.ordered) | copy-start | bytes 393220
  8.5 2.7 %copy-start = (bf16[1,4,128,128]{3,2,1,0:T(8,128)(2,1)S(1)}, bf16[1,4,128,128]{3,2,1,0:T(8,128)(2,1)}, u32[]{:S(2)}) copy-start(bf16[1,4,128,128]{3,2,1,0:T(8,128)(2,1)} %param.13) | copy-start | bytes 393220
  8.5 2.7 %copy-start.5 = (bf16[256,128]{1,0:T(8,128)(2,1)S(1)}, bf16[256,128]{1,0:T(8,128)(2,1)}, u32[]{:S(2)}) copy-start(bf16[256,128]{1,0:T(8,128)(2,1)} %get-tuple-element.41.coords) | copy-start | bytes 196612
  8.5 2.7 %copy-start.7 = (f32[64,128]{1,0:T(8,128)S(1)}, f32[64,128]{1,0:T(8,128)}, u32[]{:S(2)}) copy-start(f32[64,128]{1,0:T(8,128)} %get-tuple-element.42.passed) | copy-start | bytes 98308
  8.8 2.3 %copy-start.6 = (s32[1,5,128]{2,0,1:T(1,128)S(1)}, s32[1,5,128]{2,0,1:T(1,128)}, u32[]{:S(2)}) copy-start(s32[1,5,128]{2,0,1:T(1,128)} %param.11) | copy-start | bytes 7684
  8.8 18.6 %collective-permute-start.5 = (bf16[1280,256]{1,0:T(8,128)(2,1)S(1)}, bf16[1280,256]{1,0:T(8,128)(2,1)S(1)}, u32[]{:S(2)}, u32[]{:S(2)}) collective-permute-start(bf16[1280,256]{1,0:T(8,128)(2,1)S(1)} %get-tuple-element.53.tall), channel_id=1, source_target_pairs={{0,2},{2,0},{4,6},{6,4},{8,10},{10,8},{12,14},{14,12},{16,18},{18,... | collective-permute-start | bytes 1966088 | tf_op jit(solution)/shard_map/ppermute | solution.py:313
  11.4 8.9 %collective-permute-start.1 = (bf16[384,128]{1,0:T(8,128)(2,1)S(1)}, bf16[384,128]{1,0:T(8,128)(2,1)S(1)}, u32[]{:S(2)}, u32[]{:S(2)}) collective-permute-start(bf16[384,128]{1,0:T(8,128)(2,1)S(1)} %get-tuple-element.48), channel_id=1, source_target_pairs={{0,4},{2,6},{4,0},{6,2},{8,12},{10,14},{12,8},{14,10},{16,20},{18,... | collective-permute-start | bytes 294920 | tf_op jit(solution)/shard_map/ppermute | solution.py:313
  13.0 0.9 %copy-start.4 = (bf16[64,1024]{1,0:T(8,128)(2,1)S(1)}, bf16[64,1024]{1,0:T(8,128)(2,1)}, u32[]{:S(2)}) copy-start(bf16[64,1024]{1,0:T(8,128)(2,1)} %get-tuple-element.57.ordered) | copy-start | bytes 393220
  15.3 5.3 %collective-permute-start.3 = (bf16[64,1024]{1,0:T(8,128)(2,1)S(1)}, bf16[64,1024]{1,0:T(8,128)(2,1)S(1)}, u32[]{:S(2)}, u32[]{:S(2)}) collective-permute-start(bf16[64,1024]{1,0:T(8,128)(2,1)S(1)} %copy-done.4), channel_id=1, source_target_pairs={{0,4},{2,6},{4,8},{6,10},{8,12},{10,14},{12,16},{14,18},{16,20},{1... | collective-permute-start | bytes 393224 | tf_op jit(solution)/shard_map/ppermute | solution.py:323
  20.5 0.7 %copy-start.8 = (bf16[16,128]{1,0:T(8,128)(2,1)S(1)}, bf16[16,128]{1,0:T(8,128)(2,1)}, u32[]{:S(2)}) copy-start(bf16[16,128]{1,0:T(8,128)(2,1)} %get-tuple-element.58.marks) | copy-start | bytes 12292
  20.5 4.8 %collective-permute-start.4 = (bf16[384,128]{1,0:T(8,128)(2,1)S(1)}, bf16[384,128]{1,0:T(8,128)(2,1)S(1)}, u32[]{:S(2)}, u32[]{:S(2)}) collective-permute-start(bf16[384,128]{1,0:T(8,128)(2,1)S(1)} %get-tuple-element.62), channel_id=1, source_target_pairs={{0,8},{2,10},{4,12},{6,14},{8,0},{10,2},{12,4},{14,6},{16,24},{18,... | collective-permute-start | bytes 294920 | tf_op jit(solution)/shard_map/ppermute | solution.py:313
  25.5 7.0 %collective-permute-start.6 = (bf16[384,128]{1,0:T(8,128)(2,1)S(1)}, bf16[384,128]{1,0:T(8,128)(2,1)S(1)}, u32[]{:S(2)}, u32[]{:S(2)}) collective-permute-start(bf16[384,128]{1,0:T(8,128)(2,1)S(1)} %get-tuple-element.70), channel_id=1, source_target_pairs={{0,16},{2,18},{4,20},{6,22},{8,24},{10,26},{12,28},{14,30},{16,0},... | collective-permute-start | bytes 294920 | tf_op jit(solution)/shard_map/ppermute | solution.py:313
  29.5 5.0 %collective-permute-start.7 = (bf16[64,1024]{1,0:T(8,128)(2,1)S(1)}, bf16[64,1024]{1,0:T(8,128)(2,1)S(1)}, u32[]{:S(2)}, u32[]{:S(2)}) collective-permute-start(bf16[64,1024]{1,0:T(8,128)(2,1)S(1)} %get-tuple-element.75), channel_id=1, source_target_pairs={{0,2},{2,0},{4,6},{6,4},{8,10},{10,8},{12,14},{14,12},{16,18},{18,... | collective-permute-start | bytes 393224 | tf_op jit(solution)/shard_map/ppermute | solution.py:313
  29.6 5.7 %collective-permute-start.9 = (bf16[64,1024]{1,0:T(8,128)(2,1)S(1)}, bf16[64,1024]{1,0:T(8,128)(2,1)S(1)}, u32[]{:S(2)}, u32[]{:S(2)}) collective-permute-start(bf16[64,1024]{1,0:T(8,128)(2,1)S(1)} %get-tuple-element.76), channel_id=1, source_target_pairs={{0,28},{2,30},{4,0},{6,2},{8,4},{10,6},{12,8},{14,10},{16,12},{18,... | collective-permute-start | bytes 393224 | tf_op jit(solution)/shard_map/ppermute | solution.py:318
  32.6 1.9 %copy-start.2 = (bf16[128,1024]{1,0:T(8,128)(2,1)S(1)}, bf16[128,1024]{1,0:T(8,128)(2,1)}, u32[]{:S(2)}) copy-start(bf16[128,1024]{1,0:T(8,128)(2,1)} %interp.1) | copy-start | bytes 786436
  32.6 1.9 %collective-permute-start.8 = (bf16[320,128]{1,0:T(8,128)(2,1)S(1)}, bf16[320,128]{1,0:T(8,128)(2,1)S(1)}, u32[]{:S(2)}, u32[]{:S(2)}) collective-permute-start(bf16[320,128]{1,0:T(8,128)(2,1)S(1)} %join_level.7.own_top), channel_id=1, source_target_pairs={{0,1},{1,0},{2,3},{3,2},{4,5},{5,4},{6,7},{7,6},{8,9},{9,8},{10,11... | collective-permute-start | bytes 245768 | tf_op jit(solution)/shard_map/ppermute | solution.py:318
